TPU v7x, 32 devices: a whole 2x2x4 slice. The times are simulated.
32 devices in a mesh: rows: 32 (over z, y, x, core).
Axes of the slice: x: 2, y: 2, z: 4, core: 2. Of those that a mesh axis runs over, the one named last changes fastest.
Arguments:
- trailing: float32 [16384, 1024], P('rows'), may hold values from -50 to 50
- leaf_vectors: float32 [16384, 256], P('rows'), may hold values from -2 to 2, as said below
- leaf_factors: float32 [8192, 256], P('rows'), may hold values from -2 to 2, as said below
- tree_vectors: float32 [8192, 256], P('rows'), may hold values from -2 to 2, as said below
- tree_factors: float32 [8192, 256], P('rows'), may hold values from -2 to 2, as said below
- inverse_factor: float32 [256, 256], replicated, may hold values from -2 to 2, as said below
Outputs:
- updated: float32 [16384, 1024], P('rows')
- panel_basis: float32 [16384, 256], P('rows')
- panel_gram: float32 [256, 256], replicated
Inputs may be any that keep to these rules, and one draw needn't show every extreme that they name: Within each leaf, rows 0 to 255 of leaf_vectors form a unit lower triangular matrix (ones on the diagonal, zeros above); leaf_factors_p is the upper triangular factor for which I - leaf_vectors_p leaf_factors_p leaf_vectors_p^T is orthogonal. `leaf_factors`: each block is upper triangular and is the factor described for leaf_vectors. `tree_vectors`: each block is upper triangular, diagonal included; with Y = [I; tree_vectors_q], I - Y tree_factors_q Y^T is orthogonal. `tree_factors`: each block is upper triangular and is the factor described for tree_vectors. `inverse_factor`: upper triangular with a positive diagonal.
All inputs are finite; a program needn't handle non-finite values.
Results may differ from a plain program's by a relative error of at most 0.00018.
Values sent between devices are 32-bit elements; how exact they have to be, the bound alone decides.
No kernel may reach another device: no remote copies, remote signals or barrier semaphores. Data moves between devices by JAX's collectives and lax.ppermute only.
A program may use at most 64 MiB of HBM per device.

v0:
```python
import functools
import jax
import jax.numpy as jnp
from jax import lax
from jax.experimental import pallas as pl
from jax.experimental.pallas import tpu as pltpu
from jax.sharding import PartitionSpec as P

F32 = jnp.float32
BF16 = jnp.bfloat16
EXTRA = 8
PARAMS = pltpu.CompilerParams(vmem_limit_bytes=20 * 1024 * 1024)
WHOLE = pl.BlockSpec(memory_space=pltpu.VMEM)
SCALAR = pl.BlockSpec(memory_space=pltpu.SMEM)
AWAY = pl.BlockSpec(memory_space=pltpu.HBM)


def halves(value):
    high = value.astype(BF16)
    return high, (value - high.astype(F32)).astype(BF16)


def times(left, right, sides):
    first = jnp.concatenate([left[0], left[0], left[1]], axis=sides[0])
    second = jnp.concatenate([right[0], right[1], right[0]], axis=sides[1])
    dims = ((sides[:1], sides[1:]), ((), ()))
    return lax.dot_general(first, second, dims, preferred_element_type=F32)


def plain(left, right):
    return times(left, right, (1, 0))


def by_transpose(left, right):
    return times(left, right, (1, 1))


def pack_kernel(me_ref, *refs):
    sources, (low_ref, high_ref, part_ref), (buffer_ref, sems) = refs[:4], refs[4:7], refs[7:]
    copies = [pltpu.make_async_copy(source, buffer_ref.at[i], sems.at[i]) for i, source in enumerate(sources)]
    for copy in copies:
        copy.start()
    for copy in copies:
        copy.wait()
    core = me_ref[0] % 2
    width = buffer_ref.shape[1]
    half = width // 2
    row = lax.broadcasted_iota(jnp.int32, (width, width), 0)
    col = lax.broadcasted_iota(jnp.int32, (width, width), 1)
    both_vectors = by_core(core, buffer_ref[0], buffer_ref[2])
    both_factors = by_core(core, buffer_ref[1], buffer_ref[3])
    for vectors, factors, out_ref in zip(both_vectors, both_factors, (low_ref, high_ref)):
        packed = jnp.where(row > col, factors.T, vectors)
        diagonal = jnp.sum(jnp.where(row == col, factors, 0.0), axis=0, keepdims=True)
        for part in range(2):
            out_ref[part, :half] = packed[part * half : (part + 1) * half]
            out_ref[part, half:] = jnp.broadcast_to(diagonal, (EXTRA, width))
    part_ref[...] = low_ref[core]


def unpack(first, second):
    half = first.shape[0] - EXTRA
    width = 2 * half
    packed = jnp.concatenate([first[:half], second[:half]], axis=0)
    row = lax.broadcasted_iota(jnp.int32, (width, width), 0)
    col = lax.broadcasted_iota(jnp.int32, (width, width), 1)
    diagonal = jnp.broadcast_to(first[half : half + 1], (width, width))
    vectors = jnp.where(row <= col, packed, 0.0)
    factors = jnp.where(row > col, packed, jnp.where(row == col, diagonal, 0.0))
    return halves(vectors), halves(factors)


def by_core(core, mine, there):
    odd = core == 1
    return jnp.where(odd, there, mine), jnp.where(odd, mine, there)


def place(me):
    return (me >> 1) & 3


def by_place(me, parts, wanted):
    source = place(me) ^ wanted
    out = parts[0]
    for r in range(1, 4):
        out = jnp.where(source == r, parts[r], out)
    return out


def tree_node(low, high, reflector):
    vectors, factors = reflector
    node = by_transpose(halves(low + plain(halves(high), vectors)), factors)
    return low - node, high - by_transpose(halves(node), vectors)


def leaf_first_kernel(
    me_ref, trailing_hbm, vectors_hbm, factors_hbm, inverse_hbm,
    own_ref, away_one, away_two, rest_ref, later_ref, inverse_ref, across_ref, combined_ref,
    part_ref, vectors_ref, factors_ref, value_ref, away_ref, sems,
):
    count, rows, width = part_ref.shape
    copies = []

    def fetch(source, target):
        copies.append(pltpu.make_async_copy(source, target, sems.at[len(copies)]))
        copies[-1].start()
        return copies[-1]

    def fetch_part(b, target):
        cuts = [slice(c, c + width) for c in range(0, rows, width)]
        return [fetch(trailing_hbm.at[c, pl.ds(b * width, width)], target.at[c]) for c in cuts]

    first = [fetch(vectors_hbm, vectors_ref), fetch(factors_hbm, factors_ref)]
    parts = [fetch_part(b, part_ref.at[b]) for b in range(count)]
    last = [fetch_part(count + b, later_ref.at[b]) for b in range(later_ref.shape[0])]
    last.append([fetch(inverse_hbm, inverse_ref)])
    for copy in first:
        copy.wait()
    vectors = vectors_ref[...]
    across = halves(vectors.T)
    across_ref[0], across_ref[1] = across
    combined = halves(by_transpose(halves(vectors), halves(factors_ref[...])))
    combined_ref[0], combined_ref[1] = combined
    for b in range(count):
        for copy in parts[b]:
            copy.wait()
        leaf_block(me_ref, part_ref[b], across, combined, value_ref, rest_ref.at[b], own_ref, away_ref, b)
    panel = part_ref[0]
    value_ref[...] = plain(halves(panel.T), halves(panel))
    hand_over(me_ref, value_ref, own_ref, away_ref, count)
    cut = away_one.shape[0]
    away_one[...] = away_ref[:cut]
    away_two[...] = away_ref[cut:]
    for group in last:
        for copy in group:
            copy.wait()


def hand_over(me_ref, value_ref, own_ref, away_ref, slot):
    half = value_ref.shape[0] // 2
    core = me_ref[0] % 2
    target = slice(slot * half, (slot + 1) * half)
    own_ref[target] = value_ref[pl.ds(pl.multiple_of(core * half, half), half)]
    away_ref[target] = value_ref[pl.ds(pl.multiple_of((1 - core) * half, half), half)]


def leaf_block(me_ref, part, across, combined, value_ref, rest_ref, own_ref, away_ref, slot):
    width = value_ref.shape[0]
    out = part - plain(combined, halves(plain(across, halves(part))))
    rest_ref[...] = out[width:]
    value_ref[...] = out[:width].T
    hand_over(me_ref, value_ref, own_ref, away_ref, slot)


def leaf_second_kernel(me_ref, later_ref, across_ref, combined_ref, own_ref, rest_ref, *refs):
    aways, value_ref = refs[:-1], refs[-1]
    half = value_ref.shape[0] // 2
    across = across_ref[0], across_ref[1]
    combined = combined_ref[0], combined_ref[1]
    for b in range(later_ref.shape[0]):
        own_b = own_ref.at[pl.ds(b * half, half)]
        leaf_block(me_ref, later_ref[b], across, combined, value_ref, rest_ref.at[b], own_b, aways[b], 0)


def store_kernel(me_ref, first_ref, second_ref, inverse_ref, mark_ref, updated_hbm, basis_hbm, basis_ref, sems):
    count, width = first_ref.shape[:2]
    copies = []
    for b in range(count + second_ref.shape[0]):
        source = first_ref.at[b] if b < count else second_ref.at[b - count]
        target = updated_hbm.at[pl.ds(width, width), pl.ds(b * width, width)]
        copies.append(pltpu.make_async_copy(source, target, sems.at[b]))
        copies[-1].start()
    basis_ref[...] = plain(halves(first_ref[0]), halves(inverse_ref[...]))
    copies.append(pltpu.make_async_copy(basis_ref, basis_hbm.at[pl.ds(width, width)], sems.at[len(copies)]))
    mark_ref[...] = jnp.zeros_like(mark_ref)
    copies[-1].start()
    for copy in copies:
        copy.wait()


def core_kernel(
    me_ref, own_a_ref, own_b_ref, one_ref, two_ref, *refs
):
    more = len(refs) - 11
    there_bs, packed_ref = refs[:more], refs[more]
    sends, dones, (low_ref, high_ref) = refs[more + 1 : more + 5], refs[more + 5 : more + 9], refs[more + 9 :]
    me = me_ref[0]
    width = own_a_ref.shape[1]
    half = width // 2
    quarter = half // 4
    cut = own_a_ref.shape[0] - half
    count = cut // half + len(there_bs)
    odd = me % 2 == 1
    there_a = jnp.concatenate([one_ref[...], two_ref[...]], axis=0)
    gram = own_a_ref[cut:] + there_a[cut:]
    mine = jnp.concatenate([own_a_ref[:cut], own_b_ref[...]], axis=0)
    there = jnp.concatenate([there_a[:cut]] + [ref[...] for ref in there_bs], axis=0)
    low = jnp.where(odd, there, mine)
    high = jnp.where(odd, mine, there)
    low, high = tree_node(low, high, unpack(packed_ref[0], packed_ref[1]))
    low_ref[: count * half] = low
    low_ref[count * half :] = gram
    high_ref[...] = high
    for r in range(4):
        start = (place(me) ^ r) * quarter
        for b in range(count + 1):
            source = pl.ds(pl.multiple_of(b * half + start, quarter), quarter)
            target = slice(b * quarter, (b + 1) * quarter)
            sends[r][target] = low_ref[source]
            if b < count:
                dones[r][target] = high_ref[source]


def gather_kernel(me_ref, *refs):
    parts, (stack_ref, held_ref) = refs[:4], refs[4:]
    for r in range(1, 4):
        stack_ref[r - 1] = parts[r][...]
    held_ref[...] = by_place(me_ref[0], [ref[...] for ref in parts], 0)


def hold_kernel(me_ref, held_ref, part_ref, out_ref, *, level):
    rows = slice(0, held_ref.shape[0])
    mine = part_ref.shape[0]
    out_ref[rows] = jnp.where((me_ref[0] >> level) % 2 == 1, part_ref[rows], held_ref[...])
    if out_ref.shape[0] > mine:
        out_ref[mine:] = jnp.zeros_like(out_ref[mine:])


def relay_kernel(me_ref, part_ref, out_ref):
    out_ref[...] = part_ref[: out_ref.shape[0]]


def sort_kernel(me_ref, *refs):
    gots, (heads_ref, gram_ref) = refs[:4], refs[4:]
    cols = heads_ref.shape[1]
    parts = [ref[:cols] for ref in gots]
    for j in range(4):
        heads_ref[j] = by_place(me_ref[0], parts, j)
    gram_ref[...] = gots[0][cols:] + gots[1][cols:] + (gots[2][cols:] + gots[3][cols:])


def plane_kernel(
    me_ref, heads_ref, gram_ref, packed_ref, stack_ref, stack_there_ref, head_ref, send_ref, done_ref, held_ref, *, level
):
    me = me_ref[0]
    core = me % 2
    cols = done_ref.shape[1]
    pairs = [(packed_ref[0], packed_ref[1])]
    pairs += [by_core(core, stack_ref[r], stack_there_ref[r]) for r in range(3)]
    firsts, seconds = [pair[0] for pair in pairs], [pair[1] for pair in pairs]
    pairs = [(by_place(me, firsts, j), by_place(me, seconds, j)) for j in range(4)]
    held_ref[0], held_ref[1] = pairs[0]
    reflectors = [unpack(*pair) for pair in pairs]
    heads = [heads_ref[j] for j in range(4)]
    heads[0], heads[1] = tree_node(heads[0], heads[1], reflectors[1])
    heads[2], heads[3] = tree_node(heads[2], heads[3], reflectors[3])
    heads[0], heads[2] = tree_node(heads[0], heads[2], reflectors[2])
    for j in range(4):
        done_ref[j] = heads[j]
    head_ref[...] = heads[0]
    upper = (me >> level) % 2 == 1
    send_ref[:cols] = jnp.where(upper, plain(halves(heads[0]), reflectors[0][0]), heads[0])
    send_ref[cols:] = gram_ref[...]


def line_node(me, head, result, mine, there, held, part_ref, part_there_ref, level):
    cols = head.shape[0]
    upper = (me >> level) % 2 == 1
    others = by_core(me % 2, part_ref[...], part_there_ref[...])
    node = [jnp.where(upper, a, b) for a, b in zip(held, others)]
    following = [jnp.where(upper, b, a) for a, b in zip(held, others)]
    coeffs = by_transpose(halves(mine[:cols] + there[:cols]), unpack(*node)[1])
    low = jnp.where(upper, there[:cols], head) - coeffs
    plane = me >> 3
    below = (1 << (level - 2)) - 1
    second = (plane & below) == (1 << (level - 3))
    high = head - by_transpose(halves(coeffs), unpack(*held)[0])
    result = jnp.where(second, high, result)
    return low, result, mine[cols:] + there[cols:], following


def line_kernel(me_ref, *refs, level, cut):
    head_ref, result_ref, mine_ref, there_ref, held_ref, part_ref, part_there_ref, head_out, result_out, held_out = refs[:10]
    sends = refs[10:]
    me = me_ref[0]
    held = held_ref[0], held_ref[1]
    low, result, gram, following = line_node(
        me, head_ref[...], result_ref[...], mine_ref[...], there_ref[...], held, part_ref, part_there_ref, level
    )
    cols, quarter = low.shape[0], gram.shape[0]
    ahead = (me >> (level + 1)) % 2 == 1
    head_out[...] = low
    result_out[...] = result
    held_out[0], held_out[1] = following
    value = jnp.where(ahead, plain(halves(low), unpack(*following)[0]), low)
    if cut:
        sends[0][:quarter] = value[:quarter]
        sends[0][quarter:] = gram
        sends[1][...] = value[quarter:]
    else:
        sends[0][:cols] = value
        sends[0][cols:] = gram


def last_kernel(me_ref, *refs, level, cut):
    head_ref, result_ref, held_ref, part_ref, part_there_ref, done_ref = refs[:6]
    number = 2 if cut else 1
    mines, theres = refs[6 : 6 + number], refs[6 + number : 6 + 2 * number]
    sends, all_ref = refs[6 + 2 * number : 10 + 2 * number], refs[10 + 2 * number]
    me = me_ref[0]
    cols = head_ref.shape[0]
    quarter = sends[0].shape[0] - cols
    quarter = quarter // 2
    values = []
    for parts in (mines, theres):
        if cut:
            values.append(jnp.concatenate([parts[0][:quarter], parts[1][...], parts[0][quarter:]], axis=0))
        else:
            values.append(parts[0][...])
    held = held_ref[0], held_ref[1]
    low, result, gram, _ = line_node(
        me, head_ref[...], result_ref[...], values[0], values[1], held, part_ref, part_there_ref, level
    )
    all_ref[0] = jnp.where((me >> 3) == 0, low, result)
    for j in range(1, 4):
        all_ref[j] = done_ref[j]
    for r in range(4):
        sends[r][:cols] = all_ref[place(me) ^ r]
        sends[r][cols : cols + quarter] = low[:quarter]
        sends[r][cols + quarter :] = gram


def pass_kernel(me_ref, *refs):
    backs, dones, out_ref = refs[:4], refs[4:8], refs[8]
    odd = me_ref[0] % 2 == 1
    cols = dones[0].shape[0]
    for r in range(4):
        out_ref[r, :cols] = jnp.where(odd, backs[r][:cols], dones[r][...])
        out_ref[r, cols:] = backs[r][cols:]


def near_kernel(me_ref, *refs):
    backs, dones, (_, updated_hbm, out_ref, sems) = refs[:4], refs[4:8], refs[8:]
    count, width, half = out_ref.shape
    quarter = half // 4
    me = me_ref[0]
    core = me % 2
    odd = core == 1
    copies = []
    for b in range(count):
        rows = slice(b * quarter, (b + 1) * quarter)
        pieces = [jnp.where(odd, dones[r][rows], backs[r][rows]) for r in range(4)]
        out_ref[b] = jnp.concatenate([by_place(me, pieces, j) for j in range(4)], axis=0).T
        columns = pl.ds(pl.multiple_of(b * width + core * half, half), half)
        copies.append(pltpu.make_async_copy(out_ref.at[b], updated_hbm.at[pl.ds(0, width), columns], sems.at[b]))
        copies[-1].start()
    for copy in copies:
        copy.wait()


def far_kernel(me_ref, *refs, total):
    backs, dones = refs[:4], refs[4:8]
    there_ref, inverse_ref, _, _, updated_hbm, basis_hbm, gram_hbm = refs[8:15]
    panel_ref, sum_ref, out_ref, basis_ref, gram_ref, sems = refs[15:]
    count, width, half = out_ref.shape
    quarter = half // 4
    cols = count * quarter
    me = me_ref[0]
    core = me % 2
    odd = core == 1
    copies = []

    def put(source, target):
        copies.append(pltpu.make_async_copy(source, target, sems.at[len(copies)]))
        copies[-1].start()

    for b in range(count):
        rows = slice(b * quarter, (b + 1) * quarter)
        pieces = [there_ref[r, rows] for r in range(4)]
        far = jnp.concatenate([by_place(me, pieces, j) for j in range(4)], axis=0).T
        out_ref[b] = far
        columns = pl.ds(pl.multiple_of(b * width + (1 - core) * half, half), half)
        put(out_ref.at[b], updated_hbm.at[pl.ds(0, width), columns])
        if b == 0:
            pieces = [jnp.where(odd, dones[r][rows], backs[r][rows]) for r in range(4)]
            near = jnp.concatenate([by_place(me, pieces, j) for j in range(4)], axis=0).T
            head = jnp.concatenate(by_core(core, near, far), axis=1)
            basis = plain(halves(head), halves(inverse_ref[...]))
            basis_ref[...] = jnp.where(me == 0, 0.0, basis)
            put(basis_ref, basis_hbm.at[pl.ds(0, width)])

    def target(part, r):
        return pl.ds(pl.multiple_of(part * half + (place(me) ^ r) * quarter, quarter), quarter)

    for r in range(4):
        panel_ref[target(core, r)] = backs[r][cols : cols + quarter]
        sum_ref[target(core, r)] = backs[r][cols + quarter :]
        panel_ref[target(1 - core, r)] = there_ref[r, cols : cols + quarter]
        sum_ref[target(1 - core, r)] = there_ref[r, cols + quarter :]
    panel = halves(panel_ref[...])
    gram_ref[...] = (sum_ref[...] - by_transpose(panel, panel)) / total
    put(gram_ref, gram_hbm)
    for copy in copies:
        copy.wait()


def body(trailing, leaf_vectors, leaf_factors, tree_vectors, tree_factors, inverse_factor):
    rows, columns = trailing.shape
    width = leaf_vectors.shape[1]
    half = width // 2
    quarter = half // 4
    count = columns // width
    devices = lax.axis_size("rows")
    levels = devices.bit_length() - 1
    me = lax.axis_index("rows").astype(jnp.int32)
    me_array = me.reshape(1)
    part_shape = (half + EXTRA, width)
    latest = []

    def exchange(value, shift):
        return lax.ppermute(value, "rows", [(i, i ^ shift) for i in range(devices)])

    def among(value, shift, member):
        return lax.ppermute(value, "rows", [(i, i ^ shift if member(i) else i) for i in range(devices)])

    def around(values):
        there = [exchange(values[r], 2 * r) for r in (3, 1, 2)]
        return [values[0], there[1], there[2], there[0]]

    def shape(*dims):
        return jax.ShapeDtypeStruct(dims, F32)

    def vmem(*dims):
        return pltpu.VMEM(dims, F32)

    def sems(number):
        return pltpu.SemaphoreType.DMA((number,))

    def call(kernel, operands, outs, scratch=(), away_in=(), away_out=(), aliases=(), before=(), work=1, chained=True):
        number = len(operands)
        operands = [pltpu.with_memory_space_constraint(x, pltpu.HBM) if i in away_in else x for i, x in enumerate(operands)]
        outs = [(pltpu.HBM if i in away_out else pltpu.VMEM)(x.shape, x.dtype) for i, x in enumerate(outs)]
        unused = [*latest, *before] if chained else []

        def kernel_on(*refs):
            kernel(*refs[: number + 1], *refs[number + 1 + len(unused) :])

        values = pl.pallas_call(
            kernel_on,
            out_shape=tuple(outs),
            in_specs=[SCALAR]
            + [AWAY if i in away_in else WHOLE for i in range(number)]
            + [pl.BlockSpec(memory_space=pl.ANY)] * len(unused),
            out_specs=tuple(AWAY if i in away_out else WHOLE for i in range(len(outs))),
            scratch_shapes=list(scratch),
            input_output_aliases=dict(aliases),
            compiler_params=PARAMS,
            cost_estimate=pl.CostEstimate(flops=work, bytes_accessed=1, transcendentals=0),
        )(me_array, *operands, *unused)
        if chained and 0 not in away_out:
            latest[:] = values[:1]
        return values

    raw = [exchange(tree_vectors, 1), exchange(tree_factors, 1)]
    blocks = count // 2
    more = count - blocks
    split = jax.ShapeDtypeStruct((2, width, rows), BF16), jax.ShapeDtypeStruct((2, rows, width), BF16)
    rows_a = blocks * half + half
    own_a, away_one, away_two, rest_a, later, inverse_factor, across, combined = call(
        leaf_first_kernel, (trailing, leaf_vectors, leaf_factors, inverse_factor),
        [shape(rows_a, width), shape(rows_a // 2, width), shape(rows_a // 2, width)]
        + [shape(blocks, width, width), shape(more, rows, width), shape(width, width), *split],
        [
            vmem(blocks, rows, width), vmem(rows, width), vmem(width, width), vmem(width, width), vmem(rows_a, width),
            sems(count * (rows // width) + 3),
        ],
        range(4),
    )
    there_a = [exchange(away_one, 1), exchange(away_two, 1)]

    chip_low, chip_high, chip_part = call(
        pack_kernel, (tree_vectors, tree_factors, *raw),
        (shape(2, *part_shape), shape(2, *part_shape), shape(*part_shape)),
        [vmem(4, width, width), sems(4)], (),
    )
    plane_parts = [exchange(chip_part, 2 * r) for r in (3, 1, 2)]
    plane_parts = [plane_parts[1], plane_parts[2], plane_parts[0]]

    own_b, rest_b, *aways = call(
        leaf_second_kernel, (later, across, combined),
        [shape(more * half, width), shape(more, width, width)] + [shape(half, width)] * more,
        [vmem(width, width)], before=there_a,
    )
    theres = [exchange(away, 1) for away in aways]
    cols = count * quarter
    outs = call(
        core_kernel, (own_a, own_b, *there_a, *theres, chip_high),
        [shape(cols + quarter, width)] * 4 + [shape(cols, width)] * 4,
        [vmem(count * half + half, width), vmem(count * half, width)],
    )
    sends, dones = outs[:4], outs[4:]
    stack, held_part = call(
        gather_kernel, (chip_part, *plane_parts), (shape(3, *part_shape), shape(*part_shape)), work=1,
    )
    gots = around(sends)
    stack_there = exchange(stack, 1)
    parts = [exchange(held_part, 8)]
    long_shape = shape(cols + quarter + 8, width)
    for level in range(4, levels):
        (longer,) = call(functools.partial(hold_kernel, level=level - 1), (held_part, parts[-1]), (long_shape,))
        held_part = longer[: half + EXTRA]
        parts.append(exchange(longer, 1 << level))

    heads, gram_part = call(
        sort_kernel, gots, (shape(4, cols, width), shape(quarter, width)), work=1,
    )
    head, send, plane_done, held = call(
        functools.partial(plane_kernel, level=3), (heads, gram_part, chip_low, stack, stack_there),
        (shape(cols, width), shape(cols + quarter, width), shape(4, cols, width), shape(2, *part_shape)),
    )
    result = head
    mines, theres = [send], [exchange(send, 8)]
    parts = parts[:1] + [call(relay_kernel, (part,), (shape(*part_shape),))[0] for part in parts[1:]]
    for level in range(3, levels):
        part = parts[level - 3]
        part_there = exchange(part, 1)
        if level == levels - 1:
            sends = call(
                functools.partial(last_kernel, level=level, cut=len(mines) == 2),
                (head, result, held, part, part_there, plane_done, *mines, *theres),
                [shape(cols + 2 * quarter, width)] * 4, [vmem(4, cols, width)],
            )
        else:
            cut = False
            outs = [shape(2 * quarter, width), shape(cols - quarter, width)] if cut else [shape(cols + quarter, width)]
            head, result, held, *outs = call(
                functools.partial(line_kernel, level=level, cut=cut),
                (head, result, mines[0], theres[0], held, part, part_there),
                [shape(cols, width), shape(cols, width), shape(*held.shape)] + outs,
            )
            mines, theres = outs, [exchange(outs[0], 2 << level)]
            if cut:
                theres.append(among(outs[1], 2 << level, lambda i: (i >> 3) % (1 << (level - 2)) == 0))

    backs = around(sends)
    _, updated, basis = call(
        store_kernel, (rest_a, rest_b, inverse_factor), (shape(8, width), shape(rows, columns), shape(rows, width)),
        [vmem(width, width), sems(count + 1)], (), (1, 2),
    )
    (back,) = call(pass_kernel, (*backs, *dones), (shape(4, cols + 2 * quarter, width),))
    there = exchange(back, 1)
    (updated,) = call(
        near_kernel, (*backs, *dones, updated), (shape(rows, columns),),
        [vmem(count, width, half), sems(count)], (8,), (0,), {9: 0},
    )
    return call(
        functools.partial(far_kernel, total=float(rows * devices)),
        (*backs, *dones, there, inverse_factor, updated, basis),
        (shape(rows, columns), shape(rows, width), shape(width, width)),
        [vmem(width, width), vmem(width, width), vmem(count, width, half), vmem(width, width), vmem(width, width), sems(count + 2)],
        (10, 11), (0, 1, 2), {11: 0, 12: 1},
    )


def solution(mesh):
    in_specs = (
        P("rows", None),
        P("rows", None),
        P("rows", None),
        P("rows", None),
        P("rows", None),
        P(),
    )
    out_specs = (P("rows", None), P("rows", None), P())
    return jax.shard_map(body, mesh=mesh, in_specs=in_specs, out_specs=out_specs, check_vma=False)
```

profile of v0, /device:TPU:0, one launch (start us, length us, event | category | flops | bytes accessed | tf_op | source)
XLA Modules:
  0.0 64.8 jit_solution(2274814690897335770)
XLA Ops:
  1.2 4.2 %shard_map.85 = (f32[384,256]{1,0:T(8,128)S(1)}, f32[192,256]{1,0:T(8,128)S(1)}, f32[192,256]{1,0:T(8,128)S(1)}, f32[2,256,256]{2,1,0:T(8,128)S(1)}, f32[2,512,2...) custom-call(s32[1]{0:T(128)} %bitcast.refs_0_, ...), custom_call_target="tpu_custom_call" | custom-call | flops 1 | bytes 1 | tf_op jit(solution)/shard_map/pallas_call | solution.py:448
  6.4 3.9 %collective-permute-start.11 = (f32[136,256]{1,0:T(8,128)S(1)}, f32[136,256]{1,0:T(8,128)S(1)}, u32[]{:S(2)}, u32[]{:S(2)}) collective-permute-start(f32[136,256]{1,0:T(8,128)S(1)} %get-tuple-element.60.refs_1_), channel_id=1, source_target_pairs={{0,6},{1,7},{2,4},{3,5},{4,2},{5,3},{6,0},{7,1},{8,14},{9,15},{10,... | collective-permute-start | bytes 417800 | tf_op jit(solution)/shard_map/ppermute | solution.py:421
  11.0 1.6 %shard_map.87 = (f32[256,256]{1,0:T(8,128)S(1)}, f32[2,256,256]{2,1,0:T(8,128)S(1)}, f32[128,256]{1,0:T(8,128)S(1)}, f32[128,256]{1,0:T(8,128)S(1)}) custom-call(s32[1]{0:T(128)} %bitcast.refs_0_, f32[2,512,256]{2,1,0:T(8,128)S(1)} %get-tuple-element.46.refs_1_, bf16[2,256,512]{2,1,0:T(8,128)(2,1)S(1)} %get-tuple-element.47.refs_2_, ...), custom_call_target="tpu_custom_call" | custom-call | flops 1 | bytes 1 | tf_op jit(solution)/shard_map/pallas_call | solution.py:448
  14.1 1.3 %shard_map.88 = (f32[160,256]{1,0:T(8,128)S(1)}, f32[160,256]{1,0:T(8,128)S(1)}, f32[160,256]{1,0:T(8,128)S(1)}, f32[160,256]{1,0:T(8,128)S(1)}, f32[128,256]{1,...) custom-call(s32[1]{0:T(128)} %bitcast.refs_0_, ...), custom_call_target="tpu_custom_call" | custom-call | flops 1 | bytes 1 | tf_op jit(solution)/shard_map/pallas_call | solution.py:448
  15.4 1.8 %collective-permute-done.10.refs_3_ = f32[136,256]{1,0:T(8,128)S(1)} collective-permute-done((f32[136,256]{1,0:T(8,128)S(1)}, f32[136,256]{1,0:T(8,128)S(1)}, u32[]{:S(2)}, u32[]{:S(2)}) %collective-permute-start.10) | collective-permute-done | bytes 139296 | tf_op jit(solution)/shard_map/ppermute | solution.py:421
  17.7 1.6 %collective-permute-start.6 = (f32[160,256]{1,0:T(8,128)S(1)}, f32[160,256]{1,0:T(8,128)S(1)}, u32[]{:S(2)}, u32[]{:S(2)}) collective-permute-start(f32[160,256]{1,0:T(8,128)S(1)} %get-tuple-element.57), channel_id=1, source_target_pairs={{0,2},{1,3},{2,0},{3,1},{4,6},{5,7},{6,4},{7,5},{8,10},{9,11},{10,... | collective-permute-start | bytes 491528 | tf_op jit(solution)/shard_map/ppermute | solution.py:421
  19.8 1.4 %collective-permute-start.8 = (f32[160,256]{1,0:T(8,128)S(1)}, f32[160,256]{1,0:T(8,128)S(1)}, u32[]{:S(2)}, u32[]{:S(2)}) collective-permute-start(f32[160,256]{1,0:T(8,128)S(1)} %get-tuple-element.59), channel_id=1, source_target_pairs={{0,6},{1,7},{2,4},{3,5},{4,2},{5,3},{6,0},{7,1},{8,14},{9,15},{10,... | collective-permute-start | bytes 491528 | tf_op jit(solution)/shard_map/ppermute | solution.py:421
  21.2 1.6 %collective-permute-start.12 = (f32[136,256]{1,0:T(8,128)S(1)}, f32[136,256]{1,0:T(8,128)S(1)}, u32[]{:S(2)}, u32[]{:S(2)}) collective-permute-start(f32[136,256]{1,0:T(8,128)S(1)} %get-tuple-element.61.refs_1_), channel_id=1, source_target_pairs={{0,8},{1,9},{2,10},{3,11},{4,12},{5,13},{6,14},{7,15},{8,0},{9,1},... | collective-permute-start | bytes 417800 | tf_op jit(solution)/shard_map/ppermute | solution.py:421
  22.8 3.6 %collective-permute-done.12.refs_2_.refs_6_ = f32[136,256]{1,0:T(8,128)S(1)} collective-permute-done((f32[136,256]{1,0:T(8,128)S(1)}, f32[136,256]{1,0:T(8,128)S(1)}, u32[]{:S(2)}, u32[]{:S(2)}) %collective-permute-start.12) | collective-permute-done | bytes 139296 | tf_op jit(solution)/shard_map/ppermute | solution.py:421
  26.4 2.7 %collective-permute-start.16 = (f32[168,256]{1,0:T(8,128)S(1)}, f32[168,256]{1,0:T(8,128)S(1)}, u32[]{:S(2)}, u32[]{:S(2)}) collective-permute-start(f32[168,256]{1,0:T(8,128)S(1)} %shard_map.90.refs_5_), channel_id=1, source_target_pairs={{0,16},{1,17},{2,18},{3,19},{4,20},{5,21},{6,22},{7,23},{8,24},{9,... | collective-permute-start | bytes 516104 | tf_op jit(solution)/shard_map/ppermute | solution.py:421
  29.2 1.9 %shard_map.92 = (f32[128,256]{1,0:T(8,128)S(1)}, f32[160,256]{1,0:T(8,128)S(1)}, f32[4,128,256]{2,1,0:T(8,128)S(1)}, f32[2,136,256]{2,1,0:T(8,128)S(1)}) custom-call(s32[1]{0:T(128)} %bitcast.refs_0_, f32[4,128,256]{2,1,0:T(8,128)S(1)} %get-tuple-element.63.refs_1_.refs_6_, f32[32,256]{1,0:T(8,128)S(1)} %get-tuple-element.64.refs_2_, ...), custom_call_target="tpu_custom_call" | custom-call | flops 1 | bytes 1 | tf_op jit(solution)/shard_map/pallas_call | solution.py:448
  31.1 1.6 %collective-permute-start.14 = (f32[160,256]{1,0:T(8,128)S(1)}, f32[160,256]{1,0:T(8,128)S(1)}, u32[]{:S(2)}, u32[]{:S(2)}) collective-permute-start(f32[160,256]{1,0:T(8,128)S(1)} %get-tuple-element.66.refs_3_), channel_id=1, source_target_pairs={{0,8},{1,9},{2,10},{3,11},{4,12},{5,13},{6,14},{7,15},{8,0},{9,1},... | collective-permute-start | bytes 491528 | tf_op jit(solution)/shard_map/ppermute | solution.py:421
  32.7 3.4 %collective-permute-done.16.refs_1_ = f32[168,256]{1,0:T(8,128)S(1)} collective-permute-done((f32[168,256]{1,0:T(8,128)S(1)}, f32[168,256]{1,0:T(8,128)S(1)}, u32[]{:S(2)}, u32[]{:S(2)}) %collective-permute-start.16) | collective-permute-done | bytes 172064 | tf_op jit(solution)/shard_map/ppermute | solution.py:421
  36.2 2.6 %collective-permute-done.14.refs_4_ = f32[160,256]{1,0:T(8,128)S(1)} collective-permute-done((f32[160,256]{1,0:T(8,128)S(1)}, f32[160,256]{1,0:T(8,128)S(1)}, u32[]{:S(2)}, u32[]{:S(2)}) %collective-permute-start.14) | collective-permute-done | bytes 163872 | tf_op jit(solution)/shard_map/ppermute | solution.py:421
  39.4 2.4 %collective-permute-start.18 = (f32[160,256]{1,0:T(8,128)S(1)}, f32[160,256]{1,0:T(8,128)S(1)}, u32[]{:S(2)}, u32[]{:S(2)}) collective-permute-start(f32[160,256]{1,0:T(8,128)S(1)} %get-tuple-element.72.refs_7_), channel_id=1, source_target_pairs={{0,16},{1,17},{2,18},{3,19},{4,20},{5,21},{6,22},{7,23},{8,24},{9,... | collective-permute-start | bytes 491528 | tf_op jit(solution)/shard_map/ppermute | solution.py:421
  41.9 1.4 %collective-permute-done.17.refs_5_ = f32[136,256]{1,0:T(8,128)S(1)} collective-permute-done((f32[136,256]{1,0:T(8,128)S(1)}, f32[136,256]{1,0:T(8,128)S(1)}, u32[]{:S(2)}, u32[]{:S(2)}) %collective-permute-start.17) | collective-permute-done | bytes 139296 | tf_op jit(solution)/shard_map/ppermute | solution.py:421
  43.2 6.5 %collective-permute-done.18.refs_8_ = f32[160,256]{1,0:T(8,128)S(1)} collective-permute-done((f32[160,256]{1,0:T(8,128)S(1)}, f32[160,256]{1,0:T(8,128)S(1)}, u32[]{:S(2)}, u32[]{:S(2)}) %collective-permute-start.18) | collective-permute-done | bytes 163872 | tf_op jit(solution)/shard_map/ppermute | solution.py:421
  51.0 1.7 %collective-permute-start.20 = (f32[192,256]{1,0:T(8,128)S(1)}, f32[192,256]{1,0:T(8,128)S(1)}, u32[]{:S(2)}, u32[]{:S(2)}) collective-permute-start(f32[192,256]{1,0:T(8,128)S(1)} %get-tuple-element.75), channel_id=1, source_target_pairs={{0,4},{1,5},{2,6},{3,7},{4,0},{5,1},{6,2},{7,3},{8,12},{9,13},{10,... | collective-permute-start | bytes 589832 | tf_op jit(solution)/shard_map/ppermute | solution.py:421
  52.7 1.3 %collective-permute-start.21 = (f32[192,256]{1,0:T(8,128)S(1)}, f32[192,256]{1,0:T(8,128)S(1)}, u32[]{:S(2)}, u32[]{:S(2)}) collective-permute-start(f32[192,256]{1,0:T(8,128)S(1)} %get-tuple-element.76), channel_id=1, source_target_pairs={{0,6},{1,7},{2,4},{3,5},{4,2},{5,3},{6,0},{7,1},{8,14},{9,15},{10,... | collective-permute-start | bytes 589832 | tf_op jit(solution)/shard_map/ppermute | solution.py:421
  54.0 1.1 %shard_map.96 = (f32[8,256]{1,0:T(8,128)S(1)}, f32[512,1024]{1,0:T(8,128)}, f32[512,256]{1,0:T(8,128)}) custom-call(s32[1]{0:T(128)} %bitcast.refs_0_, f32[2,256,256]{2,1,0:T(8,128)S(1)} %get-tuple-element.81.refs_1_, f32[2,256,256]{2,1,0:T(8,128)S(1)} %get-tuple-element.82.refs_2_, f32[256,256]{1,0:T(8,128)S(1)} %get-tuple-element.83.refs_3_.refs_10_, ...), custom_call_target="tpu_custom_call" | custom-call | flops 1 | bytes 1 | tf_op jit(solution)/shard_map/pallas_call | solution.py:448
  55.1 3.2 %collective-permute-done.19.refs_2_ = f32[192,256]{1,0:T(8,128)S(1)} collective-permute-done((f32[192,256]{1,0:T(8,128)S(1)}, f32[192,256]{1,0:T(8,128)S(1)}, u32[]{:S(2)}, u32[]{:S(2)}) %collective-permute-start.19) | collective-permute-done | bytes 196640 | tf_op jit(solution)/shard_map/ppermute | solution.py:421
  58.3 2.6 %collective-permute-done.20.refs_3_ = f32[192,256]{1,0:T(8,128)S(1)} collective-permute-done((f32[192,256]{1,0:T(8,128)S(1)}, f32[192,256]{1,0:T(8,128)S(1)}, u32[]{:S(2)}, u32[]{:S(2)}) %collective-permute-start.20) | collective-permute-done | bytes 196640 | tf_op jit(solution)/shard_map/ppermute | solution.py:421
  62.0 1.3 %collective-permute-done.22.refs_9_ = f32[4,192,256]{2,1,0:T(8,128)S(1)} collective-permute-done((f32[4,192,256]{2,1,0:T(8,128)S(1)}, f32[4,192,256]{2,1,0:T(8,128)S(1)}, u32[]{:S(2)}, u32[]{:S(2)}) %collective-permute-start.22) | collective-permute-done | bytes 786464 | tf_op jit(solution)/shard_map/ppermute | solution.py:421
  63.3 1.5 %shard_map.99 = (f32[512,1024]{1,0:T(8,128)}, f32[512,256]{1,0:T(8,128)}, f32[256,256]{1,0:T(8,128)}) custom-call(s32[1]{0:T(128)} %bitcast.refs_0_, f32[192,256]{1,0:T(8,128)S(1)} %get-tuple-element.73.refs_4_.refs_1_, f32[192,256]{1,0:T(8,128)S(1)} %collective-permute-done.19.refs_2_, ...), custom_call_target="tpu_custom_call", output_to_operand_aliasing={{0}: (11, {}), {1}: (12, {})} | custom-call | flops 1 | bytes 1 | tf_op jit(solution)/shard_map/pallas_call | solution.py:448
  (41 shorter events, 7.9 us)
Async XLA Ops:
  0.6 5.4 %copy-start = (f32[256,256]{1,0:T(8,128)S(1)}, f32[256,256]{1,0:T(8,128)}, u32[]{:S(2)}) copy-start(f32[256,256]{1,0:T(8,128)} %refs_1_.3) | copy-start | bytes 786436
  0.7 5.4 %collective-permute-start = (f32[256,256]{1,0:T(8,128)}, f32[256,256]{1,0:T(8,128)S(1)}, u32[]{:S(2)}, u32[]{:S(2)}) collective-permute-start(f32[256,256]{1,0:T(8,128)} %refs_1_.3), channel_id=1, source_target_pairs={{0,1},{1,0},{2,3},{3,2},{4,5},{5,4},{6,7},{7,6},{8,9},{9,8},{10,11... | collective-permute-start | bytes 786440 | tf_op jit(solution)/shard_map/ppermute | solution.py:421
  1.2 4.8 %collective-permute-start.1 = (f32[256,256]{1,0:T(8,128)}, f32[256,256]{1,0:T(8,128)S(1)}, u32[]{:S(2)}, u32[]{:S(2)}) collective-permute-start(f32[256,256]{1,0:T(8,128)} %refs_2_.3), channel_id=1, source_target_pairs={{0,1},{1,0},{2,3},{3,2},{4,5},{5,4},{6,7},{7,6},{8,9},{9,8},{10,11... | collective-permute-start | bytes 786440 | tf_op jit(solution)/shard_map/ppermute | solution.py:421
  5.4 5.6 %collective-permute-start.2 = (f32[192,256]{1,0:T(8,128)S(1)}, f32[192,256]{1,0:T(8,128)S(1)}, u32[]{:S(2)}, u32[]{:S(2)}) collective-permute-start(f32[192,256]{1,0:T(8,128)S(1)} %get-tuple-element.50), channel_id=1, source_target_pairs={{0,1},{1,0},{2,3},{3,2},{4,5},{5,4},{6,7},{7,6},{8,9},{9,8},{10,11... | collective-permute-start | bytes 589832 | tf_op jit(solution)/shard_map/ppermute | solution.py:421
  5.9 5.1 %collective-permute-start.3 = (f32[192,256]{1,0:T(8,128)S(1)}, f32[192,256]{1,0:T(8,128)S(1)}, u32[]{:S(2)}, u32[]{:S(2)}) collective-permute-start(f32[192,256]{1,0:T(8,128)S(1)} %get-tuple-element.51), channel_id=1, source_target_pairs={{0,1},{1,0},{2,3},{3,2},{4,5},{5,4},{6,7},{7,6},{8,9},{9,8},{10,11... | collective-permute-start | bytes 589832 | tf_op jit(solution)/shard_map/ppermute | solution.py:421
  6.4 9.0 %collective-permute-start.11 = (f32[136,256]{1,0:T(8,128)S(1)}, f32[136,256]{1,0:T(8,128)S(1)}, u32[]{:S(2)}, u32[]{:S(2)}) collective-permute-start(f32[136,256]{1,0:T(8,128)S(1)} %get-tuple-element.60.refs_1_), channel_id=1, source_target_pairs={{0,6},{1,7},{2,4},{3,5},{4,2},{5,3},{6,0},{7,1},{8,14},{9,15},{10,... | collective-permute-start | bytes 417800 | tf_op jit(solution)/shard_map/ppermute | solution.py:421
  10.3 6.9 %collective-permute-start.10 = (f32[136,256]{1,0:T(8,128)S(1)}, f32[136,256]{1,0:T(8,128)S(1)}, u32[]{:S(2)}, u32[]{:S(2)}) collective-permute-start(f32[136,256]{1,0:T(8,128)S(1)} %get-tuple-element.60.refs_1_), channel_id=1, source_target_pairs={{0,4},{1,5},{2,6},{3,7},{4,0},{5,1},{6,2},{7,3},{8,12},{9,13},{10,... | collective-permute-start | bytes 417800 | tf_op jit(solution)/shard_map/ppermute | solution.py:421
  10.8 6.7 %collective-permute-start.9 = (f32[136,256]{1,0:T(8,128)S(1)}, f32[136,256]{1,0:T(8,128)S(1)}, u32[]{:S(2)}, u32[]{:S(2)}) collective-permute-start(f32[136,256]{1,0:T(8,128)S(1)} %get-tuple-element.60.refs_1_), channel_id=1, source_target_pairs={{0,2},{1,3},{2,0},{3,1},{4,6},{5,7},{6,4},{7,5},{8,10},{9,11},{10,... | collective-permute-start | bytes 417800 | tf_op jit(solution)/shard_map/ppermute | solution.py:421
  12.5 1.4 %collective-permute-start.4 = (f32[128,256]{1,0:T(8,128)S(1)}, f32[128,256]{1,0:T(8,128)S(1)}, u32[]{:S(2)}, u32[]{:S(2)}) collective-permute-start(f32[128,256]{1,0:T(8,128)S(1)} %get-tuple-element.53), channel_id=1, source_target_pairs={{0,1},{1,0},{2,3},{3,2},{4,5},{5,4},{6,7},{7,6},{8,9},{9,8},{10,11... | collective-permute-start | bytes 393224 | tf_op jit(solution)/shard_map/ppermute | solution.py:421
  12.6 1.5 %collective-permute-start.5 = (f32[128,256]{1,0:T(8,128)S(1)}, f32[128,256]{1,0:T(8,128)S(1)}, u32[]{:S(2)}, u32[]{:S(2)}) collective-permute-start(f32[128,256]{1,0:T(8,128)S(1)} %get-tuple-element.54), channel_id=1, source_target_pairs={{0,1},{1,0},{2,3},{3,2},{4,5},{5,4},{6,7},{7,6},{8,9},{9,8},{10,11... | collective-permute-start | bytes 393224 | tf_op jit(solution)/shard_map/ppermute | solution.py:421
  17.6 11.6 %collective-permute-start.13 = (f32[3,136,256]{2,1,0:T(8,128)S(1)}, f32[3,136,256]{2,1,0:T(8,128)S(1)}, u32[]{:S(2)}, u32[]{:S(2)}) collective-permute-start(f32[3,136,256]{2,1,0:T(8,128)S(1)} %get-tuple-element.62.refs_3_.refs_4_), channel_id=1, source_target_pairs={{0,1},{1,0},{2,3},{3,2},{4,5},{5,4},{6,7},{7,6},{8,9},{9,8},{10,11... | collective-permute-start | bytes 1253384 | tf_op jit(solution)/shard_map/ppermute | solution.py:421
  17.7 11.4 %collective-permute-start.6 = (f32[160,256]{1,0:T(8,128)S(1)}, f32[160,256]{1,0:T(8,128)S(1)}, u32[]{:S(2)}, u32[]{:S(2)}) collective-permute-start(f32[160,256]{1,0:T(8,128)S(1)} %get-tuple-element.57), channel_id=1, source_target_pairs={{0,2},{1,3},{2,0},{3,1},{4,6},{5,7},{6,4},{7,5},{8,10},{9,11},{10,... | collective-permute-start | bytes 491528 | tf_op jit(solution)/shard_map/ppermute | solution.py:421
  19.2 9.9 %collective-permute-start.7 = (f32[160,256]{1,0:T(8,128)S(1)}, f32[160,256]{1,0:T(8,128)S(1)}, u32[]{:S(2)}, u32[]{:S(2)}) collective-permute-start(f32[160,256]{1,0:T(8,128)S(1)} %get-tuple-element.58), channel_id=1, source_target_pairs={{0,4},{1,5},{2,6},{3,7},{4,0},{5,1},{6,2},{7,3},{8,12},{9,13},{10,... | collective-permute-start | bytes 491528 | tf_op jit(solution)/shard_map/ppermute | solution.py:421
  19.8 9.3 %collective-permute-start.8 = (f32[160,256]{1,0:T(8,128)S(1)}, f32[160,256]{1,0:T(8,128)S(1)}, u32[]{:S(2)}, u32[]{:S(2)}) collective-permute-start(f32[160,256]{1,0:T(8,128)S(1)} %get-tuple-element.59), channel_id=1, source_target_pairs={{0,6},{1,7},{2,4},{3,5},{4,2},{5,3},{6,0},{7,1},{8,14},{9,15},{10,... | collective-permute-start | bytes 491528 | tf_op jit(solution)/shard_map/ppermute | solution.py:421
  21.2 5.2 %collective-permute-start.12 = (f32[136,256]{1,0:T(8,128)S(1)}, f32[136,256]{1,0:T(8,128)S(1)}, u32[]{:S(2)}, u32[]{:S(2)}) collective-permute-start(f32[136,256]{1,0:T(8,128)S(1)} %get-tuple-element.61.refs_1_), channel_id=1, source_target_pairs={{0,8},{1,9},{2,10},{3,11},{4,12},{5,13},{6,14},{7,15},{8,0},{9,1},... | collective-permute-start | bytes 417800 | tf_op jit(solution)/shard_map/ppermute | solution.py:421
  26.4 9.7 %collective-permute-start.16 = (f32[168,256]{1,0:T(8,128)S(1)}, f32[168,256]{1,0:T(8,128)S(1)}, u32[]{:S(2)}, u32[]{:S(2)}) collective-permute-start(f32[168,256]{1,0:T(8,128)S(1)} %shard_map.90.refs_5_), channel_id=1, source_target_pairs={{0,16},{1,17},{2,18},{3,19},{4,20},{5,21},{6,22},{7,23},{8,24},{9,... | collective-permute-start | bytes 516104 | tf_op jit(solution)/shard_map/ppermute | solution.py:421
  31.1 7.7 %collective-permute-start.14 = (f32[160,256]{1,0:T(8,128)S(1)}, f32[160,256]{1,0:T(8,128)S(1)}, u32[]{:S(2)}, u32[]{:S(2)}) collective-permute-start(f32[160,256]{1,0:T(8,128)S(1)} %get-tuple-element.66.refs_3_), channel_id=1, source_target_pairs={{0,8},{1,9},{2,10},{3,11},{4,12},{5,13},{6,14},{7,15},{8,0},{9,1},... | collective-permute-start | bytes 491528 | tf_op jit(solution)/shard_map/ppermute | solution.py:421
  32.7 3.4 %collective-permute-start.15 = (f32[136,256]{1,0:T(8,128)S(1)}, f32[136,256]{1,0:T(8,128)S(1)}, u32[]{:S(2)}, u32[]{:S(2)}) collective-permute-start(f32[136,256]{1,0:T(8,128)S(1)} %collective-permute-done.12.refs_2_.refs_6_), channel_id=1, source_target_pairs={{0,1},{1,0},{2,3},{3,2},{4,5},{5,4},{6,7},{7,6},{8,9},{9,8},{10,11... | collective-permute-start | bytes 417800 | tf_op jit(solution)/shard_map/ppermute | solution.py:421
  39.4 10.3 %collective-permute-start.18 = (f32[160,256]{1,0:T(8,128)S(1)}, f32[160,256]{1,0:T(8,128)S(1)}, u32[]{:S(2)}, u32[]{:S(2)}) collective-permute-start(f32[160,256]{1,0:T(8,128)S(1)} %get-tuple-element.72.refs_7_), channel_id=1, source_target_pairs={{0,16},{1,17},{2,18},{3,19},{4,20},{5,21},{6,22},{7,23},{8,24},{9,... | collective-permute-start | bytes 491528 | tf_op jit(solution)/shard_map/ppermute | solution.py:421
  41.9 1.4 %collective-permute-start.17 = (f32[136,256]{1,0:T(8,128)S(1)}, f32[136,256]{1,0:T(8,128)S(1)}, u32[]{:S(2)}, u32[]{:S(2)}) collective-permute-start(f32[136,256]{1,0:T(8,128)S(1)} %shard_map.93.refs_8_.refs_4_), channel_id=1, source_target_pairs={{0,1},{1,0},{2,3},{3,2},{4,5},{5,4},{6,7},{7,6},{8,9},{9,8},{10,11... | collective-permute-start | bytes 417800 | tf_op jit(solution)/shard_map/ppermute | solution.py:421
  50.5 7.8 %collective-permute-start.19 = (f32[192,256]{1,0:T(8,128)S(1)}, f32[192,256]{1,0:T(8,128)S(1)}, u32[]{:S(2)}, u32[]{:S(2)}) collective-permute-start(f32[192,256]{1,0:T(8,128)S(1)} %get-tuple-element.74), channel_id=1, source_target_pairs={{0,2},{1,3},{2,0},{3,1},{4,6},{5,7},{6,4},{7,5},{8,10},{9,11},{10,... | collective-permute-start | bytes 589832 | tf_op jit(solution)/shard_map/ppermute | solution.py:421
  51.0 9.9 %collective-permute-start.20 = (f32[192,256]{1,0:T(8,128)S(1)}, f32[192,256]{1,0:T(8,128)S(1)}, u32[]{:S(2)}, u32[]{:S(2)}) collective-permute-start(f32[192,256]{1,0:T(8,128)S(1)} %get-tuple-element.75), channel_id=1, source_target_pairs={{0,4},{1,5},{2,6},{3,7},{4,0},{5,1},{6,2},{7,3},{8,12},{9,13},{10,... | collective-permute-start | bytes 589832 | tf_op jit(solution)/shard_map/ppermute | solution.py:421
  52.7 8.2 %collective-permute-start.21 = (f32[192,256]{1,0:T(8,128)S(1)}, f32[192,256]{1,0:T(8,128)S(1)}, u32[]{:S(2)}, u32[]{:S(2)}) collective-permute-start(f32[192,256]{1,0:T(8,128)S(1)} %get-tuple-element.76), channel_id=1, source_target_pairs={{0,6},{1,7},{2,4},{3,5},{4,2},{5,3},{6,0},{7,1},{8,14},{9,15},{10,... | collective-permute-start | bytes 589832 | tf_op jit(solution)/shard_map/ppermute | solution.py:421
  61.0 2.4 %collective-permute-start.22 = (f32[4,192,256]{2,1,0:T(8,128)S(1)}, f32[4,192,256]{2,1,0:T(8,128)S(1)}, u32[]{:S(2)}, u32[]{:S(2)}) collective-permute-start(f32[4,192,256]{2,1,0:T(8,128)S(1)} %shard_map.97.refs_10_.refs_13_), channel_id=1, source_target_pairs={{0,1},{1,0},{2,3},{3,2},{4,5},{5,4},{6,7},{7,6},{8,9},{9,8},{10,11... | collective-permute-start | bytes 2359304 | tf_op jit(solution)/shard_map/ppermute | solution.py:421
  (1 other events, 5.4 us)
where the time goes:
time: 64.9 us; the launch traced here: 64.8 us
  waiting for transfers between devices  27.7 us (43%)
  starting transfers between devices  21.9 us (34%)
  Pallas kernels  14.3 us (22%)
  between operations  0.81 us (1%)
    ppermute x23, waiting for transfers between devices, exchange(): return lax.ppermute(value, 'rows', [(i, i ^ shift) for i in range(devices)])  27.7 us
    ppermute x23, starting transfers between devices, exchange(): return lax.ppermute(value, 'rows', [(i, i ^ shift) for i in range(devices)])  21.9 us
    pallas_call x15, Pallas kernels, call(): pl.pallas_call(kernel_on, out_shape=tuple(outs), in_specs=[SCALAR] + [AWA...  14.3 us
  transfers between devices with their start and end apart: 23, of which 12 were waited for; matrix products, arithmetic and copies ran while one was open for 0% of the time, Pallas kernels for 18%

commit v1 on v0

--- a/solution.py
+++ b/solution.py
@@ -33,6 +33,17 @@
 
 def by_transpose(left, right):
     return times(left, right, (1, 1))
+
+
+def masks(size):
+    row = lax.broadcasted_iota(jnp.int32, (size, size), 0)
+    col = lax.broadcasted_iota(jnp.int32, (size, size), 1)
+    return row, col
+
+
+def diagonal_of(square):
+    row, col = masks(square.shape[0])
+    return jnp.sum(jnp.where(row == col, square, 0.0), axis=0, keepdims=True)
 
 
 def pack_kernel(me_ref, *refs):
@@ -43,31 +54,56 @@
     for copy in copies:
         copy.wait()
     core = me_ref[0] % 2
-    width = buffer_ref.shape[1]
-    half = width // 2
-    row = lax.broadcasted_iota(jnp.int32, (width, width), 0)
-    col = lax.broadcasted_iota(jnp.int32, (width, width), 1)
+    half = buffer_ref.shape[1] // 2
+    row, col = masks(half)
     both_vectors = by_core(core, buffer_ref[0], buffer_ref[2])
     both_factors = by_core(core, buffer_ref[1], buffer_ref[3])
     for vectors, factors, out_ref in zip(both_vectors, both_factors, (low_ref, high_ref)):
-        packed = jnp.where(row > col, factors.T, vectors)
-        diagonal = jnp.sum(jnp.where(row == col, factors, 0.0), axis=0, keepdims=True)
+        first, second = factors[:half, :half], factors[half:, half:]
+        square = jnp.where(row > col, first.T, jnp.where(row < col, second, 0.0))
+        t_rows = jnp.concatenate([square, factors[:half, half:].T], axis=1)
+        t_diagonal = jnp.concatenate([diagonal_of(first), diagonal_of(second)], axis=1)
+        first, second = vectors[:half, :half], vectors[half:, half:]
+        square = jnp.where(row <= col, first, second.T)
+        v_rows = jnp.concatenate([square, vectors[:half, half:]], axis=1)
+        v_diagonal = jnp.concatenate([diagonal_of(second)] * 2, axis=1)
+        line = lax.broadcasted_iota(jnp.int32, (EXTRA, 2 * half), 0)
+        diagonals = jnp.where(line == 0, t_diagonal, v_diagonal)
         for part in range(2):
-            out_ref[part, :half] = packed[part * half : (part + 1) * half]
-            out_ref[part, half:] = jnp.broadcast_to(diagonal, (EXTRA, width))
+            rows = slice(part * half // 2, (part + 1) * half // 2)
+            out_ref[part, : half // 2] = t_rows[rows]
+            out_ref[part, half // 2 : half // 2 + EXTRA] = diagonals
+            out_ref[part, half // 2 + EXTRA :] = v_rows[rows]
     part_ref[...] = low_ref[core]
 
 
+def unpack_factors(first, second):
+    half = first.shape[1] // 2
+    rows = jnp.concatenate([first[: half // 2], second[: half // 2]], axis=0)
+    row, col = masks(half)
+    square, corner = rows[:, :half], rows[:, half:]
+    diagonal = first[half // 2 : half // 2 + 1]
+    upper_left = jnp.where(row > col, square, jnp.where(row == col, diagonal[:, :half], 0.0))
+    lower_right = jnp.where(row > col, square.T, jnp.where(row == col, diagonal[:, half:], 0.0))
+    above = jnp.concatenate([upper_left, jnp.zeros_like(upper_left)], axis=1)
+    return halves(jnp.concatenate([above, jnp.concatenate([corner, lower_right], axis=1)], axis=0))
+
+
+def unpack_vectors(first, second):
+    half = first.shape[1] // 2
+    start = half // 2 + EXTRA
+    rows = jnp.concatenate([first[start:], second[start:]], axis=0)
+    row, col = masks(half)
+    square, corner = rows[:, :half], rows[:, half:]
+    diagonal = first[half // 2 + 1 : half // 2 + 2, :half]
+    upper_left = jnp.where(row <= col, square, 0.0)
+    lower_right = jnp.where(row < col, square.T, jnp.where(row == col, diagonal, 0.0))
+    above = jnp.concatenate([upper_left, corner], axis=1)
+    return halves(jnp.concatenate([above, jnp.concatenate([jnp.zeros_like(corner), lower_right], axis=1)], axis=0))
+
+
 def unpack(first, second):
-    half = first.shape[0] - EXTRA
-    width = 2 * half
-    packed = jnp.concatenate([first[:half], second[:half]], axis=0)
-    row = lax.broadcasted_iota(jnp.int32, (width, width), 0)
-    col = lax.broadcasted_iota(jnp.int32, (width, width), 1)
-    diagonal = jnp.broadcast_to(first[half : half + 1], (width, width))
-    vectors = jnp.where(row <= col, packed, 0.0)
-    factors = jnp.where(row > col, packed, jnp.where(row == col, diagonal, 0.0))
-    return halves(vectors), halves(factors)
+    return unpack_vectors(first, second), unpack_factors(first, second)
 
 
 def by_core(core, mine, there):
@@ -219,15 +255,8 @@
 
 
 def hold_kernel(me_ref, held_ref, part_ref, out_ref, *, level):
-    rows = slice(0, held_ref.shape[0])
-    mine = part_ref.shape[0]
-    out_ref[rows] = jnp.where((me_ref[0] >> level) % 2 == 1, part_ref[rows], held_ref[...])
-    if out_ref.shape[0] > mine:
-        out_ref[mine:] = jnp.zeros_like(out_ref[mine:])
-
-
-def relay_kernel(me_ref, part_ref, out_ref):
-    out_ref[...] = part_ref[: out_ref.shape[0]]
+    rows = slice(0, out_ref.shape[0])
+    out_ref[...] = jnp.where((me_ref[0] >> level) % 2 == 1, part_ref[rows], held_ref[rows])
 
 
 def sort_kernel(me_ref, *refs):
@@ -239,18 +268,20 @@
     gram_ref[...] = gots[0][cols:] + gots[1][cols:] + (gots[2][cols:] + gots[3][cols:])
 
 
-def plane_kernel(
-    me_ref, heads_ref, gram_ref, packed_ref, stack_ref, stack_there_ref, head_ref, send_ref, done_ref, held_ref, *, level
-):
+def prepare_kernel(me_ref, packed_ref, stack_ref, stack_there_ref, ready_ref, held_ref):
     me = me_ref[0]
-    core = me % 2
-    cols = done_ref.shape[1]
     pairs = [(packed_ref[0], packed_ref[1])]
-    pairs += [by_core(core, stack_ref[r], stack_there_ref[r]) for r in range(3)]
+    pairs += [by_core(me % 2, stack_ref[r], stack_there_ref[r]) for r in range(3)]
     firsts, seconds = [pair[0] for pair in pairs], [pair[1] for pair in pairs]
     pairs = [(by_place(me, firsts, j), by_place(me, seconds, j)) for j in range(4)]
     held_ref[0], held_ref[1] = pairs[0]
-    reflectors = [unpack(*pair) for pair in pairs]
+    for j in range(4):
+        (ready_ref[j, 0], ready_ref[j, 1]), (ready_ref[j, 2], ready_ref[j, 3]) = unpack(*pairs[j])
+
+
+def plane_kernel(me_ref, heads_ref, gram_ref, ready_ref, head_ref, send_ref, done_ref, *, level):
+    cols = done_ref.shape[1]
+    reflectors = [((ready_ref[j, 0], ready_ref[j, 1]), (ready_ref[j, 2], ready_ref[j, 3])) for j in range(4)]
     heads = [heads_ref[j] for j in range(4)]
     heads[0], heads[1] = tree_node(heads[0], heads[1], reflectors[1])
     heads[2], heads[3] = tree_node(heads[2], heads[3], reflectors[3])
@@ -258,7 +289,7 @@
     for j in range(4):
         done_ref[j] = heads[j]
     head_ref[...] = heads[0]
-    upper = (me >> level) % 2 == 1
+    upper = (me_ref[0] >> level) % 2 == 1
     send_ref[:cols] = jnp.where(upper, plain(halves(heads[0]), reflectors[0][0]), heads[0])
     send_ref[cols:] = gram_ref[...]
 
@@ -267,14 +298,16 @@
     cols = head.shape[0]
     upper = (me >> level) % 2 == 1
     others = by_core(me % 2, part_ref[...], part_there_ref[...])
-    node = [jnp.where(upper, a, b) for a, b in zip(held, others)]
-    following = [jnp.where(upper, b, a) for a, b in zip(held, others)]
-    coeffs = by_transpose(halves(mine[:cols] + there[:cols]), unpack(*node)[1])
+    whole = held[0].shape == others[0].shape
+    need = held[0].shape[1] // 4 + EXTRA
+    node = [jnp.where(upper, a[:need], b[:need]) for a, b in zip(held, others)]
+    following = [jnp.where(upper, b, a) for a, b in zip(held, others)] if whole else None
+    coeffs = by_transpose(halves(mine[:cols] + there[:cols]), unpack_factors(*node))
     low = jnp.where(upper, there[:cols], head) - coeffs
     plane = me >> 3
     below = (1 << (level - 2)) - 1
     second = (plane & below) == (1 << (level - 3))
-    high = head - by_transpose(halves(coeffs), unpack(*held)[0])
+    high = head - by_transpose(halves(coeffs), unpack_vectors(*held))
     result = jnp.where(second, high, result)
     return low, result, mine[cols:] + there[cols:], following
 
@@ -292,7 +325,7 @@
     head_out[...] = low
     result_out[...] = result
     held_out[0], held_out[1] = following
-    value = jnp.where(ahead, plain(halves(low), unpack(*following)[0]), low)
+    value = jnp.where(ahead, plain(halves(low), unpack_vectors(*following)), low)
     if cut:
         sends[0][:quarter] = value[:quarter]
         sends[0][quarter:] = gram
@@ -505,22 +538,26 @@
     gots = around(sends)
     stack_there = exchange(stack, 1)
     parts = [exchange(held_part, 8)]
-    long_shape = shape(cols + quarter + 8, width)
     for level in range(4, levels):
-        (longer,) = call(functools.partial(hold_kernel, level=level - 1), (held_part, parts[-1]), (long_shape,))
-        held_part = longer[: half + EXTRA]
-        parts.append(exchange(longer, 1 << level))
-
+        short = 3 * quarter if level == levels - 1 else half + EXTRA
+        (held_part,) = call(
+            functools.partial(hold_kernel, level=level - 1), (held_part, parts[-1]), (shape(short, width),),
+        )
+        parts.append(exchange(held_part, 1 << level))
+
+    ready, held = call(
+        prepare_kernel, (chip_low, stack, stack_there),
+        (jax.ShapeDtypeStruct((4, 4, width, width), BF16), shape(2, *part_shape)),
+    )
     heads, gram_part = call(
         sort_kernel, gots, (shape(4, cols, width), shape(quarter, width)), work=1,
     )
-    head, send, plane_done, held = call(
-        functools.partial(plane_kernel, level=3), (heads, gram_part, chip_low, stack, stack_there),
-        (shape(cols, width), shape(cols + quarter, width), shape(4, cols, width), shape(2, *part_shape)),
+    head, send, plane_done = call(
+        functools.partial(plane_kernel, level=3), (heads, gram_part, ready),
+        (shape(cols, width), shape(cols + quarter, width), shape(4, cols, width)),
     )
     result = head
     mines, theres = [send], [exchange(send, 8)]
-    parts = parts[:1] + [call(relay_kernel, (part,), (shape(*part_shape),))[0] for part in parts[1:]]
     for level in range(3, levels):
         part = parts[level - 3]
         part_there = exchange(part, 1)

time: 64.9 us -> 63.8 us (0.983)
  waiting for transfers between devices: 27.7 us -> 24.9 us
  starting transfers between devices: 21.9 us -> 23.1 us
    ppermute x23, waiting for transfers between devices: 27.7 us -> 24.9 us  [exchange(): return lax.ppermute(value, 'rows', [(i, i ^ shift) for i in range(devices)])]
    ppermute x23, starting transfers between devices: 21.9 us -> 23.1 us  [exchange(): return lax.ppermute(value, 'rows', [(i, i ^ shift) for i in range(devices)])]
  transfers between devices with their start and end apart: 23 -> 23, of which waited for: 12 -> 13; matrix products, arithmetic and copies ran while one was open for 0% -> 0% of each run, Pallas kernels for 18% -> 17%
where the time goes in v1:
time: 63.8 us; the launch traced here: 63.6 us
  waiting for transfers between devices  24.9 us (39%)
  starting transfers between devices  23.1 us (36%)
  Pallas kernels  14.8 us (23%)
  between operations  0.81 us (1%)
    ppermute x23, waiting for transfers between devices, exchange(): return lax.ppermute(value, 'rows', [(i, i ^ shift) for i in range(devices)])  24.9 us
    ppermute x23, starting transfers between devices, exchange(): return lax.ppermute(value, 'rows', [(i, i ^ shift) for i in range(devices)])  23.1 us
    pallas_call x15, Pallas kernels, call(): pl.pallas_call(kernel_on, out_shape=tuple(outs), in_specs=[SCALAR] + [AWA...  14.8 us
  transfers between devices with their start and end apart: 23, of which 13 were waited for; matrix products, arithmetic and copies ran while one was open for 0% of the time, Pallas kernels for 17%

profile of v1, /device:TPU:0, one launch (start us, length us, event | category | flops | bytes accessed | tf_op | source)
XLA Modules:
  0.0 63.6 jit_solution(17352682094008829911)
XLA Ops:
  1.2 4.2 %shard_map.85 = (f32[384,256]{1,0:T(8,128)S(1)}, f32[192,256]{1,0:T(8,128)S(1)}, f32[192,256]{1,0:T(8,128)S(1)}, f32[2,256,256]{2,1,0:T(8,128)S(1)}, f32[2,512,2...) custom-call(s32[1]{0:T(128)} %bitcast.refs_0_, ...), custom_call_target="tpu_custom_call" | custom-call | flops 1 | bytes 1 | tf_op jit(solution)/shard_map/pallas_call | solution.py:481
  6.4 3.9 %collective-permute-start.11 = (f32[136,256]{1,0:T(8,128)S(1)}, f32[136,256]{1,0:T(8,128)S(1)}, u32[]{:S(2)}, u32[]{:S(2)}) collective-permute-start(f32[136,256]{1,0:T(8,128)S(1)} %get-tuple-element.61.refs_1_), channel_id=1, source_target_pairs={{0,6},{1,7},{2,4},{3,5},{4,2},{5,3},{6,0},{7,1},{8,14},{9,15},{10,... | collective-permute-start | bytes 417800 | tf_op jit(solution)/shard_map/ppermute | solution.py:454
  10.9 1.6 %shard_map.87 = (f32[256,256]{1,0:T(8,128)S(1)}, f32[2,256,256]{2,1,0:T(8,128)S(1)}, f32[128,256]{1,0:T(8,128)S(1)}, f32[128,256]{1,0:T(8,128)S(1)}) custom-call(s32[1]{0:T(128)} %bitcast.refs_0_, f32[2,512,256]{2,1,0:T(8,128)S(1)} %get-tuple-element.47.refs_1_, bf16[2,256,512]{2,1,0:T(8,128)(2,1)S(1)} %get-tuple-element.48.refs_2_, ...), custom_call_target="tpu_custom_call" | custom-call | flops 1 | bytes 1 | tf_op jit(solution)/shard_map/pallas_call | solution.py:481
  14.1 1.3 %shard_map.88 = (f32[160,256]{1,0:T(8,128)S(1)}, f32[160,256]{1,0:T(8,128)S(1)}, f32[160,256]{1,0:T(8,128)S(1)}, f32[160,256]{1,0:T(8,128)S(1)}, f32[128,256]{1,...) custom-call(s32[1]{0:T(128)} %bitcast.refs_0_, ...), custom_call_target="tpu_custom_call" | custom-call | flops 1 | bytes 1 | tf_op jit(solution)/shard_map/pallas_call | solution.py:481
  15.4 1.7 %collective-permute-done.10.refs_3_ = f32[136,256]{1,0:T(8,128)S(1)} collective-permute-done((f32[136,256]{1,0:T(8,128)S(1)}, f32[136,256]{1,0:T(8,128)S(1)}, u32[]{:S(2)}, u32[]{:S(2)}) %collective-permute-start.10) | collective-permute-done | bytes 139296 | tf_op jit(solution)/shard_map/ppermute | solution.py:454
  17.6 1.6 %collective-permute-start.6 = (f32[160,256]{1,0:T(8,128)S(1)}, f32[160,256]{1,0:T(8,128)S(1)}, u32[]{:S(2)}, u32[]{:S(2)}) collective-permute-start(f32[160,256]{1,0:T(8,128)S(1)} %get-tuple-element.58), channel_id=1, source_target_pairs={{0,2},{1,3},{2,0},{3,1},{4,6},{5,7},{6,4},{7,5},{8,10},{9,11},{10,... | collective-permute-start | bytes 491528 | tf_op jit(solution)/shard_map/ppermute | solution.py:454
  19.8 1.4 %collective-permute-start.8 = (f32[160,256]{1,0:T(8,128)S(1)}, f32[160,256]{1,0:T(8,128)S(1)}, u32[]{:S(2)}, u32[]{:S(2)}) collective-permute-start(f32[160,256]{1,0:T(8,128)S(1)} %get-tuple-element.60), channel_id=1, source_target_pairs={{0,6},{1,7},{2,4},{3,5},{4,2},{5,3},{6,0},{7,1},{8,14},{9,15},{10,... | collective-permute-start | bytes 491528 | tf_op jit(solution)/shard_map/ppermute | solution.py:454
  21.2 1.6 %collective-permute-start.13 = (f32[136,256]{1,0:T(8,128)S(1)}, f32[136,256]{1,0:T(8,128)S(1)}, u32[]{:S(2)}, u32[]{:S(2)}) collective-permute-start(f32[136,256]{1,0:T(8,128)S(1)} %get-tuple-element.63.refs_1_), channel_id=1, source_target_pairs={{0,8},{1,9},{2,10},{3,11},{4,12},{5,13},{6,14},{7,15},{8,0},{9,1},... | collective-permute-start | bytes 417800 | tf_op jit(solution)/shard_map/ppermute | solution.py:454
  22.8 3.6 %collective-permute-done.13.refs_2_.refs_6_ = f32[136,256]{1,0:T(8,128)S(1)} collective-permute-done((f32[136,256]{1,0:T(8,128)S(1)}, f32[136,256]{1,0:T(8,128)S(1)}, u32[]{:S(2)}, u32[]{:S(2)}) %collective-permute-start.13) | collective-permute-done | bytes 139296 | tf_op jit(solution)/shard_map/ppermute | solution.py:454
  27.0 2.0 %collective-permute-done.7.refs_3_ = f32[160,256]{1,0:T(8,128)S(1)} collective-permute-done((f32[160,256]{1,0:T(8,128)S(1)}, f32[160,256]{1,0:T(8,128)S(1)}, u32[]{:S(2)}, u32[]{:S(2)}) %collective-permute-start.7) | collective-permute-done | bytes 163872 | tf_op jit(solution)/shard_map/ppermute | solution.py:454
  29.1 1.7 %shard_map.93 = (f32[128,256]{1,0:T(8,128)S(1)}, f32[160,256]{1,0:T(8,128)S(1)}, f32[4,128,256]{2,1,0:T(8,128)S(1)}) custom-call(s32[1]{0:T(128)} %bitcast.refs_0_, f32[4,128,256]{2,1,0:T(8,128)S(1)} %get-tuple-element.65.refs_1_.refs_4_, f32[32,256]{1,0:T(8,128)S(1)} %get-tuple-element.66.refs_2_, ...), custom_call_target="tpu_custom_call" | custom-call | flops 1 | bytes 1 | tf_op jit(solution)/shard_map/pallas_call | solution.py:481
  30.8 1.6 %collective-permute-start.14 = (f32[160,256]{1,0:T(8,128)S(1)}, f32[160,256]{1,0:T(8,128)S(1)}, u32[]{:S(2)}, u32[]{:S(2)}) collective-permute-start(f32[160,256]{1,0:T(8,128)S(1)} %get-tuple-element.68.refs_3_), channel_id=1, source_target_pairs={{0,8},{1,9},{2,10},{3,11},{4,12},{5,13},{6,14},{7,15},{8,0},{9,1},... | collective-permute-start | bytes 491528 | tf_op jit(solution)/shard_map/ppermute | solution.py:454
  32.5 2.6 %collective-permute-start.16 = (f32[96,256]{1,0:T(8,128)S(1)}, f32[96,256]{1,0:T(8,128)S(1)}, u32[]{:S(2)}, u32[]{:S(2)}) collective-permute-start(f32[96,256]{1,0:T(8,128)S(1)} %shard_map.90.refs_4_), channel_id=1, source_target_pairs={{0,16},{1,17},{2,18},{3,19},{4,20},{5,21},{6,22},{7,23},{8,24},{9,... | collective-permute-start | bytes 294920 | tf_op jit(solution)/shard_map/ppermute | solution.py:454
  35.1 1.3 %collective-permute-done.14.refs_4_ = f32[160,256]{1,0:T(8,128)S(1)} collective-permute-done((f32[160,256]{1,0:T(8,128)S(1)}, f32[160,256]{1,0:T(8,128)S(1)}, u32[]{:S(2)}, u32[]{:S(2)}) %collective-permute-start.14) | collective-permute-done | bytes 163872 | tf_op jit(solution)/shard_map/ppermute | solution.py:454
  37.0 3.7 %collective-permute-start.18 = (f32[160,256]{1,0:T(8,128)S(1)}, f32[160,256]{1,0:T(8,128)S(1)}, u32[]{:S(2)}, u32[]{:S(2)}) collective-permute-start(f32[160,256]{1,0:T(8,128)S(1)} %get-tuple-element.74.refs_7_), channel_id=1, source_target_pairs={{0,16},{1,17},{2,18},{3,19},{4,20},{5,21},{6,22},{7,23},{8,24},{9,... | collective-permute-start | bytes 491528 | tf_op jit(solution)/shard_map/ppermute | solution.py:454
  40.7 1.8 %collective-permute-done.16.refs_4_ = f32[96,256]{1,0:T(8,128)S(1)} collective-permute-done((f32[96,256]{1,0:T(8,128)S(1)}, f32[96,256]{1,0:T(8,128)S(1)}, u32[]{:S(2)}, u32[]{:S(2)}) %collective-permute-start.16) | collective-permute-done | bytes 98336 | tf_op jit(solution)/shard_map/ppermute | solution.py:454
  42.5 1.3 %collective-permute-done.17.refs_5_ = f32[96,256]{1,0:T(8,128)S(1)} collective-permute-done((f32[96,256]{1,0:T(8,128)S(1)}, f32[96,256]{1,0:T(8,128)S(1)}, u32[]{:S(2)}, u32[]{:S(2)}) %collective-permute-start.17) | collective-permute-done | bytes 98336 | tf_op jit(solution)/shard_map/ppermute | solution.py:454
  43.8 3.9 %collective-permute-done.18.refs_8_ = f32[160,256]{1,0:T(8,128)S(1)} collective-permute-done((f32[160,256]{1,0:T(8,128)S(1)}, f32[160,256]{1,0:T(8,128)S(1)}, u32[]{:S(2)}, u32[]{:S(2)}) %collective-permute-start.18) | collective-permute-done | bytes 163872 | tf_op jit(solution)/shard_map/ppermute | solution.py:454
  49.0 1.4 %collective-permute-start.20 = (f32[192,256]{1,0:T(8,128)S(1)}, f32[192,256]{1,0:T(8,128)S(1)}, u32[]{:S(2)}, u32[]{:S(2)}) collective-permute-start(f32[192,256]{1,0:T(8,128)S(1)} %get-tuple-element.77), channel_id=1, source_target_pairs={{0,4},{1,5},{2,6},{3,7},{4,0},{5,1},{6,2},{7,3},{8,12},{9,13},{10,... | collective-permute-start | bytes 589832 | tf_op jit(solution)/shard_map/ppermute | solution.py:454
  50.5 1.5 %collective-permute-start.21 = (f32[192,256]{1,0:T(8,128)S(1)}, f32[192,256]{1,0:T(8,128)S(1)}, u32[]{:S(2)}, u32[]{:S(2)}) collective-permute-start(f32[192,256]{1,0:T(8,128)S(1)} %get-tuple-element.78), channel_id=1, source_target_pairs={{0,6},{1,7},{2,4},{3,5},{4,2},{5,3},{6,0},{7,1},{8,14},{9,15},{10,... | collective-permute-start | bytes 589832 | tf_op jit(solution)/shard_map/ppermute | solution.py:454
  53.1 3.2 %collective-permute-done.19.refs_2_ = f32[192,256]{1,0:T(8,128)S(1)} collective-permute-done((f32[192,256]{1,0:T(8,128)S(1)}, f32[192,256]{1,0:T(8,128)S(1)}, u32[]{:S(2)}, u32[]{:S(2)}) %collective-permute-start.19) | collective-permute-done | bytes 196640 | tf_op jit(solution)/shard_map/ppermute | solution.py:454
  56.3 3.5 %collective-permute-done.20.refs_3_ = f32[192,256]{1,0:T(8,128)S(1)} collective-permute-done((f32[192,256]{1,0:T(8,128)S(1)}, f32[192,256]{1,0:T(8,128)S(1)}, u32[]{:S(2)}, u32[]{:S(2)}) %collective-permute-start.20) | collective-permute-done | bytes 196640 | tf_op jit(solution)/shard_map/ppermute | solution.py:454
  60.9 1.3 %collective-permute-done.22.refs_9_ = f32[4,192,256]{2,1,0:T(8,128)S(1)} collective-permute-done((f32[4,192,256]{2,1,0:T(8,128)S(1)}, f32[4,192,256]{2,1,0:T(8,128)S(1)}, u32[]{:S(2)}, u32[]{:S(2)}) %collective-permute-start.22) | collective-permute-done | bytes 786464 | tf_op jit(solution)/shard_map/ppermute | solution.py:454
  62.2 1.5 %shard_map.99 = (f32[512,1024]{1,0:T(8,128)}, f32[512,256]{1,0:T(8,128)}, f32[256,256]{1,0:T(8,128)}) custom-call(s32[1]{0:T(128)} %bitcast.refs_0_, f32[192,256]{1,0:T(8,128)S(1)} %get-tuple-element.75.refs_4_.refs_1_, f32[192,256]{1,0:T(8,128)S(1)} %collective-permute-done.19.refs_2_, ...), custom_call_target="tpu_custom_call", output_to_operand_aliasing={{0}: (11, {}), {1}: (12, {})} | custom-call | flops 1 | bytes 1 | tf_op jit(solution)/shard_map/pallas_call | solution.py:481
  (41 shorter events, 9.6 us)
Async XLA Ops:
  0.6 5.4 %copy-start = (f32[256,256]{1,0:T(8,128)S(1)}, f32[256,256]{1,0:T(8,128)}, u32[]{:S(2)}) copy-start(f32[256,256]{1,0:T(8,128)} %refs_1_.3) | copy-start | bytes 786436
  0.7 5.4 %collective-permute-start = (f32[256,256]{1,0:T(8,128)}, f32[256,256]{1,0:T(8,128)S(1)}, u32[]{:S(2)}, u32[]{:S(2)}) collective-permute-start(f32[256,256]{1,0:T(8,128)} %refs_1_.3), channel_id=1, source_target_pairs={{0,1},{1,0},{2,3},{3,2},{4,5},{5,4},{6,7},{7,6},{8,9},{9,8},{10,11... | collective-permute-start | bytes 786440 | tf_op jit(solution)/shard_map/ppermute | solution.py:454
  1.2 4.8 %collective-permute-start.1 = (f32[256,256]{1,0:T(8,128)}, f32[256,256]{1,0:T(8,128)S(1)}, u32[]{:S(2)}, u32[]{:S(2)}) collective-permute-start(f32[256,256]{1,0:T(8,128)} %refs_2_.3), channel_id=1, source_target_pairs={{0,1},{1,0},{2,3},{3,2},{4,5},{5,4},{6,7},{7,6},{8,9},{9,8},{10,11... | collective-permute-start | bytes 786440 | tf_op jit(solution)/shard_map/ppermute | solution.py:454
  5.4 5.5 %collective-permute-start.2 = (f32[192,256]{1,0:T(8,128)S(1)}, f32[192,256]{1,0:T(8,128)S(1)}, u32[]{:S(2)}, u32[]{:S(2)}) collective-permute-start(f32[192,256]{1,0:T(8,128)S(1)} %get-tuple-element.51), channel_id=1, source_target_pairs={{0,1},{1,0},{2,3},{3,2},{4,5},{5,4},{6,7},{7,6},{8,9},{9,8},{10,11... | collective-permute-start | bytes 589832 | tf_op jit(solution)/shard_map/ppermute | solution.py:454
  5.9 5.0 %collective-permute-start.3 = (f32[192,256]{1,0:T(8,128)S(1)}, f32[192,256]{1,0:T(8,128)S(1)}, u32[]{:S(2)}, u32[]{:S(2)}) collective-permute-start(f32[192,256]{1,0:T(8,128)S(1)} %get-tuple-element.52), channel_id=1, source_target_pairs={{0,1},{1,0},{2,3},{3,2},{4,5},{5,4},{6,7},{7,6},{8,9},{9,8},{10,11... | collective-permute-start | bytes 589832 | tf_op jit(solution)/shard_map/ppermute | solution.py:454
  6.4 9.1 %collective-permute-start.11 = (f32[136,256]{1,0:T(8,128)S(1)}, f32[136,256]{1,0:T(8,128)S(1)}, u32[]{:S(2)}, u32[]{:S(2)}) collective-permute-start(f32[136,256]{1,0:T(8,128)S(1)} %get-tuple-element.61.refs_1_), channel_id=1, source_target_pairs={{0,6},{1,7},{2,4},{3,5},{4,2},{5,3},{6,0},{7,1},{8,14},{9,15},{10,... | collective-permute-start | bytes 417800 | tf_op jit(solution)/shard_map/ppermute | solution.py:454
  10.3 6.9 %collective-permute-start.10 = (f32[136,256]{1,0:T(8,128)S(1)}, f32[136,256]{1,0:T(8,128)S(1)}, u32[]{:S(2)}, u32[]{:S(2)}) collective-permute-start(f32[136,256]{1,0:T(8,128)S(1)} %get-tuple-element.61.refs_1_), channel_id=1, source_target_pairs={{0,4},{1,5},{2,6},{3,7},{4,0},{5,1},{6,2},{7,3},{8,12},{9,13},{10,... | collective-permute-start | bytes 417800 | tf_op jit(solution)/shard_map/ppermute | solution.py:454
  10.8 6.7 %collective-permute-start.9 = (f32[136,256]{1,0:T(8,128)S(1)}, f32[136,256]{1,0:T(8,128)S(1)}, u32[]{:S(2)}, u32[]{:S(2)}) collective-permute-start(f32[136,256]{1,0:T(8,128)S(1)} %get-tuple-element.61.refs_1_), channel_id=1, source_target_pairs={{0,2},{1,3},{2,0},{3,1},{4,6},{5,7},{6,4},{7,5},{8,10},{9,11},{10,... | collective-permute-start | bytes 417800 | tf_op jit(solution)/shard_map/ppermute | solution.py:454
  12.5 1.4 %collective-permute-start.4 = (f32[128,256]{1,0:T(8,128)S(1)}, f32[128,256]{1,0:T(8,128)S(1)}, u32[]{:S(2)}, u32[]{:S(2)}) collective-permute-start(f32[128,256]{1,0:T(8,128)S(1)} %get-tuple-element.54), channel_id=1, source_target_pairs={{0,1},{1,0},{2,3},{3,2},{4,5},{5,4},{6,7},{7,6},{8,9},{9,8},{10,11... | collective-permute-start | bytes 393224 | tf_op jit(solution)/shard_map/ppermute | solution.py:454
  12.6 1.5 %collective-permute-start.5 = (f32[128,256]{1,0:T(8,128)S(1)}, f32[128,256]{1,0:T(8,128)S(1)}, u32[]{:S(2)}, u32[]{:S(2)}) collective-permute-start(f32[128,256]{1,0:T(8,128)S(1)} %get-tuple-element.55), channel_id=1, source_target_pairs={{0,1},{1,0},{2,3},{3,2},{4,5},{5,4},{6,7},{7,6},{8,9},{9,8},{10,11... | collective-permute-start | bytes 393224 | tf_op jit(solution)/shard_map/ppermute | solution.py:454
  17.6 8.8 %collective-permute-start.12 = (f32[3,136,256]{2,1,0:T(8,128)S(1)}, f32[3,136,256]{2,1,0:T(8,128)S(1)}, u32[]{:S(2)}, u32[]{:S(2)}) collective-permute-start(f32[3,136,256]{2,1,0:T(8,128)S(1)} %get-tuple-element.62.refs_3_.refs_2_), channel_id=1, source_target_pairs={{0,1},{1,0},{2,3},{3,2},{4,5},{5,4},{6,7},{7,6},{8,9},{9,8},{10,11... | collective-permute-start | bytes 1253384 | tf_op jit(solution)/shard_map/ppermute | solution.py:454
  17.6 9.3 %collective-permute-start.6 = (f32[160,256]{1,0:T(8,128)S(1)}, f32[160,256]{1,0:T(8,128)S(1)}, u32[]{:S(2)}, u32[]{:S(2)}) collective-permute-start(f32[160,256]{1,0:T(8,128)S(1)} %get-tuple-element.58), channel_id=1, source_target_pairs={{0,2},{1,3},{2,0},{3,1},{4,6},{5,7},{6,4},{7,5},{8,10},{9,11},{10,... | collective-permute-start | bytes 491528 | tf_op jit(solution)/shard_map/ppermute | solution.py:454
  19.2 9.8 %collective-permute-start.7 = (f32[160,256]{1,0:T(8,128)S(1)}, f32[160,256]{1,0:T(8,128)S(1)}, u32[]{:S(2)}, u32[]{:S(2)}) collective-permute-start(f32[160,256]{1,0:T(8,128)S(1)} %get-tuple-element.59), channel_id=1, source_target_pairs={{0,4},{1,5},{2,6},{3,7},{4,0},{5,1},{6,2},{7,3},{8,12},{9,13},{10,... | collective-permute-start | bytes 491528 | tf_op jit(solution)/shard_map/ppermute | solution.py:454
  19.8 9.2 %collective-permute-start.8 = (f32[160,256]{1,0:T(8,128)S(1)}, f32[160,256]{1,0:T(8,128)S(1)}, u32[]{:S(2)}, u32[]{:S(2)}) collective-permute-start(f32[160,256]{1,0:T(8,128)S(1)} %get-tuple-element.60), channel_id=1, source_target_pairs={{0,6},{1,7},{2,4},{3,5},{4,2},{5,3},{6,0},{7,1},{8,14},{9,15},{10,... | collective-permute-start | bytes 491528 | tf_op jit(solution)/shard_map/ppermute | solution.py:454
  21.2 5.2 %collective-permute-start.13 = (f32[136,256]{1,0:T(8,128)S(1)}, f32[136,256]{1,0:T(8,128)S(1)}, u32[]{:S(2)}, u32[]{:S(2)}) collective-permute-start(f32[136,256]{1,0:T(8,128)S(1)} %get-tuple-element.63.refs_1_), channel_id=1, source_target_pairs={{0,8},{1,9},{2,10},{3,11},{4,12},{5,13},{6,14},{7,15},{8,0},{9,1},... | collective-permute-start | bytes 417800 | tf_op jit(solution)/shard_map/ppermute | solution.py:454
  30.8 5.5 %collective-permute-start.14 = (f32[160,256]{1,0:T(8,128)S(1)}, f32[160,256]{1,0:T(8,128)S(1)}, u32[]{:S(2)}, u32[]{:S(2)}) collective-permute-start(f32[160,256]{1,0:T(8,128)S(1)} %get-tuple-element.68.refs_3_), channel_id=1, source_target_pairs={{0,8},{1,9},{2,10},{3,11},{4,12},{5,13},{6,14},{7,15},{8,0},{9,1},... | collective-permute-start | bytes 491528 | tf_op jit(solution)/shard_map/ppermute | solution.py:454
  32.5 2.6 %collective-permute-start.15 = (f32[136,256]{1,0:T(8,128)S(1)}, f32[136,256]{1,0:T(8,128)S(1)}, u32[]{:S(2)}, u32[]{:S(2)}) collective-permute-start(f32[136,256]{1,0:T(8,128)S(1)} %collective-permute-done.13.refs_2_.refs_6_), channel_id=1, source_target_pairs={{0,1},{1,0},{2,3},{3,2},{4,5},{5,4},{6,7},{7,6},{8,9},{9,8},{10,11... | collective-permute-start | bytes 417800 | tf_op jit(solution)/shard_map/ppermute | solution.py:454
  32.5 10.0 %collective-permute-start.16 = (f32[96,256]{1,0:T(8,128)S(1)}, f32[96,256]{1,0:T(8,128)S(1)}, u32[]{:S(2)}, u32[]{:S(2)}) collective-permute-start(f32[96,256]{1,0:T(8,128)S(1)} %shard_map.90.refs_4_), channel_id=1, source_target_pairs={{0,16},{1,17},{2,18},{3,19},{4,20},{5,21},{6,22},{7,23},{8,24},{9,... | collective-permute-start | bytes 294920 | tf_op jit(solution)/shard_map/ppermute | solution.py:454
  37.0 10.7 %collective-permute-start.18 = (f32[160,256]{1,0:T(8,128)S(1)}, f32[160,256]{1,0:T(8,128)S(1)}, u32[]{:S(2)}, u32[]{:S(2)}) collective-permute-start(f32[160,256]{1,0:T(8,128)S(1)} %get-tuple-element.74.refs_7_), channel_id=1, source_target_pairs={{0,16},{1,17},{2,18},{3,19},{4,20},{5,21},{6,22},{7,23},{8,24},{9,... | collective-permute-start | bytes 491528 | tf_op jit(solution)/shard_map/ppermute | solution.py:454
  42.5 1.3 %collective-permute-start.17 = (f32[96,256]{1,0:T(8,128)S(1)}, f32[96,256]{1,0:T(8,128)S(1)}, u32[]{:S(2)}, u32[]{:S(2)}) collective-permute-start(f32[96,256]{1,0:T(8,128)S(1)} %collective-permute-done.16.refs_4_), channel_id=1, source_target_pairs={{0,1},{1,0},{2,3},{3,2},{4,5},{5,4},{6,7},{7,6},{8,9},{9,8},{10,11... | collective-permute-start | bytes 294920 | tf_op jit(solution)/shard_map/ppermute | solution.py:454
  48.5 7.8 %collective-permute-start.19 = (f32[192,256]{1,0:T(8,128)S(1)}, f32[192,256]{1,0:T(8,128)S(1)}, u32[]{:S(2)}, u32[]{:S(2)}) collective-permute-start(f32[192,256]{1,0:T(8,128)S(1)} %get-tuple-element.76), channel_id=1, source_target_pairs={{0,2},{1,3},{2,0},{3,1},{4,6},{5,7},{6,4},{7,5},{8,10},{9,11},{10,... | collective-permute-start | bytes 589832 | tf_op jit(solution)/shard_map/ppermute | solution.py:454
  49.0 10.7 %collective-permute-start.20 = (f32[192,256]{1,0:T(8,128)S(1)}, f32[192,256]{1,0:T(8,128)S(1)}, u32[]{:S(2)}, u32[]{:S(2)}) collective-permute-start(f32[192,256]{1,0:T(8,128)S(1)} %get-tuple-element.77), channel_id=1, source_target_pairs={{0,4},{1,5},{2,6},{3,7},{4,0},{5,1},{6,2},{7,3},{8,12},{9,13},{10,... | collective-permute-start | bytes 589832 | tf_op jit(solution)/shard_map/ppermute | solution.py:454
  50.5 9.3 %collective-permute-start.21 = (f32[192,256]{1,0:T(8,128)S(1)}, f32[192,256]{1,0:T(8,128)S(1)}, u32[]{:S(2)}, u32[]{:S(2)}) collective-permute-start(f32[192,256]{1,0:T(8,128)S(1)} %get-tuple-element.78), channel_id=1, source_target_pairs={{0,6},{1,7},{2,4},{3,5},{4,2},{5,3},{6,0},{7,1},{8,14},{9,15},{10,... | collective-permute-start | bytes 589832 | tf_op jit(solution)/shard_map/ppermute | solution.py:454
  59.8 2.4 %collective-permute-start.22 = (f32[4,192,256]{2,1,0:T(8,128)S(1)}, f32[4,192,256]{2,1,0:T(8,128)S(1)}, u32[]{:S(2)}, u32[]{:S(2)}) collective-permute-start(f32[4,192,256]{2,1,0:T(8,128)S(1)} %shard_map.97.refs_10_.refs_13_), channel_id=1, source_target_pairs={{0,1},{1,0},{2,3},{3,2},{4,5},{5,4},{6,7},{7,6},{8,9},{9,8},{10,11... | collective-permute-start | bytes 2359304 | tf_op jit(solution)/shard_map/ppermute | solution.py:454
  (1 other events, 5.4 us)

commit v2 on v1

--- a/solution.py
+++ b/solution.py
@@ -217,9 +217,9 @@
 def core_kernel(
     me_ref, own_a_ref, own_b_ref, one_ref, two_ref, *refs
 ):
-    more = len(refs) - 11
+    more = len(refs) - 12
     there_bs, packed_ref = refs[:more], refs[more]
-    sends, dones, (low_ref, high_ref) = refs[more + 1 : more + 5], refs[more + 5 : more + 9], refs[more + 9 :]
+    sends, dones, (gram_ref, low_ref, high_ref) = refs[more + 1 : more + 5], refs[more + 5 : more + 9], refs[more + 9 :]
     me = me_ref[0]
     width = own_a_ref.shape[1]
     half = width // 2
@@ -228,23 +228,21 @@
     count = cut // half + len(there_bs)
     odd = me % 2 == 1
     there_a = jnp.concatenate([one_ref[...], two_ref[...]], axis=0)
-    gram = own_a_ref[cut:] + there_a[cut:]
+    gram_ref[...] = own_a_ref[cut:] + there_a[cut:]
     mine = jnp.concatenate([own_a_ref[:cut], own_b_ref[...]], axis=0)
     there = jnp.concatenate([there_a[:cut]] + [ref[...] for ref in there_bs], axis=0)
     low = jnp.where(odd, there, mine)
     high = jnp.where(odd, mine, there)
     low, high = tree_node(low, high, unpack(packed_ref[0], packed_ref[1]))
-    low_ref[: count * half] = low
-    low_ref[count * half :] = gram
+    low_ref[...] = low
     high_ref[...] = high
     for r in range(4):
         start = (place(me) ^ r) * quarter
-        for b in range(count + 1):
+        for b in range(count):
             source = pl.ds(pl.multiple_of(b * half + start, quarter), quarter)
             target = slice(b * quarter, (b + 1) * quarter)
             sends[r][target] = low_ref[source]
-            if b < count:
-                dones[r][target] = high_ref[source]
+            dones[r][target] = high_ref[source]
 
 
 def gather_kernel(me_ref, *refs):
@@ -260,12 +258,19 @@
 
 
 def sort_kernel(me_ref, *refs):
-    gots, (heads_ref, gram_ref) = refs[:4], refs[4:]
-    cols = heads_ref.shape[1]
-    parts = [ref[:cols] for ref in gots]
+    parts = [ref[...] for ref in refs[:4]]
     for j in range(4):
-        heads_ref[j] = by_place(me_ref[0], parts, j)
-    gram_ref[...] = gots[0][cols:] + gots[1][cols:] + (gots[2][cols:] + gots[3][cols:])
+        refs[4][j] = by_place(me_ref[0], parts, j)
+
+
+def add_kernel(me_ref, first_ref, second_ref, out_ref):
+    out_ref[...] = first_ref[...] + second_ref[...]
+
+
+def fill(send_ref, value):
+    cols = value.shape[0]
+    send_ref[:cols] = value
+    send_ref[cols:] = jnp.zeros_like(send_ref[cols:])
 
 
 def prepare_kernel(me_ref, packed_ref, stack_ref, stack_there_ref, ready_ref, held_ref):
@@ -279,8 +284,7 @@
         (ready_ref[j, 0], ready_ref[j, 1]), (ready_ref[j, 2], ready_ref[j, 3]) = unpack(*pairs[j])
 
 
-def plane_kernel(me_ref, heads_ref, gram_ref, ready_ref, head_ref, send_ref, done_ref, *, level):
-    cols = done_ref.shape[1]
+def plane_kernel(me_ref, heads_ref, ready_ref, head_ref, send_ref, done_ref, *, level):
     reflectors = [((ready_ref[j, 0], ready_ref[j, 1]), (ready_ref[j, 2], ready_ref[j, 3])) for j in range(4)]
     heads = [heads_ref[j] for j in range(4)]
     heads[0], heads[1] = tree_node(heads[0], heads[1], reflectors[1])
@@ -290,86 +294,61 @@
         done_ref[j] = heads[j]
     head_ref[...] = heads[0]
     upper = (me_ref[0] >> level) % 2 == 1
-    send_ref[:cols] = jnp.where(upper, plain(halves(heads[0]), reflectors[0][0]), heads[0])
-    send_ref[cols:] = gram_ref[...]
-
-
-def line_node(me, head, result, mine, there, held, part_ref, part_there_ref, level):
-    cols = head.shape[0]
+    fill(send_ref, jnp.where(upper, plain(halves(heads[0]), reflectors[0][0]), heads[0]))
+
+
+def line_node(me_ref, head_ref, result_ref, mine_ref, there_ref, held_ref, part_ref, part_there_ref, level):
+    me = me_ref[0]
+    cols = head_ref.shape[0]
     upper = (me >> level) % 2 == 1
+    held = held_ref[0], held_ref[1]
     others = by_core(me % 2, part_ref[...], part_there_ref[...])
     whole = held[0].shape == others[0].shape
     need = held[0].shape[1] // 4 + EXTRA
     node = [jnp.where(upper, a[:need], b[:need]) for a, b in zip(held, others)]
     following = [jnp.where(upper, b, a) for a, b in zip(held, others)] if whole else None
-    coeffs = by_transpose(halves(mine[:cols] + there[:cols]), unpack_factors(*node))
-    low = jnp.where(upper, there[:cols], head) - coeffs
+    head, there = head_ref[...], there_ref[:cols]
+    coeffs = by_transpose(halves(mine_ref[:cols] + there), unpack_factors(*node))
+    low = jnp.where(upper, there, head) - coeffs
     plane = me >> 3
     below = (1 << (level - 2)) - 1
     second = (plane & below) == (1 << (level - 3))
     high = head - by_transpose(halves(coeffs), unpack_vectors(*held))
-    result = jnp.where(second, high, result)
-    return low, result, mine[cols:] + there[cols:], following
-
-
-def line_kernel(me_ref, *refs, level, cut):
-    head_ref, result_ref, mine_ref, there_ref, held_ref, part_ref, part_there_ref, head_out, result_out, held_out = refs[:10]
-    sends = refs[10:]
-    me = me_ref[0]
-    held = held_ref[0], held_ref[1]
-    low, result, gram, following = line_node(
-        me, head_ref[...], result_ref[...], mine_ref[...], there_ref[...], held, part_ref, part_there_ref, level
-    )
-    cols, quarter = low.shape[0], gram.shape[0]
-    ahead = (me >> (level + 1)) % 2 == 1
+    return low, jnp.where(second, high, result_ref[...]), following
+
+
+def line_kernel(me_ref, *refs, level):
+    head_out, result_out, held_out, send_ref = refs[7:]
+    low, result, following = line_node(me_ref, *refs[:7], level)
+    ahead = (me_ref[0] >> (level + 1)) % 2 == 1
     head_out[...] = low
     result_out[...] = result
     held_out[0], held_out[1] = following
-    value = jnp.where(ahead, plain(halves(low), unpack_vectors(*following)), low)
-    if cut:
-        sends[0][:quarter] = value[:quarter]
-        sends[0][quarter:] = gram
-        sends[1][...] = value[quarter:]
-    else:
-        sends[0][:cols] = value
-        sends[0][cols:] = gram
-
-
-def last_kernel(me_ref, *refs, level, cut):
-    head_ref, result_ref, held_ref, part_ref, part_there_ref, done_ref = refs[:6]
-    number = 2 if cut else 1
-    mines, theres = refs[6 : 6 + number], refs[6 + number : 6 + 2 * number]
-    sends, all_ref = refs[6 + 2 * number : 10 + 2 * number], refs[10 + 2 * number]
+    fill(send_ref, jnp.where(ahead, plain(halves(low), unpack_vectors(*following)), low))
+
+
+def last_kernel(me_ref, *refs, level):
+    done_ref, sends, all_ref = refs[7], refs[8:12], refs[12]
     me = me_ref[0]
-    cols = head_ref.shape[0]
-    quarter = sends[0].shape[0] - cols
-    quarter = quarter // 2
-    values = []
-    for parts in (mines, theres):
-        if cut:
-            values.append(jnp.concatenate([parts[0][:quarter], parts[1][...], parts[0][quarter:]], axis=0))
-        else:
-            values.append(parts[0][...])
-    held = held_ref[0], held_ref[1]
-    low, result, gram, _ = line_node(
-        me, head_ref[...], result_ref[...], values[0], values[1], held, part_ref, part_there_ref, level
-    )
+    low, result, _ = line_node(me_ref, *refs[:7], level)
+    cols = low.shape[0]
     all_ref[0] = jnp.where((me >> 3) == 0, low, result)
     for j in range(1, 4):
         all_ref[j] = done_ref[j]
     for r in range(4):
         sends[r][:cols] = all_ref[place(me) ^ r]
-        sends[r][cols : cols + quarter] = low[:quarter]
-        sends[r][cols + quarter :] = gram
+        sends[r][cols:] = low[: sends[r].shape[0] - cols]
 
 
 def pass_kernel(me_ref, *refs):
-    backs, dones, out_ref = refs[:4], refs[4:8], refs[8]
+    backs, dones, (gram_ref, out_ref) = refs[:4], refs[4:8], refs[8:]
     odd = me_ref[0] % 2 == 1
-    cols = dones[0].shape[0]
+    cols, rows = dones[0].shape[0], backs[0].shape[0]
+    quarter = rows - cols
     for r in range(4):
         out_ref[r, :cols] = jnp.where(odd, backs[r][:cols], dones[r][...])
-        out_ref[r, cols:] = backs[r][cols:]
+        out_ref[r, cols:rows] = backs[r][cols:]
+        out_ref[r, rows:] = gram_ref[r * quarter : (r + 1) * quarter]
 
 
 def near_kernel(me_ref, *refs):
@@ -393,8 +372,8 @@
 
 def far_kernel(me_ref, *refs, total):
     backs, dones = refs[:4], refs[4:8]
-    there_ref, inverse_ref, _, _, updated_hbm, basis_hbm, gram_hbm = refs[8:15]
-    panel_ref, sum_ref, out_ref, basis_ref, gram_ref, sems = refs[15:]
+    there_ref, half_ref, inverse_ref, _, _, updated_hbm, basis_hbm, gram_hbm = refs[8:16]
+    panel_ref, sum_ref, out_ref, basis_ref, gram_ref, sems = refs[16:]
     count, width, half = out_ref.shape
     quarter = half // 4
     cols = count * quarter
@@ -426,10 +405,11 @@
         return pl.ds(pl.multiple_of(part * half + (place(me) ^ r) * quarter, quarter), quarter)
 
     for r in range(4):
-        panel_ref[target(core, r)] = backs[r][cols : cols + quarter]
-        sum_ref[target(core, r)] = backs[r][cols + quarter :]
+        panel_ref[target(core, r)] = backs[r][cols:]
         panel_ref[target(1 - core, r)] = there_ref[r, cols : cols + quarter]
-        sum_ref[target(1 - core, r)] = there_ref[r, cols + quarter :]
+        rows = pl.ds(pl.multiple_of((1 - core) * half + r * quarter, quarter), quarter)
+        sum_ref[rows] = there_ref[r, cols + quarter :]
+    sum_ref[pl.ds(pl.multiple_of(core * half, half), half)] = half_ref[...]
     panel = halves(panel_ref[...])
     gram_ref[...] = (sum_ref[...] - by_transpose(panel, panel)) / total
     put(gram_ref, gram_hbm)
@@ -528,10 +508,14 @@
     cols = count * quarter
     outs = call(
         core_kernel, (own_a, own_b, *there_a, *theres, chip_high),
-        [shape(cols + quarter, width)] * 4 + [shape(cols, width)] * 4,
-        [vmem(count * half + half, width), vmem(count * half, width)],
-    )
-    sends, dones = outs[:4], outs[4:]
+        [shape(cols, width)] * 8 + [shape(half, width)],
+        [vmem(count * half, width), vmem(count * half, width)],
+    )
+    sends, dones, gram_half = outs[:4], outs[4:8], outs[8]
+    for level in (levels - 1, 1, 2, *range(3, levels - 1)):
+        (gram_half,) = call(
+            add_kernel, (gram_half, exchange(gram_half, 1 << level)), (shape(half, width),), chained=False
+        )
     stack, held_part = call(
         gather_kernel, (chip_part, *plane_parts), (shape(3, *part_shape), shape(*part_shape)), work=1,
     )
@@ -542,6 +526,7 @@
         short = 3 * quarter if level == levels - 1 else half + EXTRA
         (held_part,) = call(
             functools.partial(hold_kernel, level=level - 1), (held_part, parts[-1]), (shape(short, width),),
+            chained=False,
         )
         parts.append(exchange(held_part, 1 << level))
 
@@ -549,42 +534,32 @@
         prepare_kernel, (chip_low, stack, stack_there),
         (jax.ShapeDtypeStruct((4, 4, width, width), BF16), shape(2, *part_shape)),
     )
-    heads, gram_part = call(
-        sort_kernel, gots, (shape(4, cols, width), shape(quarter, width)), work=1,
-    )
+    (heads,) = call(sort_kernel, gots, (shape(4, cols, width),))
     head, send, plane_done = call(
-        functools.partial(plane_kernel, level=3), (heads, gram_part, ready),
-        (shape(cols, width), shape(cols + quarter, width), shape(4, cols, width)),
+        functools.partial(plane_kernel, level=3), (heads, ready),
+        (shape(cols, width), shape(cols + 24, width), shape(4, cols, width)),
     )
     result = head
-    mines, theres = [send], [exchange(send, 8)]
     for level in range(3, levels):
         part = parts[level - 3]
-        part_there = exchange(part, 1)
+        operands = (head, result, send, exchange(send, 1 << level), held, part, exchange(part, 1))
         if level == levels - 1:
             sends = call(
-                functools.partial(last_kernel, level=level, cut=len(mines) == 2),
-                (head, result, held, part, part_there, plane_done, *mines, *theres),
-                [shape(cols + 2 * quarter, width)] * 4, [vmem(4, cols, width)],
+                functools.partial(last_kernel, level=level), (*operands, plane_done),
+                [shape(cols + quarter, width)] * 4, [vmem(4, cols, width)],
             )
         else:
-            cut = False
-            outs = [shape(2 * quarter, width), shape(cols - quarter, width)] if cut else [shape(cols + quarter, width)]
-            head, result, held, *outs = call(
-                functools.partial(line_kernel, level=level, cut=cut),
-                (head, result, mines[0], theres[0], held, part, part_there),
-                [shape(cols, width), shape(cols, width), shape(*held.shape)] + outs,
+            head, result, held, send = call(
+                functools.partial(line_kernel, level=level), operands,
+                [shape(cols, width), shape(cols, width), shape(*held.shape), shape(cols + 8, width)],
             )
-            mines, theres = outs, [exchange(outs[0], 2 << level)]
-            if cut:
-                theres.append(among(outs[1], 2 << level, lambda i: (i >> 3) % (1 << (level - 2)) == 0))
 
     backs = around(sends)
     _, updated, basis = call(
         store_kernel, (rest_a, rest_b, inverse_factor), (shape(8, width), shape(rows, columns), shape(rows, width)),
         [vmem(width, width), sems(count + 1)], (), (1, 2),
     )
-    (back,) = call(pass_kernel, (*backs, *dones), (shape(4, cols + 2 * quarter, width),))
+    (back,) = call(pass_kernel, (*backs, *dones, gram_half), (shape(4, cols + 2 * quarter, width),))
     there = exchange(back, 1)
     (updated,) = call(
         near_kernel, (*backs, *dones, updated), (shape(rows, columns),),
@@ -592,10 +567,10 @@
     )
     return call(
         functools.partial(far_kernel, total=float(rows * devices)),
-        (*backs, *dones, there, inverse_factor, updated, basis),
+        (*backs, *dones, there, gram_half, inverse_factor, updated, basis),
         (shape(rows, columns), shape(rows, width), shape(width, width)),
         [vmem(width, width), vmem(width, width), vmem(count, width, half), vmem(width, width), vmem(width, width), sems(count + 2)],
-        (10, 11), (0, 1, 2), {11: 0, 12: 1},
+        (11, 12), (0, 1, 2), {12: 0, 13: 1},
     )
 
 

time: 63.8 us -> 60.9 us (0.955)
  waiting for transfers between devices: 24.9 us -> 17.4 us
  starting transfers between devices: 23.1 us -> 27.6 us
    ppermute x23 -> x27, waiting for transfers between devices: 24.9 us -> 17.4 us  [exchange(): return lax.ppermute(value, 'rows', [(i, i ^ shift) for i in range(devices)])]
    ppermute x23 -> x27, starting transfers between devices: 23.1 us -> 27.6 us  [exchange(): return lax.ppermute(value, 'rows', [(i, i ^ shift) for i in range(devices)])]
    pallas_call x15 -> x19, Pallas kernels: 14.8 us -> 14.8 us  [call(): pl.pallas_call(kernel_on, out_shape=tuple(outs), in_specs=[SCALAR] + [AWA...]
  transfers between devices with their start and end apart: 23 -> 27, of which waited for: 13 -> 12; matrix products, arithmetic and copies ran while one was open for 0% -> 0% of each run, Pallas kernels for 17% -> 22%
where the time goes in v2:
time: 60.9 us; the launch traced here: 60.8 us
  starting transfers between devices  27.6 us (45%)
  waiting for transfers between devices  17.4 us (29%)
  Pallas kernels  14.8 us (24%)
  between operations  0.83 us (1%)
    ppermute x27, starting transfers between devices, exchange(): return lax.ppermute(value, 'rows', [(i, i ^ shift) for i in range(devices)])  27.6 us
    ppermute x27, waiting for transfers between devices, exchange(): return lax.ppermute(value, 'rows', [(i, i ^ shift) for i in range(devices)])  17.4 us
    pallas_call x19, Pallas kernels, call(): pl.pallas_call(kernel_on, out_shape=tuple(outs), in_specs=[SCALAR] + [AWA...  14.8 us
  transfers between devices with their start and end apart: 27, of which 12 were waited for; matrix products, arithmetic and copies ran while one was open for 0% of the time, Pallas kernels for 22%

profile of v2, /device:TPU:0, one launch (start us, length us, event | category | flops | bytes accessed | tf_op | source)
XLA Modules:
  0.0 60.8 jit_solution(9068605796694848137)
XLA Ops:
  1.2 4.2 %shard_map.85 = (f32[384,256]{1,0:T(8,128)S(1)}, f32[192,256]{1,0:T(8,128)S(1)}, f32[192,256]{1,0:T(8,128)S(1)}, f32[2,256,256]{2,1,0:T(8,128)S(1)}, f32[2,512,2...) custom-call(s32[1]{0:T(128)} %bitcast.refs_0_, ...), custom_call_target="tpu_custom_call" | custom-call | flops 1 | bytes 1 | tf_op jit(solution)/shard_map/pallas_call | solution.py:461
  6.4 3.9 %collective-permute-start.11 = (f32[136,256]{1,0:T(8,128)S(1)}, f32[136,256]{1,0:T(8,128)S(1)}, u32[]{:S(2)}, u32[]{:S(2)}) collective-permute-start(f32[136,256]{1,0:T(8,128)S(1)} %get-tuple-element.60.refs_1_), channel_id=1, source_target_pairs={{0,6},{1,7},{2,4},{3,5},{4,2},{5,3},{6,0},{7,1},{8,14},{9,15},{10,... | collective-permute-start | bytes 417800 | tf_op jit(solution)/shard_map/ppermute | solution.py:434
  10.9 1.6 %shard_map.87 = (f32[256,256]{1,0:T(8,128)S(1)}, f32[2,256,256]{2,1,0:T(8,128)S(1)}, f32[128,256]{1,0:T(8,128)S(1)}, f32[128,256]{1,0:T(8,128)S(1)}) custom-call(s32[1]{0:T(128)} %bitcast.refs_0_, f32[2,512,256]{2,1,0:T(8,128)S(1)} %get-tuple-element.46.refs_1_, bf16[2,256,512]{2,1,0:T(8,128)(2,1)S(1)} %get-tuple-element.47.refs_2_, ...), custom_call_target="tpu_custom_call" | custom-call | flops 1 | bytes 1 | tf_op jit(solution)/shard_map/pallas_call | solution.py:461
  14.1 1.3 %shard_map.88 = (f32[128,256]{1,0:T(8,128)S(1)}, f32[128,256]{1,0:T(8,128)S(1)}, f32[128,256]{1,0:T(8,128)S(1)}, f32[128,256]{1,0:T(8,128)S(1)}, f32[128,256]{1,...) custom-call(s32[1]{0:T(128)} %bitcast.refs_0_, ...), custom_call_target="tpu_custom_call" | custom-call | flops 1 | bytes 1 | tf_op jit(solution)/shard_map/pallas_call | solution.py:461
  15.4 1.7 %collective-permute-done.10.refs_3_ = f32[136,256]{1,0:T(8,128)S(1)} collective-permute-done((f32[136,256]{1,0:T(8,128)S(1)}, f32[136,256]{1,0:T(8,128)S(1)}, u32[]{:S(2)}, u32[]{:S(2)}) %collective-permute-start.10) | collective-permute-done | bytes 139296 | tf_op jit(solution)/shard_map/ppermute | solution.py:434
  17.6 1.6 %collective-permute-start.6 = (f32[128,256]{1,0:T(8,128)S(1)}, f32[128,256]{1,0:T(8,128)S(1)}, u32[]{:S(2)}, u32[]{:S(2)}) collective-permute-start(f32[128,256]{1,0:T(8,128)S(1)} %get-tuple-element.57), channel_id=1, source_target_pairs={{0,2},{1,3},{2,0},{3,1},{4,6},{5,7},{6,4},{7,5},{8,10},{9,11},{10,... | collective-permute-start | bytes 393224 | tf_op jit(solution)/shard_map/ppermute | solution.py:434
  19.8 1.4 %collective-permute-start.8 = (f32[128,256]{1,0:T(8,128)S(1)}, f32[128,256]{1,0:T(8,128)S(1)}, u32[]{:S(2)}, u32[]{:S(2)}) collective-permute-start(f32[128,256]{1,0:T(8,128)S(1)} %get-tuple-element.59), channel_id=1, source_target_pairs={{0,6},{1,7},{2,4},{3,5},{4,2},{5,3},{6,0},{7,1},{8,14},{9,15},{10,... | collective-permute-start | bytes 393224 | tf_op jit(solution)/shard_map/ppermute | solution.py:434
  21.2 1.6 %collective-permute-start.14 = (f32[136,256]{1,0:T(8,128)S(1)}, f32[136,256]{1,0:T(8,128)S(1)}, u32[]{:S(2)}, u32[]{:S(2)}) collective-permute-start(f32[136,256]{1,0:T(8,128)S(1)} %get-tuple-element.66.refs_1_), channel_id=1, source_target_pairs={{0,8},{1,9},{2,10},{3,11},{4,12},{5,13},{6,14},{7,15},{8,0},{9,1},... | collective-permute-start | bytes 417800 | tf_op jit(solution)/shard_map/ppermute | solution.py:434
  22.8 2.6 %collective-permute-start.22 = (f32[128,256]{1,0:T(8,128)S(1)}, f32[128,256]{1,0:T(8,128)S(1)}, u32[]{:S(2)}, u32[]{:S(2)}) collective-permute-start(f32[128,256]{1,0:T(8,128)S(1)} %get-tuple-element.80.refs_1_), channel_id=1, source_target_pairs={{0,16},{1,17},{2,18},{3,19},{4,20},{5,21},{6,22},{7,23},{8,24},{9,... | collective-permute-start | bytes 393224 | tf_op jit(solution)/shard_map/ppermute | solution.py:434
  25.9 1.7 %collective-permute-done.7.refs_3_ = f32[128,256]{1,0:T(8,128)S(1)} collective-permute-done((f32[128,256]{1,0:T(8,128)S(1)}, f32[128,256]{1,0:T(8,128)S(1)}, u32[]{:S(2)}, u32[]{:S(2)}) %collective-permute-start.7) | collective-permute-done | bytes 131104 | tf_op jit(solution)/shard_map/ppermute | solution.py:434
  27.7 1.7 %shard_map.92 = (f32[128,256]{1,0:T(8,128)S(1)}, f32[152,256]{1,0:T(8,128)S(1)}, f32[4,128,256]{2,1,0:T(8,128)S(1)}) custom-call(s32[1]{0:T(128)} %bitcast.refs_0_, f32[4,128,256]{2,1,0:T(8,128)S(1)} %shard_map.91.refs_1_.refs_3_, bf16[4,4,256,256]{3,2,1,0:T(8,128)(2,1)S(1)} %get-tuple-element.62.refs_5_.refs_2_, f32[4,128,256]{2,1,0:T(8,128)S(1)} %shard_map.91.refs_1_.refs_3_), custom_call_target="tpu_custom_call" | custom-call | flops 1 | bytes 1 | tf_op jit(solution)/shard_map/pallas_call | solution.py:461
  29.4 1.6 %collective-permute-start.13 = (f32[152,256]{1,0:T(8,128)S(1)}, f32[152,256]{1,0:T(8,128)S(1)}, u32[]{:S(2)}, u32[]{:S(2)}) collective-permute-start(f32[152,256]{1,0:T(8,128)S(1)} %get-tuple-element.64.refs_3_), channel_id=1, source_target_pairs={{0,8},{1,9},{2,10},{3,11},{4,12},{5,13},{6,14},{7,15},{8,0},{9,1},... | collective-permute-start | bytes 466952 | tf_op jit(solution)/shard_map/ppermute | solution.py:434
  31.3 1.7 %collective-permute-start.23 = (f32[128,256]{1,0:T(8,128)S(1)}, f32[128,256]{1,0:T(8,128)S(1)}, u32[]{:S(2)}, u32[]{:S(2)}) collective-permute-start(f32[128,256]{1,0:T(8,128)S(1)} %shard_map.96.refs_1_), channel_id=1, source_target_pairs={{0,2},{1,3},{2,0},{3,1},{4,6},{5,7},{6,4},{7,5},{8,10},{9,11},{10,... | collective-permute-start | bytes 393224 | tf_op jit(solution)/shard_map/ppermute | solution.py:434
  33.0 1.3 %collective-permute-start.17 = (f32[96,256]{1,0:T(8,128)S(1)}, f32[96,256]{1,0:T(8,128)S(1)}, u32[]{:S(2)}, u32[]{:S(2)}) collective-permute-start(f32[96,256]{1,0:T(8,128)S(1)} %shard_map.94), channel_id=1, source_target_pairs={{0,16},{1,17},{2,18},{3,19},{4,20},{5,21},{6,22},{7,23},{8,24},{9,... | collective-permute-start | bytes 294920 | tf_op jit(solution)/shard_map/ppermute | solution.py:434
  35.4 3.7 %collective-permute-start.16 = (f32[136,256]{1,0:T(8,128)S(1)}, f32[136,256]{1,0:T(8,128)S(1)}, u32[]{:S(2)}, u32[]{:S(2)}) collective-permute-start(f32[136,256]{1,0:T(8,128)S(1)} %get-tuple-element.69.refs_3_), channel_id=1, source_target_pairs={{0,16},{1,17},{2,18},{3,19},{4,20},{5,21},{6,22},{7,23},{8,24},{9,... | collective-permute-start | bytes 417800 | tf_op jit(solution)/shard_map/ppermute | solution.py:434
  39.1 4.2 %collective-permute-done.17.refs_6_ = f32[96,256]{1,0:T(8,128)S(1)} collective-permute-done((f32[96,256]{1,0:T(8,128)S(1)}, f32[96,256]{1,0:T(8,128)S(1)}, u32[]{:S(2)}, u32[]{:S(2)}) %collective-permute-start.17) | collective-permute-done | bytes 98336 | tf_op jit(solution)/shard_map/ppermute | solution.py:434
  43.3 1.5 %collective-permute-start.24 = (f32[128,256]{1,0:T(8,128)S(1)}, f32[128,256]{1,0:T(8,128)S(1)}, u32[]{:S(2)}, u32[]{:S(2)}) collective-permute-start(f32[128,256]{1,0:T(8,128)S(1)} %shard_map.97.refs_1_), channel_id=1, source_target_pairs={{0,4},{1,5},{2,6},{3,7},{4,0},{5,1},{6,2},{7,3},{8,12},{9,13},{10,... | collective-permute-start | bytes 393224 | tf_op jit(solution)/shard_map/ppermute | solution.py:434
  46.4 1.6 %collective-permute-start.19 = (f32[160,256]{1,0:T(8,128)S(1)}, f32[160,256]{1,0:T(8,128)S(1)}, u32[]{:S(2)}, u32[]{:S(2)}) collective-permute-start(f32[160,256]{1,0:T(8,128)S(1)} %get-tuple-element.73), channel_id=1, source_target_pairs={{0,2},{1,3},{2,0},{3,1},{4,6},{5,7},{6,4},{7,5},{8,10},{9,11},{10,... | collective-permute-start | bytes 491528 | tf_op jit(solution)/shard_map/ppermute | solution.py:434
  48.6 1.3 %collective-permute-start.21 = (f32[160,256]{1,0:T(8,128)S(1)}, f32[160,256]{1,0:T(8,128)S(1)}, u32[]{:S(2)}, u32[]{:S(2)}) collective-permute-start(f32[160,256]{1,0:T(8,128)S(1)} %get-tuple-element.75), channel_id=1, source_target_pairs={{0,6},{1,7},{2,4},{3,5},{4,2},{5,3},{6,0},{7,1},{8,14},{9,15},{10,... | collective-permute-start | bytes 491528 | tf_op jit(solution)/shard_map/ppermute | solution.py:434
  50.0 5.0 %collective-permute-done.25.refs_2_ = f32[128,256]{1,0:T(8,128)S(1)} collective-permute-done((f32[128,256]{1,0:T(8,128)S(1)}, f32[128,256]{1,0:T(8,128)S(1)}, u32[]{:S(2)}, u32[]{:S(2)}) %collective-permute-start.25) | collective-permute-done | bytes 131104 | tf_op jit(solution)/shard_map/ppermute | solution.py:434
  55.0 1.1 %shard_map.100 = (f32[8,256]{1,0:T(8,128)S(1)}, f32[512,1024]{1,0:T(8,128)}, f32[512,256]{1,0:T(8,128)}) custom-call(s32[1]{0:T(128)} %bitcast.refs_0_, f32[2,256,256]{2,1,0:T(8,128)S(1)} %get-tuple-element.81.refs_1_, f32[2,256,256]{2,1,0:T(8,128)S(1)} %get-tuple-element.82.refs_2_, f32[256,256]{1,0:T(8,128)S(1)} %get-tuple-element.83.refs_3_.refs_11_, ...), custom_call_target="tpu_custom_call" | custom-call | flops 1 | bytes 1 | tf_op jit(solution)/shard_map/pallas_call | solution.py:461
  57.1 0.9 %shard_map.102.refs_12_ = f32[512,1024]{1,0:T(8,128)} custom-call(s32[1]{0:T(128)} %bitcast.refs_0_, f32[160,256]{1,0:T(8,128)S(1)} %get-tuple-element.72.refs_4_.refs_1_, f32[160,256]{1,0:T(8,128)S(1)} %collective-permute-done.19.refs_2_, f32[160,256]{1,0:T(8,128)S(1)} %collective-permute-done.20.refs_3_, ...), custom_call_target="tpu_custom_call", output_to_operand_aliasing={{}: (9, {})} | custom-call | flops 1 | bytes 1 | tf_op jit(solution)/shard_map/pallas_call | solution.py:461
  58.0 1.3 %collective-permute-done.26.refs_9_ = f32[4,192,256]{2,1,0:T(8,128)S(1)} collective-permute-done((f32[4,192,256]{2,1,0:T(8,128)S(1)}, f32[4,192,256]{2,1,0:T(8,128)S(1)}, u32[]{:S(2)}, u32[]{:S(2)}) %collective-permute-start.26) | collective-permute-done | bytes 786464 | tf_op jit(solution)/shard_map/ppermute | solution.py:434
  59.3 1.4 %shard_map.103 = (f32[512,1024]{1,0:T(8,128)}, f32[512,256]{1,0:T(8,128)}, f32[256,256]{1,0:T(8,128)}) custom-call(s32[1]{0:T(128)} %bitcast.refs_0_, f32[160,256]{1,0:T(8,128)S(1)} %get-tuple-element.72.refs_4_.refs_1_, f32[160,256]{1,0:T(8,128)S(1)} %collective-permute-done.19.refs_2_, ...), custom_call_target="tpu_custom_call", output_to_operand_aliasing={{0}: (12, {}), {1}: (13, {})} | custom-call | flops 1 | bytes 1 | tf_op jit(solution)/shard_map/pallas_call | solution.py:461
  (53 shorter events, 10.0 us)
Async XLA Ops:
  0.7 5.4 %collective-permute-start = (f32[256,256]{1,0:T(8,128)}, f32[256,256]{1,0:T(8,128)S(1)}, u32[]{:S(2)}, u32[]{:S(2)}) collective-permute-start(f32[256,256]{1,0:T(8,128)} %refs_1_.3), channel_id=1, source_target_pairs={{0,1},{1,0},{2,3},{3,2},{4,5},{5,4},{6,7},{7,6},{8,9},{9,8},{10,11... | collective-permute-start | bytes 786440 | tf_op jit(solution)/shard_map/ppermute | solution.py:434
  1.2 4.8 %collective-permute-start.1 = (f32[256,256]{1,0:T(8,128)}, f32[256,256]{1,0:T(8,128)S(1)}, u32[]{:S(2)}, u32[]{:S(2)}) collective-permute-start(f32[256,256]{1,0:T(8,128)} %refs_2_.3), channel_id=1, source_target_pairs={{0,1},{1,0},{2,3},{3,2},{4,5},{5,4},{6,7},{7,6},{8,9},{9,8},{10,11... | collective-permute-start | bytes 786440 | tf_op jit(solution)/shard_map/ppermute | solution.py:434
  5.4 5.5 %collective-permute-start.2 = (f32[192,256]{1,0:T(8,128)S(1)}, f32[192,256]{1,0:T(8,128)S(1)}, u32[]{:S(2)}, u32[]{:S(2)}) collective-permute-start(f32[192,256]{1,0:T(8,128)S(1)} %get-tuple-element.50), channel_id=1, source_target_pairs={{0,1},{1,0},{2,3},{3,2},{4,5},{5,4},{6,7},{7,6},{8,9},{9,8},{10,11... | collective-permute-start | bytes 589832 | tf_op jit(solution)/shard_map/ppermute | solution.py:434
  5.9 5.0 %collective-permute-start.3 = (f32[192,256]{1,0:T(8,128)S(1)}, f32[192,256]{1,0:T(8,128)S(1)}, u32[]{:S(2)}, u32[]{:S(2)}) collective-permute-start(f32[192,256]{1,0:T(8,128)S(1)} %get-tuple-element.51), channel_id=1, source_target_pairs={{0,1},{1,0},{2,3},{3,2},{4,5},{5,4},{6,7},{7,6},{8,9},{9,8},{10,11... | collective-permute-start | bytes 589832 | tf_op jit(solution)/shard_map/ppermute | solution.py:434
  6.4 9.1 %collective-permute-start.11 = (f32[136,256]{1,0:T(8,128)S(1)}, f32[136,256]{1,0:T(8,128)S(1)}, u32[]{:S(2)}, u32[]{:S(2)}) collective-permute-start(f32[136,256]{1,0:T(8,128)S(1)} %get-tuple-element.60.refs_1_), channel_id=1, source_target_pairs={{0,6},{1,7},{2,4},{3,5},{4,2},{5,3},{6,0},{7,1},{8,14},{9,15},{10,... | collective-permute-start | bytes 417800 | tf_op jit(solution)/shard_map/ppermute | solution.py:434
  10.3 6.9 %collective-permute-start.10 = (f32[136,256]{1,0:T(8,128)S(1)}, f32[136,256]{1,0:T(8,128)S(1)}, u32[]{:S(2)}, u32[]{:S(2)}) collective-permute-start(f32[136,256]{1,0:T(8,128)S(1)} %get-tuple-element.60.refs_1_), channel_id=1, source_target_pairs={{0,4},{1,5},{2,6},{3,7},{4,0},{5,1},{6,2},{7,3},{8,12},{9,13},{10,... | collective-permute-start | bytes 417800 | tf_op jit(solution)/shard_map/ppermute | solution.py:434
  10.8 6.7 %collective-permute-start.9 = (f32[136,256]{1,0:T(8,128)S(1)}, f32[136,256]{1,0:T(8,128)S(1)}, u32[]{:S(2)}, u32[]{:S(2)}) collective-permute-start(f32[136,256]{1,0:T(8,128)S(1)} %get-tuple-element.60.refs_1_), channel_id=1, source_target_pairs={{0,2},{1,3},{2,0},{3,1},{4,6},{5,7},{6,4},{7,5},{8,10},{9,11},{10,... | collective-permute-start | bytes 417800 | tf_op jit(solution)/shard_map/ppermute | solution.py:434
  17.6 5.2 %collective-permute-start.12 = (f32[3,136,256]{2,1,0:T(8,128)S(1)}, f32[3,136,256]{2,1,0:T(8,128)S(1)}, u32[]{:S(2)}, u32[]{:S(2)}) collective-permute-start(f32[3,136,256]{2,1,0:T(8,128)S(1)} %get-tuple-element.61.refs_2_.refs_4_), channel_id=1, source_target_pairs={{0,1},{1,0},{2,3},{3,2},{4,5},{5,4},{6,7},{7,6},{8,9},{9,8},{10,11... | collective-permute-start | bytes 1253384 | tf_op jit(solution)/shard_map/ppermute | solution.py:434
  17.6 8.3 %collective-permute-start.6 = (f32[128,256]{1,0:T(8,128)S(1)}, f32[128,256]{1,0:T(8,128)S(1)}, u32[]{:S(2)}, u32[]{:S(2)}) collective-permute-start(f32[128,256]{1,0:T(8,128)S(1)} %get-tuple-element.57), channel_id=1, source_target_pairs={{0,2},{1,3},{2,0},{3,1},{4,6},{5,7},{6,4},{7,5},{8,10},{9,11},{10,... | collective-permute-start | bytes 393224 | tf_op jit(solution)/shard_map/ppermute | solution.py:434
  19.2 8.4 %collective-permute-start.7 = (f32[128,256]{1,0:T(8,128)S(1)}, f32[128,256]{1,0:T(8,128)S(1)}, u32[]{:S(2)}, u32[]{:S(2)}) collective-permute-start(f32[128,256]{1,0:T(8,128)S(1)} %get-tuple-element.58), channel_id=1, source_target_pairs={{0,4},{1,5},{2,6},{3,7},{4,0},{5,1},{6,2},{7,3},{8,12},{9,13},{10,... | collective-permute-start | bytes 393224 | tf_op jit(solution)/shard_map/ppermute | solution.py:434
  19.8 7.8 %collective-permute-start.8 = (f32[128,256]{1,0:T(8,128)S(1)}, f32[128,256]{1,0:T(8,128)S(1)}, u32[]{:S(2)}, u32[]{:S(2)}) collective-permute-start(f32[128,256]{1,0:T(8,128)S(1)} %get-tuple-element.59), channel_id=1, source_target_pairs={{0,6},{1,7},{2,4},{3,5},{4,2},{5,3},{6,0},{7,1},{8,14},{9,15},{10,... | collective-permute-start | bytes 393224 | tf_op jit(solution)/shard_map/ppermute | solution.py:434
  21.2 9.9 %collective-permute-start.14 = (f32[136,256]{1,0:T(8,128)S(1)}, f32[136,256]{1,0:T(8,128)S(1)}, u32[]{:S(2)}, u32[]{:S(2)}) collective-permute-start(f32[136,256]{1,0:T(8,128)S(1)} %get-tuple-element.66.refs_1_), channel_id=1, source_target_pairs={{0,8},{1,9},{2,10},{3,11},{4,12},{5,13},{6,14},{7,15},{8,0},{9,1},... | collective-permute-start | bytes 417800 | tf_op jit(solution)/shard_map/ppermute | solution.py:434
  22.8 8.6 %collective-permute-start.22 = (f32[128,256]{1,0:T(8,128)S(1)}, f32[128,256]{1,0:T(8,128)S(1)}, u32[]{:S(2)}, u32[]{:S(2)}) collective-permute-start(f32[128,256]{1,0:T(8,128)S(1)} %get-tuple-element.80.refs_1_), channel_id=1, source_target_pairs={{0,16},{1,17},{2,18},{3,19},{4,20},{5,21},{6,22},{7,23},{8,24},{9,... | collective-permute-start | bytes 393224 | tf_op jit(solution)/shard_map/ppermute | solution.py:434
  29.4 5.3 %collective-permute-start.13 = (f32[152,256]{1,0:T(8,128)S(1)}, f32[152,256]{1,0:T(8,128)S(1)}, u32[]{:S(2)}, u32[]{:S(2)}) collective-permute-start(f32[152,256]{1,0:T(8,128)S(1)} %get-tuple-element.64.refs_3_), channel_id=1, source_target_pairs={{0,8},{1,9},{2,10},{3,11},{4,12},{5,13},{6,14},{7,15},{8,0},{9,1},... | collective-permute-start | bytes 466952 | tf_op jit(solution)/shard_map/ppermute | solution.py:434
  31.1 3.3 %collective-permute-start.15 = (f32[136,256]{1,0:T(8,128)S(1)}, f32[136,256]{1,0:T(8,128)S(1)}, u32[]{:S(2)}, u32[]{:S(2)}) collective-permute-start(f32[136,256]{1,0:T(8,128)S(1)} %collective-permute-done.14.refs_6_.refs_2_), channel_id=1, source_target_pairs={{0,1},{1,0},{2,3},{3,2},{4,5},{5,4},{6,7},{7,6},{8,9},{9,8},{10,11... | collective-permute-start | bytes 417800 | tf_op jit(solution)/shard_map/ppermute | solution.py:434
  31.3 12.0 %collective-permute-start.23 = (f32[128,256]{1,0:T(8,128)S(1)}, f32[128,256]{1,0:T(8,128)S(1)}, u32[]{:S(2)}, u32[]{:S(2)}) collective-permute-start(f32[128,256]{1,0:T(8,128)S(1)} %shard_map.96.refs_1_), channel_id=1, source_target_pairs={{0,2},{1,3},{2,0},{3,1},{4,6},{5,7},{6,4},{7,5},{8,10},{9,11},{10,... | collective-permute-start | bytes 393224 | tf_op jit(solution)/shard_map/ppermute | solution.py:434
  33.0 10.3 %collective-permute-start.17 = (f32[96,256]{1,0:T(8,128)S(1)}, f32[96,256]{1,0:T(8,128)S(1)}, u32[]{:S(2)}, u32[]{:S(2)}) collective-permute-start(f32[96,256]{1,0:T(8,128)S(1)} %shard_map.94), channel_id=1, source_target_pairs={{0,16},{1,17},{2,18},{3,19},{4,20},{5,21},{6,22},{7,23},{8,24},{9,... | collective-permute-start | bytes 294920 | tf_op jit(solution)/shard_map/ppermute | solution.py:434
  35.4 10.2 %collective-permute-start.16 = (f32[136,256]{1,0:T(8,128)S(1)}, f32[136,256]{1,0:T(8,128)S(1)}, u32[]{:S(2)}, u32[]{:S(2)}) collective-permute-start(f32[136,256]{1,0:T(8,128)S(1)} %get-tuple-element.69.refs_3_), channel_id=1, source_target_pairs={{0,16},{1,17},{2,18},{3,19},{4,20},{5,21},{6,22},{7,23},{8,24},{9,... | collective-permute-start | bytes 417800 | tf_op jit(solution)/shard_map/ppermute | solution.py:434
  43.3 6.6 %collective-permute-start.24 = (f32[128,256]{1,0:T(8,128)S(1)}, f32[128,256]{1,0:T(8,128)S(1)}, u32[]{:S(2)}, u32[]{:S(2)}) collective-permute-start(f32[128,256]{1,0:T(8,128)S(1)} %shard_map.97.refs_1_), channel_id=1, source_target_pairs={{0,4},{1,5},{2,6},{3,7},{4,0},{5,1},{6,2},{7,3},{8,12},{9,13},{10,... | collective-permute-start | bytes 393224 | tf_op jit(solution)/shard_map/ppermute | solution.py:434
  46.4 9.7 %collective-permute-start.19 = (f32[160,256]{1,0:T(8,128)S(1)}, f32[160,256]{1,0:T(8,128)S(1)}, u32[]{:S(2)}, u32[]{:S(2)}) collective-permute-start(f32[160,256]{1,0:T(8,128)S(1)} %get-tuple-element.73), channel_id=1, source_target_pairs={{0,2},{1,3},{2,0},{3,1},{4,6},{5,7},{6,4},{7,5},{8,10},{9,11},{10,... | collective-permute-start | bytes 491528 | tf_op jit(solution)/shard_map/ppermute | solution.py:434
  47.9 9.0 %collective-permute-start.20 = (f32[160,256]{1,0:T(8,128)S(1)}, f32[160,256]{1,0:T(8,128)S(1)}, u32[]{:S(2)}, u32[]{:S(2)}) collective-permute-start(f32[160,256]{1,0:T(8,128)S(1)} %get-tuple-element.74), channel_id=1, source_target_pairs={{0,4},{1,5},{2,6},{3,7},{4,0},{5,1},{6,2},{7,3},{8,12},{9,13},{10,... | collective-permute-start | bytes 491528 | tf_op jit(solution)/shard_map/ppermute | solution.py:434
  48.6 8.3 %collective-permute-start.21 = (f32[160,256]{1,0:T(8,128)S(1)}, f32[160,256]{1,0:T(8,128)S(1)}, u32[]{:S(2)}, u32[]{:S(2)}) collective-permute-start(f32[160,256]{1,0:T(8,128)S(1)} %get-tuple-element.75), channel_id=1, source_target_pairs={{0,6},{1,7},{2,4},{3,5},{4,2},{5,3},{6,0},{7,1},{8,14},{9,15},{10,... | collective-permute-start | bytes 491528 | tf_op jit(solution)/shard_map/ppermute | solution.py:434
  50.0 5.0 %collective-permute-start.25 = (f32[128,256]{1,0:T(8,128)S(1)}, f32[128,256]{1,0:T(8,128)S(1)}, u32[]{:S(2)}, u32[]{:S(2)}) collective-permute-start(f32[128,256]{1,0:T(8,128)S(1)} %shard_map.98.refs_1_), channel_id=1, source_target_pairs={{0,8},{1,9},{2,10},{3,11},{4,12},{5,13},{6,14},{7,15},{8,0},{9,1},... | collective-permute-start | bytes 393224 | tf_op jit(solution)/shard_map/ppermute | solution.py:434
  57.0 2.4 %collective-permute-start.26 = (f32[4,192,256]{2,1,0:T(8,128)S(1)}, f32[4,192,256]{2,1,0:T(8,128)S(1)}, u32[]{:S(2)}, u32[]{:S(2)}) collective-permute-start(f32[4,192,256]{2,1,0:T(8,128)S(1)} %shard_map.101.refs_10_.refs_14_), channel_id=1, source_target_pairs={{0,1},{1,0},{2,3},{3,2},{4,5},{5,4},{6,7},{7,6},{8,9},{9,8},{10,11... | collective-permute-start | bytes 2359304 | tf_op jit(solution)/shard_map/ppermute | solution.py:434
  (5 other events, 15.2 us)

commit v3 on v2

--- a/solution.py
+++ b/solution.py
@@ -243,6 +243,8 @@
             target = slice(b * quarter, (b + 1) * quarter)
             sends[r][target] = low_ref[source]
             dones[r][target] = high_ref[source]
+        if sends[r].shape[0] > count * quarter:
+            sends[r][count * quarter :] = jnp.zeros_like(sends[r][count * quarter :])
 
 
 def gather_kernel(me_ref, *refs):
@@ -258,7 +260,7 @@
 
 
 def sort_kernel(me_ref, *refs):
-    parts = [ref[...] for ref in refs[:4]]
+    parts = [ref[: refs[4].shape[1]] for ref in refs[:4]]
     for j in range(4):
         refs[4][j] = by_place(me_ref[0], parts, j)
 
@@ -270,7 +272,8 @@
 def fill(send_ref, value):
     cols = value.shape[0]
     send_ref[:cols] = value
-    send_ref[cols:] = jnp.zeros_like(send_ref[cols:])
+    if send_ref.shape[0] > cols:
+        send_ref[cols:] = jnp.zeros_like(send_ref[cols:])
 
 
 def prepare_kernel(me_ref, packed_ref, stack_ref, stack_there_ref, ready_ref, held_ref):
@@ -347,7 +350,7 @@
     quarter = rows - cols
     for r in range(4):
         out_ref[r, :cols] = jnp.where(odd, backs[r][:cols], dones[r][...])
-        out_ref[r, cols:rows] = backs[r][cols:]
+        out_ref[r, cols:rows] = backs[r][cols:rows]
         out_ref[r, rows:] = gram_ref[r * quarter : (r + 1) * quarter]
 
 
@@ -405,7 +408,7 @@
         return pl.ds(pl.multiple_of(part * half + (place(me) ^ r) * quarter, quarter), quarter)
 
     for r in range(4):
-        panel_ref[target(core, r)] = backs[r][cols:]
+        panel_ref[target(core, r)] = backs[r][cols : cols + quarter]
         panel_ref[target(1 - core, r)] = there_ref[r, cols : cols + quarter]
         rows = pl.ds(pl.multiple_of((1 - core) * half + r * quarter, quarter), quarter)
         sum_ref[rows] = there_ref[r, cols + quarter :]
@@ -508,7 +511,7 @@
     cols = count * quarter
     outs = call(
         core_kernel, (own_a, own_b, *there_a, *theres, chip_high),
-        [shape(cols, width)] * 8 + [shape(half, width)],
+        [shape(cols, width)] * 3 + [shape(cols + 8, width)] + [shape(cols, width)] * 4 + [shape(half, width)],
         [vmem(count * half, width), vmem(count * half, width)],
     )
     sends, dones, gram_half = outs[:4], outs[4:8], outs[8]
@@ -523,7 +526,7 @@
     stack_there = exchange(stack, 1)
     parts = [exchange(held_part, 8)]
     for level in range(4, levels):
-        short = 3 * quarter if level == levels - 1 else half + EXTRA
+        short = half // 2 + EXTRA if level == levels - 1 else half + EXTRA
         (held_part,) = call(
             functools.partial(hold_kernel, level=level - 1), (held_part, parts[-1]), (shape(short, width),),
             chained=False,
@@ -546,12 +549,12 @@
         if level == levels - 1:
             sends = call(
                 functools.partial(last_kernel, level=level), (*operands, plane_done),
-                [shape(cols + quarter, width)] * 4, [vmem(4, cols, width)],
+                [shape(cols + quarter, width)] * 3 + [shape(cols + quarter + 8, width)], [vmem(4, cols, width)],
             )
         else:
             head, result, held, send = call(
                 functools.partial(line_kernel, level=level), operands,
-                [shape(cols, width), shape(cols, width), shape(*held.shape), shape(cols + 8, width)],
+                [shape(cols, width), shape(cols, width), shape(*held.shape), shape(cols + 0, width)],
             )
 
     backs = around(sends)

time: 60.9 us -> 60.5 us (level)
  waiting for transfers between devices: 17.4 us -> 16.4 us
    ppermute x27, waiting for transfers between devices: 17.4 us -> 16.4 us  [exchange(): return lax.ppermute(value, 'rows', [(i, i ^ shift) for i in range(devices)])]
where the time goes in v3:
time: 60.5 us; the launch traced here: 60.3 us
  starting transfers between devices  28.2 us (47%)
  waiting for transfers between devices  16.4 us (27%)
  Pallas kernels  14.9 us (25%)
  between operations  0.82 us (1%)
    ppermute x27, starting transfers between devices, exchange(): return lax.ppermute(value, 'rows', [(i, i ^ shift) for i in range(devices)])  28.2 us
    ppermute x27, waiting for transfers between devices, exchange(): return lax.ppermute(value, 'rows', [(i, i ^ shift) for i in range(devices)])  16.4 us
    pallas_call x19, Pallas kernels, call(): pl.pallas_call(kernel_on, out_shape=tuple(outs), in_specs=[SCALAR] + [AWA...  14.9 us
  transfers between devices with their start and end apart: 27, of which 12 were waited for; matrix products, arithmetic and copies ran while one was open for 0% of the time, Pallas kernels for 22%

profile of v3, /device:TPU:0, one launch (start us, length us, event | category | flops | bytes accessed | tf_op | source)
XLA Modules:
  0.0 60.3 jit_solution(18043737016034743596)
XLA Ops:
  1.2 4.2 %shard_map.85 = (f32[384,256]{1,0:T(8,128)S(1)}, f32[192,256]{1,0:T(8,128)S(1)}, f32[192,256]{1,0:T(8,128)S(1)}, f32[2,256,256]{2,1,0:T(8,128)S(1)}, f32[2,512,2...) custom-call(s32[1]{0:T(128)} %bitcast.refs_0_, ...), custom_call_target="tpu_custom_call" | custom-call | flops 1 | bytes 1 | tf_op jit(solution)/shard_map/pallas_call | solution.py:464
  6.4 3.9 %collective-permute-start.11 = (f32[136,256]{1,0:T(8,128)S(1)}, f32[136,256]{1,0:T(8,128)S(1)}, u32[]{:S(2)}, u32[]{:S(2)}) collective-permute-start(f32[136,256]{1,0:T(8,128)S(1)} %get-tuple-element.60.refs_1_), channel_id=1, source_target_pairs={{0,6},{1,7},{2,4},{3,5},{4,2},{5,3},{6,0},{7,1},{8,14},{9,15},{10,... | collective-permute-start | bytes 417800 | tf_op jit(solution)/shard_map/ppermute | solution.py:437
  10.9 1.6 %shard_map.87 = (f32[256,256]{1,0:T(8,128)S(1)}, f32[2,256,256]{2,1,0:T(8,128)S(1)}, f32[128,256]{1,0:T(8,128)S(1)}, f32[128,256]{1,0:T(8,128)S(1)}) custom-call(s32[1]{0:T(128)} %bitcast.refs_0_, f32[2,512,256]{2,1,0:T(8,128)S(1)} %get-tuple-element.46.refs_1_, bf16[2,256,512]{2,1,0:T(8,128)(2,1)S(1)} %get-tuple-element.47.refs_2_, ...), custom_call_target="tpu_custom_call" | custom-call | flops 1 | bytes 1 | tf_op jit(solution)/shard_map/pallas_call | solution.py:464
  14.1 1.3 %shard_map.88 = (f32[128,256]{1,0:T(8,128)S(1)}, f32[128,256]{1,0:T(8,128)S(1)}, f32[128,256]{1,0:T(8,128)S(1)}, f32[136,256]{1,0:T(8,128)S(1)}, f32[128,256]{1,...) custom-call(s32[1]{0:T(128)} %bitcast.refs_0_, ...), custom_call_target="tpu_custom_call" | custom-call | flops 1 | bytes 1 | tf_op jit(solution)/shard_map/pallas_call | solution.py:464
  15.5 1.7 %collective-permute-done.10.refs_3_ = f32[136,256]{1,0:T(8,128)S(1)} collective-permute-done((f32[136,256]{1,0:T(8,128)S(1)}, f32[136,256]{1,0:T(8,128)S(1)}, u32[]{:S(2)}, u32[]{:S(2)}) %collective-permute-start.10) | collective-permute-done | bytes 139296 | tf_op jit(solution)/shard_map/ppermute | solution.py:437
  17.6 1.6 %collective-permute-start.8 = (f32[136,256]{1,0:T(8,128)S(1)}, f32[136,256]{1,0:T(8,128)S(1)}, u32[]{:S(2)}, u32[]{:S(2)}) collective-permute-start(f32[136,256]{1,0:T(8,128)S(1)} %get-tuple-element.59), channel_id=1, source_target_pairs={{0,6},{1,7},{2,4},{3,5},{4,2},{5,3},{6,0},{7,1},{8,14},{9,15},{10,... | collective-permute-start | bytes 417800 | tf_op jit(solution)/shard_map/ppermute | solution.py:437
  19.2 1.4 %collective-permute-start.6 = (f32[128,256]{1,0:T(8,128)S(1)}, f32[128,256]{1,0:T(8,128)S(1)}, u32[]{:S(2)}, u32[]{:S(2)}) collective-permute-start(f32[128,256]{1,0:T(8,128)S(1)} %get-tuple-element.57), channel_id=1, source_target_pairs={{0,2},{1,3},{2,0},{3,1},{4,6},{5,7},{6,4},{7,5},{8,10},{9,11},{10,... | collective-permute-start | bytes 393224 | tf_op jit(solution)/shard_map/ppermute | solution.py:437
  21.2 1.6 %collective-permute-start.14 = (f32[136,256]{1,0:T(8,128)S(1)}, f32[136,256]{1,0:T(8,128)S(1)}, u32[]{:S(2)}, u32[]{:S(2)}) collective-permute-start(f32[136,256]{1,0:T(8,128)S(1)} %get-tuple-element.66.refs_1_), channel_id=1, source_target_pairs={{0,8},{1,9},{2,10},{3,11},{4,12},{5,13},{6,14},{7,15},{8,0},{9,1},... | collective-permute-start | bytes 417800 | tf_op jit(solution)/shard_map/ppermute | solution.py:437
  22.8 2.6 %collective-permute-start.22 = (f32[128,256]{1,0:T(8,128)S(1)}, f32[128,256]{1,0:T(8,128)S(1)}, u32[]{:S(2)}, u32[]{:S(2)}) collective-permute-start(f32[128,256]{1,0:T(8,128)S(1)} %get-tuple-element.80.refs_1_), channel_id=1, source_target_pairs={{0,16},{1,17},{2,18},{3,19},{4,20},{5,21},{6,22},{7,23},{8,24},{9,... | collective-permute-start | bytes 393224 | tf_op jit(solution)/shard_map/ppermute | solution.py:437
  25.9 1.5 %collective-permute-done.6.refs_2_ = f32[128,256]{1,0:T(8,128)S(1)} collective-permute-done((f32[128,256]{1,0:T(8,128)S(1)}, f32[128,256]{1,0:T(8,128)S(1)}, u32[]{:S(2)}, u32[]{:S(2)}) %collective-permute-start.6) | collective-permute-done | bytes 131104 | tf_op jit(solution)/shard_map/ppermute | solution.py:437
  27.5 1.7 %shard_map.92 = (f32[128,256]{1,0:T(8,128)S(1)}, f32[152,256]{1,0:T(8,128)S(1)}, f32[4,128,256]{2,1,0:T(8,128)S(1)}) custom-call(s32[1]{0:T(128)} %bitcast.refs_0_, f32[4,128,256]{2,1,0:T(8,128)S(1)} %shard_map.91.refs_1_.refs_3_, bf16[4,4,256,256]{3,2,1,0:T(8,128)(2,1)S(1)} %get-tuple-element.62.refs_5_.refs_2_, f32[4,128,256]{2,1,0:T(8,128)S(1)} %shard_map.91.refs_1_.refs_3_), custom_call_target="tpu_custom_call" | custom-call | flops 1 | bytes 1 | tf_op jit(solution)/shard_map/pallas_call | solution.py:464
  29.3 1.6 %collective-permute-start.13 = (f32[152,256]{1,0:T(8,128)S(1)}, f32[152,256]{1,0:T(8,128)S(1)}, u32[]{:S(2)}, u32[]{:S(2)}) collective-permute-start(f32[152,256]{1,0:T(8,128)S(1)} %get-tuple-element.64.refs_3_), channel_id=1, source_target_pairs={{0,8},{1,9},{2,10},{3,11},{4,12},{5,13},{6,14},{7,15},{8,0},{9,1},... | collective-permute-start | bytes 466952 | tf_op jit(solution)/shard_map/ppermute | solution.py:437
  31.3 1.6 %collective-permute-start.23 = (f32[128,256]{1,0:T(8,128)S(1)}, f32[128,256]{1,0:T(8,128)S(1)}, u32[]{:S(2)}, u32[]{:S(2)}) collective-permute-start(f32[128,256]{1,0:T(8,128)S(1)} %shard_map.96.refs_1_), channel_id=1, source_target_pairs={{0,2},{1,3},{2,0},{3,1},{4,6},{5,7},{6,4},{7,5},{8,10},{9,11},{10,... | collective-permute-start | bytes 393224 | tf_op jit(solution)/shard_map/ppermute | solution.py:437
  32.9 2.3 %collective-permute-start.17 = (f32[72,256]{1,0:T(8,128)S(1)}, f32[72,256]{1,0:T(8,128)S(1)}, u32[]{:S(2)}, u32[]{:S(2)}) collective-permute-start(f32[72,256]{1,0:T(8,128)S(1)} %shard_map.94), channel_id=1, source_target_pairs={{0,16},{1,17},{2,18},{3,19},{4,20},{5,21},{6,22},{7,23},{8,24},{9,... | collective-permute-start | bytes 221192 | tf_op jit(solution)/shard_map/ppermute | solution.py:437
  35.9 3.4 %collective-permute-start.16 = (f32[128,256]{1,0:T(8,128)S(1)}, f32[128,256]{1,0:T(8,128)S(1)}, u32[]{:S(2)}, u32[]{:S(2)}) collective-permute-start(f32[128,256]{1,0:T(8,128)S(1)} %get-tuple-element.69.refs_3_), channel_id=1, source_target_pairs={{0,16},{1,17},{2,18},{3,19},{4,20},{5,21},{6,22},{7,23},{8,24},{9,... | collective-permute-start | bytes 393224 | tf_op jit(solution)/shard_map/ppermute | solution.py:437
  39.4 1.5 %collective-permute-start.24 = (f32[128,256]{1,0:T(8,128)S(1)}, f32[128,256]{1,0:T(8,128)S(1)}, u32[]{:S(2)}, u32[]{:S(2)}) collective-permute-start(f32[128,256]{1,0:T(8,128)S(1)} %shard_map.97.refs_1_), channel_id=1, source_target_pairs={{0,4},{1,5},{2,6},{3,7},{4,0},{5,1},{6,2},{7,3},{8,12},{9,13},{10,... | collective-permute-start | bytes 393224 | tf_op jit(solution)/shard_map/ppermute | solution.py:437
  40.9 1.3 %collective-permute-done.18.refs_7_ = f32[72,256]{1,0:T(8,128)S(1)} collective-permute-done((f32[72,256]{1,0:T(8,128)S(1)}, f32[72,256]{1,0:T(8,128)S(1)}, u32[]{:S(2)}, u32[]{:S(2)}) %collective-permute-start.18) | collective-permute-done | bytes 73760 | tf_op jit(solution)/shard_map/ppermute | solution.py:437
  42.2 2.9 %collective-permute-done.16.refs_4_ = f32[128,256]{1,0:T(8,128)S(1)} collective-permute-done((f32[128,256]{1,0:T(8,128)S(1)}, f32[128,256]{1,0:T(8,128)S(1)}, u32[]{:S(2)}, u32[]{:S(2)}) %collective-permute-start.16) | collective-permute-done | bytes 131104 | tf_op jit(solution)/shard_map/ppermute | solution.py:437
  45.8 1.4 %collective-permute-start.21 = (f32[168,256]{1,0:T(8,128)S(1)}, f32[168,256]{1,0:T(8,128)S(1)}, u32[]{:S(2)}, u32[]{:S(2)}) collective-permute-start(f32[168,256]{1,0:T(8,128)S(1)} %get-tuple-element.75), channel_id=1, source_target_pairs={{0,6},{1,7},{2,4},{3,5},{4,2},{5,3},{6,0},{7,1},{8,14},{9,15},{10,... | collective-permute-start | bytes 516104 | tf_op jit(solution)/shard_map/ppermute | solution.py:437
  48.2 1.2 %collective-permute-start.20 = (f32[160,256]{1,0:T(8,128)S(1)}, f32[160,256]{1,0:T(8,128)S(1)}, u32[]{:S(2)}, u32[]{:S(2)}) collective-permute-start(f32[160,256]{1,0:T(8,128)S(1)} %get-tuple-element.74), channel_id=1, source_target_pairs={{0,4},{1,5},{2,6},{3,7},{4,0},{5,1},{6,2},{7,3},{8,12},{9,13},{10,... | collective-permute-start | bytes 491528 | tf_op jit(solution)/shard_map/ppermute | solution.py:437
  49.5 5.0 %collective-permute-done.25.refs_2_ = f32[128,256]{1,0:T(8,128)S(1)} collective-permute-done((f32[128,256]{1,0:T(8,128)S(1)}, f32[128,256]{1,0:T(8,128)S(1)}, u32[]{:S(2)}, u32[]{:S(2)}) %collective-permute-start.25) | collective-permute-done | bytes 131104 | tf_op jit(solution)/shard_map/ppermute | solution.py:437
  54.5 1.1 %shard_map.100 = (f32[8,256]{1,0:T(8,128)S(1)}, f32[512,1024]{1,0:T(8,128)}, f32[512,256]{1,0:T(8,128)}) custom-call(s32[1]{0:T(128)} %bitcast.refs_0_, f32[2,256,256]{2,1,0:T(8,128)S(1)} %get-tuple-element.81.refs_1_, f32[2,256,256]{2,1,0:T(8,128)S(1)} %get-tuple-element.82.refs_2_, f32[256,256]{1,0:T(8,128)S(1)} %get-tuple-element.83.refs_3_.refs_11_, ...), custom_call_target="tpu_custom_call" | custom-call | flops 1 | bytes 1 | tf_op jit(solution)/shard_map/pallas_call | solution.py:464
  57.5 1.3 %collective-permute-done.26.refs_9_ = f32[4,192,256]{2,1,0:T(8,128)S(1)} collective-permute-done((f32[4,192,256]{2,1,0:T(8,128)S(1)}, f32[4,192,256]{2,1,0:T(8,128)S(1)}, u32[]{:S(2)}, u32[]{:S(2)}) %collective-permute-start.26) | collective-permute-done | bytes 786464 | tf_op jit(solution)/shard_map/ppermute | solution.py:437
  58.9 1.4 %shard_map.103 = (f32[512,1024]{1,0:T(8,128)}, f32[512,256]{1,0:T(8,128)}, f32[256,256]{1,0:T(8,128)}) custom-call(s32[1]{0:T(128)} %bitcast.refs_0_, f32[160,256]{1,0:T(8,128)S(1)} %get-tuple-element.72.refs_4_.refs_1_, f32[160,256]{1,0:T(8,128)S(1)} %collective-permute-done.19.refs_2_, ...), custom_call_target="tpu_custom_call", output_to_operand_aliasing={{0}: (12, {}), {1}: (13, {})} | custom-call | flops 1 | bytes 1 | tf_op jit(solution)/shard_map/pallas_call | solution.py:464
  (53 shorter events, 10.3 us)
Async XLA Ops:
  0.7 5.4 %collective-permute-start = (f32[256,256]{1,0:T(8,128)}, f32[256,256]{1,0:T(8,128)S(1)}, u32[]{:S(2)}, u32[]{:S(2)}) collective-permute-start(f32[256,256]{1,0:T(8,128)} %refs_1_.3), channel_id=1, source_target_pairs={{0,1},{1,0},{2,3},{3,2},{4,5},{5,4},{6,7},{7,6},{8,9},{9,8},{10,11... | collective-permute-start | bytes 786440 | tf_op jit(solution)/shard_map/ppermute | solution.py:437
  1.2 4.8 %collective-permute-start.1 = (f32[256,256]{1,0:T(8,128)}, f32[256,256]{1,0:T(8,128)S(1)}, u32[]{:S(2)}, u32[]{:S(2)}) collective-permute-start(f32[256,256]{1,0:T(8,128)} %refs_2_.3), channel_id=1, source_target_pairs={{0,1},{1,0},{2,3},{3,2},{4,5},{5,4},{6,7},{7,6},{8,9},{9,8},{10,11... | collective-permute-start | bytes 786440 | tf_op jit(solution)/shard_map/ppermute | solution.py:437
  5.4 5.5 %collective-permute-start.2 = (f32[192,256]{1,0:T(8,128)S(1)}, f32[192,256]{1,0:T(8,128)S(1)}, u32[]{:S(2)}, u32[]{:S(2)}) collective-permute-start(f32[192,256]{1,0:T(8,128)S(1)} %get-tuple-element.50), channel_id=1, source_target_pairs={{0,1},{1,0},{2,3},{3,2},{4,5},{5,4},{6,7},{7,6},{8,9},{9,8},{10,11... | collective-permute-start | bytes 589832 | tf_op jit(solution)/shard_map/ppermute | solution.py:437
  5.9 5.0 %collective-permute-start.3 = (f32[192,256]{1,0:T(8,128)S(1)}, f32[192,256]{1,0:T(8,128)S(1)}, u32[]{:S(2)}, u32[]{:S(2)}) collective-permute-start(f32[192,256]{1,0:T(8,128)S(1)} %get-tuple-element.51), channel_id=1, source_target_pairs={{0,1},{1,0},{2,3},{3,2},{4,5},{5,4},{6,7},{7,6},{8,9},{9,8},{10,11... | collective-permute-start | bytes 589832 | tf_op jit(solution)/shard_map/ppermute | solution.py:437
  6.4 9.1 %collective-permute-start.11 = (f32[136,256]{1,0:T(8,128)S(1)}, f32[136,256]{1,0:T(8,128)S(1)}, u32[]{:S(2)}, u32[]{:S(2)}) collective-permute-start(f32[136,256]{1,0:T(8,128)S(1)} %get-tuple-element.60.refs_1_), channel_id=1, source_target_pairs={{0,6},{1,7},{2,4},{3,5},{4,2},{5,3},{6,0},{7,1},{8,14},{9,15},{10,... | collective-permute-start | bytes 417800 | tf_op jit(solution)/shard_map/ppermute | solution.py:437
  10.3 6.9 %collective-permute-start.10 = (f32[136,256]{1,0:T(8,128)S(1)}, f32[136,256]{1,0:T(8,128)S(1)}, u32[]{:S(2)}, u32[]{:S(2)}) collective-permute-start(f32[136,256]{1,0:T(8,128)S(1)} %get-tuple-element.60.refs_1_), channel_id=1, source_target_pairs={{0,4},{1,5},{2,6},{3,7},{4,0},{5,1},{6,2},{7,3},{8,12},{9,13},{10,... | collective-permute-start | bytes 417800 | tf_op jit(solution)/shard_map/ppermute | solution.py:437
  10.8 6.7 %collective-permute-start.9 = (f32[136,256]{1,0:T(8,128)S(1)}, f32[136,256]{1,0:T(8,128)S(1)}, u32[]{:S(2)}, u32[]{:S(2)}) collective-permute-start(f32[136,256]{1,0:T(8,128)S(1)} %get-tuple-element.60.refs_1_), channel_id=1, source_target_pairs={{0,2},{1,3},{2,0},{3,1},{4,6},{5,7},{6,4},{7,5},{8,10},{9,11},{10,... | collective-permute-start | bytes 417800 | tf_op jit(solution)/shard_map/ppermute | solution.py:437
  17.6 5.2 %collective-permute-start.12 = (f32[3,136,256]{2,1,0:T(8,128)S(1)}, f32[3,136,256]{2,1,0:T(8,128)S(1)}, u32[]{:S(2)}, u32[]{:S(2)}) collective-permute-start(f32[3,136,256]{2,1,0:T(8,128)S(1)} %get-tuple-element.61.refs_2_.refs_4_), channel_id=1, source_target_pairs={{0,1},{1,0},{2,3},{3,2},{4,5},{5,4},{6,7},{7,6},{8,9},{9,8},{10,11... | collective-permute-start | bytes 1253384 | tf_op jit(solution)/shard_map/ppermute | solution.py:437
  17.6 9.8 %collective-permute-start.8 = (f32[136,256]{1,0:T(8,128)S(1)}, f32[136,256]{1,0:T(8,128)S(1)}, u32[]{:S(2)}, u32[]{:S(2)}) collective-permute-start(f32[136,256]{1,0:T(8,128)S(1)} %get-tuple-element.59), channel_id=1, source_target_pairs={{0,6},{1,7},{2,4},{3,5},{4,2},{5,3},{6,0},{7,1},{8,14},{9,15},{10,... | collective-permute-start | bytes 417800 | tf_op jit(solution)/shard_map/ppermute | solution.py:437
  19.2 8.2 %collective-permute-start.6 = (f32[128,256]{1,0:T(8,128)S(1)}, f32[128,256]{1,0:T(8,128)S(1)}, u32[]{:S(2)}, u32[]{:S(2)}) collective-permute-start(f32[128,256]{1,0:T(8,128)S(1)} %get-tuple-element.57), channel_id=1, source_target_pairs={{0,2},{1,3},{2,0},{3,1},{4,6},{5,7},{6,4},{7,5},{8,10},{9,11},{10,... | collective-permute-start | bytes 393224 | tf_op jit(solution)/shard_map/ppermute | solution.py:437
  20.6 6.9 %collective-permute-start.7 = (f32[128,256]{1,0:T(8,128)S(1)}, f32[128,256]{1,0:T(8,128)S(1)}, u32[]{:S(2)}, u32[]{:S(2)}) collective-permute-start(f32[128,256]{1,0:T(8,128)S(1)} %get-tuple-element.58), channel_id=1, source_target_pairs={{0,4},{1,5},{2,6},{3,7},{4,0},{5,1},{6,2},{7,3},{8,12},{9,13},{10,... | collective-permute-start | bytes 393224 | tf_op jit(solution)/shard_map/ppermute | solution.py:437
  21.2 9.7 %collective-permute-start.14 = (f32[136,256]{1,0:T(8,128)S(1)}, f32[136,256]{1,0:T(8,128)S(1)}, u32[]{:S(2)}, u32[]{:S(2)}) collective-permute-start(f32[136,256]{1,0:T(8,128)S(1)} %get-tuple-element.66.refs_1_), channel_id=1, source_target_pairs={{0,8},{1,9},{2,10},{3,11},{4,12},{5,13},{6,14},{7,15},{8,0},{9,1},... | collective-permute-start | bytes 417800 | tf_op jit(solution)/shard_map/ppermute | solution.py:437
  22.8 8.6 %collective-permute-start.22 = (f32[128,256]{1,0:T(8,128)S(1)}, f32[128,256]{1,0:T(8,128)S(1)}, u32[]{:S(2)}, u32[]{:S(2)}) collective-permute-start(f32[128,256]{1,0:T(8,128)S(1)} %get-tuple-element.80.refs_1_), channel_id=1, source_target_pairs={{0,16},{1,17},{2,18},{3,19},{4,20},{5,21},{6,22},{7,23},{8,24},{9,... | collective-permute-start | bytes 393224 | tf_op jit(solution)/shard_map/ppermute | solution.py:437
  29.3 6.0 %collective-permute-start.13 = (f32[152,256]{1,0:T(8,128)S(1)}, f32[152,256]{1,0:T(8,128)S(1)}, u32[]{:S(2)}, u32[]{:S(2)}) collective-permute-start(f32[152,256]{1,0:T(8,128)S(1)} %get-tuple-element.64.refs_3_), channel_id=1, source_target_pairs={{0,8},{1,9},{2,10},{3,11},{4,12},{5,13},{6,14},{7,15},{8,0},{9,1},... | collective-permute-start | bytes 466952 | tf_op jit(solution)/shard_map/ppermute | solution.py:437
  30.9 4.3 %collective-permute-start.15 = (f32[136,256]{1,0:T(8,128)S(1)}, f32[136,256]{1,0:T(8,128)S(1)}, u32[]{:S(2)}, u32[]{:S(2)}) collective-permute-start(f32[136,256]{1,0:T(8,128)S(1)} %collective-permute-done.14.refs_6_.refs_2_), channel_id=1, source_target_pairs={{0,1},{1,0},{2,3},{3,2},{4,5},{5,4},{6,7},{7,6},{8,9},{9,8},{10,11... | collective-permute-start | bytes 417800 | tf_op jit(solution)/shard_map/ppermute | solution.py:437
  31.3 8.1 %collective-permute-start.23 = (f32[128,256]{1,0:T(8,128)S(1)}, f32[128,256]{1,0:T(8,128)S(1)}, u32[]{:S(2)}, u32[]{:S(2)}) collective-permute-start(f32[128,256]{1,0:T(8,128)S(1)} %shard_map.96.refs_1_), channel_id=1, source_target_pairs={{0,2},{1,3},{2,0},{3,1},{4,6},{5,7},{6,4},{7,5},{8,10},{9,11},{10,... | collective-permute-start | bytes 393224 | tf_op jit(solution)/shard_map/ppermute | solution.py:437
  32.9 8.0 %collective-permute-start.17 = (f32[72,256]{1,0:T(8,128)S(1)}, f32[72,256]{1,0:T(8,128)S(1)}, u32[]{:S(2)}, u32[]{:S(2)}) collective-permute-start(f32[72,256]{1,0:T(8,128)S(1)} %shard_map.94), channel_id=1, source_target_pairs={{0,16},{1,17},{2,18},{3,19},{4,20},{5,21},{6,22},{7,23},{8,24},{9,... | collective-permute-start | bytes 221192 | tf_op jit(solution)/shard_map/ppermute | solution.py:437
  35.9 9.2 %collective-permute-start.16 = (f32[128,256]{1,0:T(8,128)S(1)}, f32[128,256]{1,0:T(8,128)S(1)}, u32[]{:S(2)}, u32[]{:S(2)}) collective-permute-start(f32[128,256]{1,0:T(8,128)S(1)} %get-tuple-element.69.refs_3_), channel_id=1, source_target_pairs={{0,16},{1,17},{2,18},{3,19},{4,20},{5,21},{6,22},{7,23},{8,24},{9,... | collective-permute-start | bytes 393224 | tf_op jit(solution)/shard_map/ppermute | solution.py:437
  39.4 10.0 %collective-permute-start.24 = (f32[128,256]{1,0:T(8,128)S(1)}, f32[128,256]{1,0:T(8,128)S(1)}, u32[]{:S(2)}, u32[]{:S(2)}) collective-permute-start(f32[128,256]{1,0:T(8,128)S(1)} %shard_map.97.refs_1_), channel_id=1, source_target_pairs={{0,4},{1,5},{2,6},{3,7},{4,0},{5,1},{6,2},{7,3},{8,12},{9,13},{10,... | collective-permute-start | bytes 393224 | tf_op jit(solution)/shard_map/ppermute | solution.py:437
  45.8 10.6 %collective-permute-start.21 = (f32[168,256]{1,0:T(8,128)S(1)}, f32[168,256]{1,0:T(8,128)S(1)}, u32[]{:S(2)}, u32[]{:S(2)}) collective-permute-start(f32[168,256]{1,0:T(8,128)S(1)} %get-tuple-element.75), channel_id=1, source_target_pairs={{0,6},{1,7},{2,4},{3,5},{4,2},{5,3},{6,0},{7,1},{8,14},{9,15},{10,... | collective-permute-start | bytes 516104 | tf_op jit(solution)/shard_map/ppermute | solution.py:437
  47.3 8.3 %collective-permute-start.19 = (f32[160,256]{1,0:T(8,128)S(1)}, f32[160,256]{1,0:T(8,128)S(1)}, u32[]{:S(2)}, u32[]{:S(2)}) collective-permute-start(f32[160,256]{1,0:T(8,128)S(1)} %get-tuple-element.73), channel_id=1, source_target_pairs={{0,2},{1,3},{2,0},{3,1},{4,6},{5,7},{6,4},{7,5},{8,10},{9,11},{10,... | collective-permute-start | bytes 491528 | tf_op jit(solution)/shard_map/ppermute | solution.py:437
  48.2 8.2 %collective-permute-start.20 = (f32[160,256]{1,0:T(8,128)S(1)}, f32[160,256]{1,0:T(8,128)S(1)}, u32[]{:S(2)}, u32[]{:S(2)}) collective-permute-start(f32[160,256]{1,0:T(8,128)S(1)} %get-tuple-element.74), channel_id=1, source_target_pairs={{0,4},{1,5},{2,6},{3,7},{4,0},{5,1},{6,2},{7,3},{8,12},{9,13},{10,... | collective-permute-start | bytes 491528 | tf_op jit(solution)/shard_map/ppermute | solution.py:437
  49.4 5.0 %collective-permute-start.25 = (f32[128,256]{1,0:T(8,128)S(1)}, f32[128,256]{1,0:T(8,128)S(1)}, u32[]{:S(2)}, u32[]{:S(2)}) collective-permute-start(f32[128,256]{1,0:T(8,128)S(1)} %shard_map.98.refs_1_), channel_id=1, source_target_pairs={{0,8},{1,9},{2,10},{3,11},{4,12},{5,13},{6,14},{7,15},{8,0},{9,1},... | collective-permute-start | bytes 393224 | tf_op jit(solution)/shard_map/ppermute | solution.py:437
  56.5 2.4 %collective-permute-start.26 = (f32[4,192,256]{2,1,0:T(8,128)S(1)}, f32[4,192,256]{2,1,0:T(8,128)S(1)}, u32[]{:S(2)}, u32[]{:S(2)}) collective-permute-start(f32[4,192,256]{2,1,0:T(8,128)S(1)} %shard_map.101.refs_10_.refs_14_), channel_id=1, source_target_pairs={{0,1},{1,0},{2,3},{3,2},{4,5},{5,4},{6,7},{7,6},{8,9},{9,8},{10,11... | collective-permute-start | bytes 2359304 | tf_op jit(solution)/shard_map/ppermute | solution.py:437
  (5 other events, 15.0 us)

commit v4 on v3

--- a/solution.py
+++ b/solution.py
@@ -148,10 +148,10 @@
 
     first = [fetch(vectors_hbm, vectors_ref), fetch(factors_hbm, factors_ref)]
     parts = [fetch_part(b, part_ref.at[b]) for b in range(count)]
+    for copy in first:
+        copy.wait()
     last = [fetch_part(count + b, later_ref.at[b]) for b in range(later_ref.shape[0])]
     last.append([fetch(inverse_hbm, inverse_ref)])
-    for copy in first:
-        copy.wait()
     vectors = vectors_ref[...]
     across = halves(vectors.T)
     across_ref[0], across_ref[1] = across
@@ -344,14 +344,12 @@
 
 
 def pass_kernel(me_ref, *refs):
-    backs, dones, (gram_ref, out_ref) = refs[:4], refs[4:8], refs[8:]
+    backs, dones, out_ref = refs[:4], refs[4:8], refs[8]
     odd = me_ref[0] % 2 == 1
-    cols, rows = dones[0].shape[0], backs[0].shape[0]
-    quarter = rows - cols
+    cols, rows = dones[0].shape[0], out_ref.shape[1]
     for r in range(4):
         out_ref[r, :cols] = jnp.where(odd, backs[r][:cols], dones[r][...])
-        out_ref[r, cols:rows] = backs[r][cols:rows]
-        out_ref[r, rows:] = gram_ref[r * quarter : (r + 1) * quarter]
+        out_ref[r, cols:] = backs[r][cols:rows]
 
 
 def near_kernel(me_ref, *refs):
@@ -375,8 +373,8 @@
 
 def far_kernel(me_ref, *refs, total):
     backs, dones = refs[:4], refs[4:8]
-    there_ref, half_ref, inverse_ref, _, _, updated_hbm, basis_hbm, gram_hbm = refs[8:16]
-    panel_ref, sum_ref, out_ref, basis_ref, gram_ref, sems = refs[16:]
+    there_ref, half_ref, half_there, inverse_ref, _, _, updated_hbm, basis_hbm, gram_hbm = refs[8:17]
+    panel_ref, sum_ref, out_ref, basis_ref, gram_ref, sems = refs[17:]
     count, width, half = out_ref.shape
     quarter = half // 4
     cols = count * quarter
@@ -389,6 +387,17 @@
         copies.append(pltpu.make_async_copy(source, target, sems.at[len(copies)]))
         copies[-1].start()
 
+    def target(part, r):
+        return pl.ds(pl.multiple_of(part * half + (place(me) ^ r) * quarter, quarter), quarter)
+
+    for r in range(4):
+        panel_ref[target(core, r)] = backs[r][cols : cols + quarter]
+        panel_ref[target(1 - core, r)] = there_ref[r, cols:]
+    sum_ref[pl.ds(pl.multiple_of(core * half, half), half)] = half_ref[...]
+    sum_ref[pl.ds(pl.multiple_of((1 - core) * half, half), half)] = half_there[...]
+    panel = halves(panel_ref[...])
+    gram_ref[...] = (sum_ref[...] - by_transpose(panel, panel)) / total
+    put(gram_ref, gram_hbm)
     for b in range(count):
         rows = slice(b * quarter, (b + 1) * quarter)
         pieces = [there_ref[r, rows] for r in range(4)]
@@ -403,19 +412,6 @@
             basis = plain(halves(head), halves(inverse_ref[...]))
             basis_ref[...] = jnp.where(me == 0, 0.0, basis)
             put(basis_ref, basis_hbm.at[pl.ds(0, width)])
-
-    def target(part, r):
-        return pl.ds(pl.multiple_of(part * half + (place(me) ^ r) * quarter, quarter), quarter)
-
-    for r in range(4):
-        panel_ref[target(core, r)] = backs[r][cols : cols + quarter]
-        panel_ref[target(1 - core, r)] = there_ref[r, cols : cols + quarter]
-        rows = pl.ds(pl.multiple_of((1 - core) * half + r * quarter, quarter), quarter)
-        sum_ref[rows] = there_ref[r, cols + quarter :]
-    sum_ref[pl.ds(pl.multiple_of(core * half, half), half)] = half_ref[...]
-    panel = halves(panel_ref[...])
-    gram_ref[...] = (sum_ref[...] - by_transpose(panel, panel)) / total
-    put(gram_ref, gram_hbm)
     for copy in copies:
         copy.wait()
 
@@ -562,7 +558,8 @@
         store_kernel, (rest_a, rest_b, inverse_factor), (shape(8, width), shape(rows, columns), shape(rows, width)),
         [vmem(width, width), sems(count + 1)], (), (1, 2),
     )
-    (back,) = call(pass_kernel, (*backs, *dones, gram_half), (shape(4, cols + 2 * quarter, width),))
+    gram_there = exchange(gram_half, 1)
+    (back,) = call(pass_kernel, (*backs, *dones), (shape(4, cols + quarter, width),), before=(gram_half,))
     there = exchange(back, 1)
     (updated,) = call(
         near_kernel, (*backs, *dones, updated), (shape(rows, columns),),
@@ -570,10 +567,10 @@
     )
     return call(
         functools.partial(far_kernel, total=float(rows * devices)),
-        (*backs, *dones, there, gram_half, inverse_factor, updated, basis),
+        (*backs, *dones, there, gram_half, gram_there, inverse_factor, updated, basis),
         (shape(rows, columns), shape(rows, width), shape(width, width)),
         [vmem(width, width), vmem(width, width), vmem(count, width, half), vmem(width, width), vmem(width, width), sems(count + 2)],
-        (11, 12), (0, 1, 2), {12: 0, 13: 1},
+        (12, 13), (0, 1, 2), {13: 0, 14: 1},
     )
 
 

time: 60.5 us -> 60.5 us (level)
    ppermute x27 -> x28, starting transfers between devices: 28.2 us -> 28.7 us  [exchange(): return lax.ppermute(value, 'rows', [(i, i ^ shift) for i in range(devices)])]
    ppermute x27 -> x28, waiting for transfers between devices: 16.4 us -> 15.9 us  [exchange(): return lax.ppermute(value, 'rows', [(i, i ^ shift) for i in range(devices)])]
  transfers between devices with their start and end apart: 27 -> 28, of which waited for: 12 -> 12; matrix products, arithmetic and copies ran while one was open for 0% -> 0% of each run, Pallas kernels for 22% -> 22%
where the time goes in v4:
time: 60.5 us; the launch traced here: 60.3 us
  starting transfers between devices  28.7 us (47%)
  waiting for transfers between devices  15.9 us (26%)
  Pallas kernels  14.9 us (25%)
  between operations  0.82 us (1%)
    ppermute x28, starting transfers between devices, exchange(): return lax.ppermute(value, 'rows', [(i, i ^ shift) for i in range(devices)])  28.7 us
    ppermute x28, waiting for transfers between devices, exchange(): return lax.ppermute(value, 'rows', [(i, i ^ shift) for i in range(devices)])  15.9 us
    pallas_call x19, Pallas kernels, call(): pl.pallas_call(kernel_on, out_shape=tuple(outs), in_specs=[SCALAR] + [AWA...  14.9 us
  transfers between devices with their start and end apart: 28, of which 12 were waited for; matrix products, arithmetic and copies ran while one was open for 0% of the time, Pallas kernels for 22%

profile of v4, /device:TPU:0, one launch (start us, length us, event | category | flops | bytes accessed | tf_op | source)
XLA Modules:
  0.0 60.3 jit_solution(3829769092717151366)
XLA Ops:
  1.2 4.2 %shard_map.85 = (f32[384,256]{1,0:T(8,128)S(1)}, f32[192,256]{1,0:T(8,128)S(1)}, f32[192,256]{1,0:T(8,128)S(1)}, f32[2,256,256]{2,1,0:T(8,128)S(1)}, f32[2,512,2...) custom-call(s32[1]{0:T(128)} %bitcast.refs_0_, ...), custom_call_target="tpu_custom_call" | custom-call | flops 1 | bytes 1 | tf_op jit(solution)/shard_map/pallas_call | solution.py:460
  6.4 3.9 %collective-permute-start.11 = (f32[136,256]{1,0:T(8,128)S(1)}, f32[136,256]{1,0:T(8,128)S(1)}, u32[]{:S(2)}, u32[]{:S(2)}) collective-permute-start(f32[136,256]{1,0:T(8,128)S(1)} %get-tuple-element.60.refs_1_), channel_id=1, source_target_pairs={{0,6},{1,7},{2,4},{3,5},{4,2},{5,3},{6,0},{7,1},{8,14},{9,15},{10,... | collective-permute-start | bytes 417800 | tf_op jit(solution)/shard_map/ppermute | solution.py:433
  10.9 1.6 %shard_map.87 = (f32[256,256]{1,0:T(8,128)S(1)}, f32[2,256,256]{2,1,0:T(8,128)S(1)}, f32[128,256]{1,0:T(8,128)S(1)}, f32[128,256]{1,0:T(8,128)S(1)}) custom-call(s32[1]{0:T(128)} %bitcast.refs_0_, f32[2,512,256]{2,1,0:T(8,128)S(1)} %get-tuple-element.46.refs_1_, bf16[2,256,512]{2,1,0:T(8,128)(2,1)S(1)} %get-tuple-element.47.refs_2_, ...), custom_call_target="tpu_custom_call" | custom-call | flops 1 | bytes 1 | tf_op jit(solution)/shard_map/pallas_call | solution.py:460
  14.1 1.3 %shard_map.88 = (f32[128,256]{1,0:T(8,128)S(1)}, f32[128,256]{1,0:T(8,128)S(1)}, f32[128,256]{1,0:T(8,128)S(1)}, f32[136,256]{1,0:T(8,128)S(1)}, f32[128,256]{1,...) custom-call(s32[1]{0:T(128)} %bitcast.refs_0_, ...), custom_call_target="tpu_custom_call" | custom-call | flops 1 | bytes 1 | tf_op jit(solution)/shard_map/pallas_call | solution.py:460
  15.5 1.7 %collective-permute-done.10.refs_3_ = f32[136,256]{1,0:T(8,128)S(1)} collective-permute-done((f32[136,256]{1,0:T(8,128)S(1)}, f32[136,256]{1,0:T(8,128)S(1)}, u32[]{:S(2)}, u32[]{:S(2)}) %collective-permute-start.10) | collective-permute-done | bytes 139296 | tf_op jit(solution)/shard_map/ppermute | solution.py:433
  17.6 1.6 %collective-permute-start.8 = (f32[136,256]{1,0:T(8,128)S(1)}, f32[136,256]{1,0:T(8,128)S(1)}, u32[]{:S(2)}, u32[]{:S(2)}) collective-permute-start(f32[136,256]{1,0:T(8,128)S(1)} %get-tuple-element.59), channel_id=1, source_target_pairs={{0,6},{1,7},{2,4},{3,5},{4,2},{5,3},{6,0},{7,1},{8,14},{9,15},{10,... | collective-permute-start | bytes 417800 | tf_op jit(solution)/shard_map/ppermute | solution.py:433
  19.2 1.4 %collective-permute-start.6 = (f32[128,256]{1,0:T(8,128)S(1)}, f32[128,256]{1,0:T(8,128)S(1)}, u32[]{:S(2)}, u32[]{:S(2)}) collective-permute-start(f32[128,256]{1,0:T(8,128)S(1)} %get-tuple-element.57), channel_id=1, source_target_pairs={{0,2},{1,3},{2,0},{3,1},{4,6},{5,7},{6,4},{7,5},{8,10},{9,11},{10,... | collective-permute-start | bytes 393224 | tf_op jit(solution)/shard_map/ppermute | solution.py:433
  21.2 1.6 %collective-permute-start.14 = (f32[136,256]{1,0:T(8,128)S(1)}, f32[136,256]{1,0:T(8,128)S(1)}, u32[]{:S(2)}, u32[]{:S(2)}) collective-permute-start(f32[136,256]{1,0:T(8,128)S(1)} %get-tuple-element.66.refs_1_), channel_id=1, source_target_pairs={{0,8},{1,9},{2,10},{3,11},{4,12},{5,13},{6,14},{7,15},{8,0},{9,1},... | collective-permute-start | bytes 417800 | tf_op jit(solution)/shard_map/ppermute | solution.py:433
  22.8 2.6 %collective-permute-start.22 = (f32[128,256]{1,0:T(8,128)S(1)}, f32[128,256]{1,0:T(8,128)S(1)}, u32[]{:S(2)}, u32[]{:S(2)}) collective-permute-start(f32[128,256]{1,0:T(8,128)S(1)} %get-tuple-element.84.refs_1_), channel_id=1, source_target_pairs={{0,16},{1,17},{2,18},{3,19},{4,20},{5,21},{6,22},{7,23},{8,24},{9,... | collective-permute-start | bytes 393224 | tf_op jit(solution)/shard_map/ppermute | solution.py:433
  25.9 1.5 %collective-permute-done.6.refs_2_ = f32[128,256]{1,0:T(8,128)S(1)} collective-permute-done((f32[128,256]{1,0:T(8,128)S(1)}, f32[128,256]{1,0:T(8,128)S(1)}, u32[]{:S(2)}, u32[]{:S(2)}) %collective-permute-start.6) | collective-permute-done | bytes 131104 | tf_op jit(solution)/shard_map/ppermute | solution.py:433
  27.5 1.7 %shard_map.92 = (f32[128,256]{1,0:T(8,128)S(1)}, f32[152,256]{1,0:T(8,128)S(1)}, f32[4,128,256]{2,1,0:T(8,128)S(1)}) custom-call(s32[1]{0:T(128)} %bitcast.refs_0_, f32[4,128,256]{2,1,0:T(8,128)S(1)} %shard_map.91.refs_1_.refs_3_, bf16[4,4,256,256]{3,2,1,0:T(8,128)(2,1)S(1)} %get-tuple-element.62.refs_5_.refs_2_, f32[4,128,256]{2,1,0:T(8,128)S(1)} %shard_map.91.refs_1_.refs_3_), custom_call_target="tpu_custom_call" | custom-call | flops 1 | bytes 1 | tf_op jit(solution)/shard_map/pallas_call | solution.py:460
  29.3 1.6 %collective-permute-start.13 = (f32[152,256]{1,0:T(8,128)S(1)}, f32[152,256]{1,0:T(8,128)S(1)}, u32[]{:S(2)}, u32[]{:S(2)}) collective-permute-start(f32[152,256]{1,0:T(8,128)S(1)} %get-tuple-element.64.refs_3_), channel_id=1, source_target_pairs={{0,8},{1,9},{2,10},{3,11},{4,12},{5,13},{6,14},{7,15},{8,0},{9,1},... | collective-permute-start | bytes 466952 | tf_op jit(solution)/shard_map/ppermute | solution.py:433
  31.3 1.6 %collective-permute-start.23 = (f32[128,256]{1,0:T(8,128)S(1)}, f32[128,256]{1,0:T(8,128)S(1)}, u32[]{:S(2)}, u32[]{:S(2)}) collective-permute-start(f32[128,256]{1,0:T(8,128)S(1)} %shard_map.97.refs_1_), channel_id=1, source_target_pairs={{0,2},{1,3},{2,0},{3,1},{4,6},{5,7},{6,4},{7,5},{8,10},{9,11},{10,... | collective-permute-start | bytes 393224 | tf_op jit(solution)/shard_map/ppermute | solution.py:433
  32.9 2.3 %collective-permute-start.17 = (f32[72,256]{1,0:T(8,128)S(1)}, f32[72,256]{1,0:T(8,128)S(1)}, u32[]{:S(2)}, u32[]{:S(2)}) collective-permute-start(f32[72,256]{1,0:T(8,128)S(1)} %shard_map.94), channel_id=1, source_target_pairs={{0,16},{1,17},{2,18},{3,19},{4,20},{5,21},{6,22},{7,23},{8,24},{9,... | collective-permute-start | bytes 221192 | tf_op jit(solution)/shard_map/ppermute | solution.py:433
  35.9 3.4 %collective-permute-start.16 = (f32[128,256]{1,0:T(8,128)S(1)}, f32[128,256]{1,0:T(8,128)S(1)}, u32[]{:S(2)}, u32[]{:S(2)}) collective-permute-start(f32[128,256]{1,0:T(8,128)S(1)} %get-tuple-element.69.refs_3_), channel_id=1, source_target_pairs={{0,16},{1,17},{2,18},{3,19},{4,20},{5,21},{6,22},{7,23},{8,24},{9,... | collective-permute-start | bytes 393224 | tf_op jit(solution)/shard_map/ppermute | solution.py:433
  39.4 1.5 %collective-permute-start.24 = (f32[128,256]{1,0:T(8,128)S(1)}, f32[128,256]{1,0:T(8,128)S(1)}, u32[]{:S(2)}, u32[]{:S(2)}) collective-permute-start(f32[128,256]{1,0:T(8,128)S(1)} %shard_map.98.refs_1_), channel_id=1, source_target_pairs={{0,4},{1,5},{2,6},{3,7},{4,0},{5,1},{6,2},{7,3},{8,12},{9,13},{10,... | collective-permute-start | bytes 393224 | tf_op jit(solution)/shard_map/ppermute | solution.py:433
  40.9 1.3 %collective-permute-done.18.refs_7_ = f32[72,256]{1,0:T(8,128)S(1)} collective-permute-done((f32[72,256]{1,0:T(8,128)S(1)}, f32[72,256]{1,0:T(8,128)S(1)}, u32[]{:S(2)}, u32[]{:S(2)}) %collective-permute-start.18) | collective-permute-done | bytes 73760 | tf_op jit(solution)/shard_map/ppermute | solution.py:433
  42.2 2.9 %collective-permute-done.16.refs_4_ = f32[128,256]{1,0:T(8,128)S(1)} collective-permute-done((f32[128,256]{1,0:T(8,128)S(1)}, f32[128,256]{1,0:T(8,128)S(1)}, u32[]{:S(2)}, u32[]{:S(2)}) %collective-permute-start.16) | collective-permute-done | bytes 131104 | tf_op jit(solution)/shard_map/ppermute | solution.py:433
  45.8 1.4 %collective-permute-start.21 = (f32[168,256]{1,0:T(8,128)S(1)}, f32[168,256]{1,0:T(8,128)S(1)}, u32[]{:S(2)}, u32[]{:S(2)}) collective-permute-start(f32[168,256]{1,0:T(8,128)S(1)} %get-tuple-element.75), channel_id=1, source_target_pairs={{0,6},{1,7},{2,4},{3,5},{4,2},{5,3},{6,0},{7,1},{8,14},{9,15},{10,... | collective-permute-start | bytes 516104 | tf_op jit(solution)/shard_map/ppermute | solution.py:433
  47.3 0.9 %collective-permute-start.19 = (f32[160,256]{1,0:T(8,128)S(1)}, f32[160,256]{1,0:T(8,128)S(1)}, u32[]{:S(2)}, u32[]{:S(2)}) collective-permute-start(f32[160,256]{1,0:T(8,128)S(1)} %get-tuple-element.73), channel_id=1, source_target_pairs={{0,2},{1,3},{2,0},{3,1},{4,6},{5,7},{6,4},{7,5},{8,10},{9,11},{10,... | collective-permute-start | bytes 491528 | tf_op jit(solution)/shard_map/ppermute | solution.py:433
  48.2 1.2 %collective-permute-start.20 = (f32[160,256]{1,0:T(8,128)S(1)}, f32[160,256]{1,0:T(8,128)S(1)}, u32[]{:S(2)}, u32[]{:S(2)}) collective-permute-start(f32[160,256]{1,0:T(8,128)S(1)} %get-tuple-element.74), channel_id=1, source_target_pairs={{0,4},{1,5},{2,6},{3,7},{4,0},{5,1},{6,2},{7,3},{8,12},{9,13},{10,... | collective-permute-start | bytes 491528 | tf_op jit(solution)/shard_map/ppermute | solution.py:433
  49.5 5.0 %collective-permute-done.25.refs_2_ = f32[128,256]{1,0:T(8,128)S(1)} collective-permute-done((f32[128,256]{1,0:T(8,128)S(1)}, f32[128,256]{1,0:T(8,128)S(1)}, u32[]{:S(2)}, u32[]{:S(2)}) %collective-permute-start.25) | collective-permute-done | bytes 131104 | tf_op jit(solution)/shard_map/ppermute | solution.py:433
  54.5 1.1 %shard_map.96 = (f32[8,256]{1,0:T(8,128)S(1)}, f32[512,1024]{1,0:T(8,128)}, f32[512,256]{1,0:T(8,128)}) custom-call(s32[1]{0:T(128)} %bitcast.refs_0_, f32[2,256,256]{2,1,0:T(8,128)S(1)} %get-tuple-element.80.refs_1_, f32[2,256,256]{2,1,0:T(8,128)S(1)} %get-tuple-element.81.refs_2_, f32[256,256]{1,0:T(8,128)S(1)} %get-tuple-element.82.refs_3_.refs_12_, ...), custom_call_target="tpu_custom_call" | custom-call | flops 1 | bytes 1 | tf_op jit(solution)/shard_map/pallas_call | solution.py:460
  58.8 1.5 %shard_map.103 = (f32[512,1024]{1,0:T(8,128)}, f32[512,256]{1,0:T(8,128)}, f32[256,256]{1,0:T(8,128)}) custom-call(s32[1]{0:T(128)} %bitcast.refs_0_, f32[160,256]{1,0:T(8,128)S(1)} %get-tuple-element.72.refs_4_.refs_1_, f32[160,256]{1,0:T(8,128)S(1)} %collective-permute-done.19.refs_2_, ...), custom_call_target="tpu_custom_call", output_to_operand_aliasing={{0}: (13, {}), {1}: (14, {})} | custom-call | flops 1 | bytes 1 | tf_op jit(solution)/shard_map/pallas_call | solution.py:460
  (55 shorter events, 10.7 us)
Async XLA Ops:
  0.7 5.4 %collective-permute-start = (f32[256,256]{1,0:T(8,128)}, f32[256,256]{1,0:T(8,128)S(1)}, u32[]{:S(2)}, u32[]{:S(2)}) collective-permute-start(f32[256,256]{1,0:T(8,128)} %refs_1_.3), channel_id=1, source_target_pairs={{0,1},{1,0},{2,3},{3,2},{4,5},{5,4},{6,7},{7,6},{8,9},{9,8},{10,11... | collective-permute-start | bytes 786440 | tf_op jit(solution)/shard_map/ppermute | solution.py:433
  1.2 4.8 %collective-permute-start.1 = (f32[256,256]{1,0:T(8,128)}, f32[256,256]{1,0:T(8,128)S(1)}, u32[]{:S(2)}, u32[]{:S(2)}) collective-permute-start(f32[256,256]{1,0:T(8,128)} %refs_2_.3), channel_id=1, source_target_pairs={{0,1},{1,0},{2,3},{3,2},{4,5},{5,4},{6,7},{7,6},{8,9},{9,8},{10,11... | collective-permute-start | bytes 786440 | tf_op jit(solution)/shard_map/ppermute | solution.py:433
  5.4 5.5 %collective-permute-start.2 = (f32[192,256]{1,0:T(8,128)S(1)}, f32[192,256]{1,0:T(8,128)S(1)}, u32[]{:S(2)}, u32[]{:S(2)}) collective-permute-start(f32[192,256]{1,0:T(8,128)S(1)} %get-tuple-element.50), channel_id=1, source_target_pairs={{0,1},{1,0},{2,3},{3,2},{4,5},{5,4},{6,7},{7,6},{8,9},{9,8},{10,11... | collective-permute-start | bytes 589832 | tf_op jit(solution)/shard_map/ppermute | solution.py:433
  5.9 5.0 %collective-permute-start.3 = (f32[192,256]{1,0:T(8,128)S(1)}, f32[192,256]{1,0:T(8,128)S(1)}, u32[]{:S(2)}, u32[]{:S(2)}) collective-permute-start(f32[192,256]{1,0:T(8,128)S(1)} %get-tuple-element.51), channel_id=1, source_target_pairs={{0,1},{1,0},{2,3},{3,2},{4,5},{5,4},{6,7},{7,6},{8,9},{9,8},{10,11... | collective-permute-start | bytes 589832 | tf_op jit(solution)/shard_map/ppermute | solution.py:433
  6.4 9.1 %collective-permute-start.11 = (f32[136,256]{1,0:T(8,128)S(1)}, f32[136,256]{1,0:T(8,128)S(1)}, u32[]{:S(2)}, u32[]{:S(2)}) collective-permute-start(f32[136,256]{1,0:T(8,128)S(1)} %get-tuple-element.60.refs_1_), channel_id=1, source_target_pairs={{0,6},{1,7},{2,4},{3,5},{4,2},{5,3},{6,0},{7,1},{8,14},{9,15},{10,... | collective-permute-start | bytes 417800 | tf_op jit(solution)/shard_map/ppermute | solution.py:433
  10.3 6.9 %collective-permute-start.10 = (f32[136,256]{1,0:T(8,128)S(1)}, f32[136,256]{1,0:T(8,128)S(1)}, u32[]{:S(2)}, u32[]{:S(2)}) collective-permute-start(f32[136,256]{1,0:T(8,128)S(1)} %get-tuple-element.60.refs_1_), channel_id=1, source_target_pairs={{0,4},{1,5},{2,6},{3,7},{4,0},{5,1},{6,2},{7,3},{8,12},{9,13},{10,... | collective-permute-start | bytes 417800 | tf_op jit(solution)/shard_map/ppermute | solution.py:433
  10.8 6.7 %collective-permute-start.9 = (f32[136,256]{1,0:T(8,128)S(1)}, f32[136,256]{1,0:T(8,128)S(1)}, u32[]{:S(2)}, u32[]{:S(2)}) collective-permute-start(f32[136,256]{1,0:T(8,128)S(1)} %get-tuple-element.60.refs_1_), channel_id=1, source_target_pairs={{0,2},{1,3},{2,0},{3,1},{4,6},{5,7},{6,4},{7,5},{8,10},{9,11},{10,... | collective-permute-start | bytes 417800 | tf_op jit(solution)/shard_map/ppermute | solution.py:433
  17.6 5.2 %collective-permute-start.12 = (f32[3,136,256]{2,1,0:T(8,128)S(1)}, f32[3,136,256]{2,1,0:T(8,128)S(1)}, u32[]{:S(2)}, u32[]{:S(2)}) collective-permute-start(f32[3,136,256]{2,1,0:T(8,128)S(1)} %get-tuple-element.61.refs_2_.refs_4_), channel_id=1, source_target_pairs={{0,1},{1,0},{2,3},{3,2},{4,5},{5,4},{6,7},{7,6},{8,9},{9,8},{10,11... | collective-permute-start | bytes 1253384 | tf_op jit(solution)/shard_map/ppermute | solution.py:433
  17.6 9.8 %collective-permute-start.8 = (f32[136,256]{1,0:T(8,128)S(1)}, f32[136,256]{1,0:T(8,128)S(1)}, u32[]{:S(2)}, u32[]{:S(2)}) collective-permute-start(f32[136,256]{1,0:T(8,128)S(1)} %get-tuple-element.59), channel_id=1, source_target_pairs={{0,6},{1,7},{2,4},{3,5},{4,2},{5,3},{6,0},{7,1},{8,14},{9,15},{10,... | collective-permute-start | bytes 417800 | tf_op jit(solution)/shard_map/ppermute | solution.py:433
  19.2 8.2 %collective-permute-start.6 = (f32[128,256]{1,0:T(8,128)S(1)}, f32[128,256]{1,0:T(8,128)S(1)}, u32[]{:S(2)}, u32[]{:S(2)}) collective-permute-start(f32[128,256]{1,0:T(8,128)S(1)} %get-tuple-element.57), channel_id=1, source_target_pairs={{0,2},{1,3},{2,0},{3,1},{4,6},{5,7},{6,4},{7,5},{8,10},{9,11},{10,... | collective-permute-start | bytes 393224 | tf_op jit(solution)/shard_map/ppermute | solution.py:433
  20.6 6.9 %collective-permute-start.7 = (f32[128,256]{1,0:T(8,128)S(1)}, f32[128,256]{1,0:T(8,128)S(1)}, u32[]{:S(2)}, u32[]{:S(2)}) collective-permute-start(f32[128,256]{1,0:T(8,128)S(1)} %get-tuple-element.58), channel_id=1, source_target_pairs={{0,4},{1,5},{2,6},{3,7},{4,0},{5,1},{6,2},{7,3},{8,12},{9,13},{10,... | collective-permute-start | bytes 393224 | tf_op jit(solution)/shard_map/ppermute | solution.py:433
  21.2 9.7 %collective-permute-start.14 = (f32[136,256]{1,0:T(8,128)S(1)}, f32[136,256]{1,0:T(8,128)S(1)}, u32[]{:S(2)}, u32[]{:S(2)}) collective-permute-start(f32[136,256]{1,0:T(8,128)S(1)} %get-tuple-element.66.refs_1_), channel_id=1, source_target_pairs={{0,8},{1,9},{2,10},{3,11},{4,12},{5,13},{6,14},{7,15},{8,0},{9,1},... | collective-permute-start | bytes 417800 | tf_op jit(solution)/shard_map/ppermute | solution.py:433
  22.8 8.6 %collective-permute-start.22 = (f32[128,256]{1,0:T(8,128)S(1)}, f32[128,256]{1,0:T(8,128)S(1)}, u32[]{:S(2)}, u32[]{:S(2)}) collective-permute-start(f32[128,256]{1,0:T(8,128)S(1)} %get-tuple-element.84.refs_1_), channel_id=1, source_target_pairs={{0,16},{1,17},{2,18},{3,19},{4,20},{5,21},{6,22},{7,23},{8,24},{9,... | collective-permute-start | bytes 393224 | tf_op jit(solution)/shard_map/ppermute | solution.py:433
  29.3 6.0 %collective-permute-start.13 = (f32[152,256]{1,0:T(8,128)S(1)}, f32[152,256]{1,0:T(8,128)S(1)}, u32[]{:S(2)}, u32[]{:S(2)}) collective-permute-start(f32[152,256]{1,0:T(8,128)S(1)} %get-tuple-element.64.refs_3_), channel_id=1, source_target_pairs={{0,8},{1,9},{2,10},{3,11},{4,12},{5,13},{6,14},{7,15},{8,0},{9,1},... | collective-permute-start | bytes 466952 | tf_op jit(solution)/shard_map/ppermute | solution.py:433
  30.9 4.3 %collective-permute-start.15 = (f32[136,256]{1,0:T(8,128)S(1)}, f32[136,256]{1,0:T(8,128)S(1)}, u32[]{:S(2)}, u32[]{:S(2)}) collective-permute-start(f32[136,256]{1,0:T(8,128)S(1)} %collective-permute-done.14.refs_6_.refs_2_), channel_id=1, source_target_pairs={{0,1},{1,0},{2,3},{3,2},{4,5},{5,4},{6,7},{7,6},{8,9},{9,8},{10,11... | collective-permute-start | bytes 417800 | tf_op jit(solution)/shard_map/ppermute | solution.py:433
  31.3 8.1 %collective-permute-start.23 = (f32[128,256]{1,0:T(8,128)S(1)}, f32[128,256]{1,0:T(8,128)S(1)}, u32[]{:S(2)}, u32[]{:S(2)}) collective-permute-start(f32[128,256]{1,0:T(8,128)S(1)} %shard_map.97.refs_1_), channel_id=1, source_target_pairs={{0,2},{1,3},{2,0},{3,1},{4,6},{5,7},{6,4},{7,5},{8,10},{9,11},{10,... | collective-permute-start | bytes 393224 | tf_op jit(solution)/shard_map/ppermute | solution.py:433
  32.9 8.0 %collective-permute-start.17 = (f32[72,256]{1,0:T(8,128)S(1)}, f32[72,256]{1,0:T(8,128)S(1)}, u32[]{:S(2)}, u32[]{:S(2)}) collective-permute-start(f32[72,256]{1,0:T(8,128)S(1)} %shard_map.94), channel_id=1, source_target_pairs={{0,16},{1,17},{2,18},{3,19},{4,20},{5,21},{6,22},{7,23},{8,24},{9,... | collective-permute-start | bytes 221192 | tf_op jit(solution)/shard_map/ppermute | solution.py:433
  35.9 9.2 %collective-permute-start.16 = (f32[128,256]{1,0:T(8,128)S(1)}, f32[128,256]{1,0:T(8,128)S(1)}, u32[]{:S(2)}, u32[]{:S(2)}) collective-permute-start(f32[128,256]{1,0:T(8,128)S(1)} %get-tuple-element.69.refs_3_), channel_id=1, source_target_pairs={{0,16},{1,17},{2,18},{3,19},{4,20},{5,21},{6,22},{7,23},{8,24},{9,... | collective-permute-start | bytes 393224 | tf_op jit(solution)/shard_map/ppermute | solution.py:433
  39.4 10.0 %collective-permute-start.24 = (f32[128,256]{1,0:T(8,128)S(1)}, f32[128,256]{1,0:T(8,128)S(1)}, u32[]{:S(2)}, u32[]{:S(2)}) collective-permute-start(f32[128,256]{1,0:T(8,128)S(1)} %shard_map.98.refs_1_), channel_id=1, source_target_pairs={{0,4},{1,5},{2,6},{3,7},{4,0},{5,1},{6,2},{7,3},{8,12},{9,13},{10,... | collective-permute-start | bytes 393224 | tf_op jit(solution)/shard_map/ppermute | solution.py:433
  45.8 10.6 %collective-permute-start.21 = (f32[168,256]{1,0:T(8,128)S(1)}, f32[168,256]{1,0:T(8,128)S(1)}, u32[]{:S(2)}, u32[]{:S(2)}) collective-permute-start(f32[168,256]{1,0:T(8,128)S(1)} %get-tuple-element.75), channel_id=1, source_target_pairs={{0,6},{1,7},{2,4},{3,5},{4,2},{5,3},{6,0},{7,1},{8,14},{9,15},{10,... | collective-permute-start | bytes 516104 | tf_op jit(solution)/shard_map/ppermute | solution.py:433
  47.3 8.3 %collective-permute-start.19 = (f32[160,256]{1,0:T(8,128)S(1)}, f32[160,256]{1,0:T(8,128)S(1)}, u32[]{:S(2)}, u32[]{:S(2)}) collective-permute-start(f32[160,256]{1,0:T(8,128)S(1)} %get-tuple-element.73), channel_id=1, source_target_pairs={{0,2},{1,3},{2,0},{3,1},{4,6},{5,7},{6,4},{7,5},{8,10},{9,11},{10,... | collective-permute-start | bytes 491528 | tf_op jit(solution)/shard_map/ppermute | solution.py:433
  48.2 8.2 %collective-permute-start.20 = (f32[160,256]{1,0:T(8,128)S(1)}, f32[160,256]{1,0:T(8,128)S(1)}, u32[]{:S(2)}, u32[]{:S(2)}) collective-permute-start(f32[160,256]{1,0:T(8,128)S(1)} %get-tuple-element.74), channel_id=1, source_target_pairs={{0,4},{1,5},{2,6},{3,7},{4,0},{5,1},{6,2},{7,3},{8,12},{9,13},{10,... | collective-permute-start | bytes 491528 | tf_op jit(solution)/shard_map/ppermute | solution.py:433
  49.4 5.0 %collective-permute-start.25 = (f32[128,256]{1,0:T(8,128)S(1)}, f32[128,256]{1,0:T(8,128)S(1)}, u32[]{:S(2)}, u32[]{:S(2)}) collective-permute-start(f32[128,256]{1,0:T(8,128)S(1)} %shard_map.99.refs_1_), channel_id=1, source_target_pairs={{0,8},{1,9},{2,10},{3,11},{4,12},{5,13},{6,14},{7,15},{8,0},{9,1},... | collective-permute-start | bytes 393224 | tf_op jit(solution)/shard_map/ppermute | solution.py:433
  56.5 2.4 %collective-permute-start.26 = (f32[4,160,256]{2,1,0:T(8,128)S(1)}, f32[4,160,256]{2,1,0:T(8,128)S(1)}, u32[]{:S(2)}, u32[]{:S(2)}) collective-permute-start(f32[4,160,256]{2,1,0:T(8,128)S(1)} %shard_map.101.refs_10_.refs_15_), channel_id=1, source_target_pairs={{0,1},{1,0},{2,3},{3,2},{4,5},{5,4},{6,7},{7,6},{8,9},{9,8},{10,11... | collective-permute-start | bytes 1966088 | tf_op jit(solution)/shard_map/ppermute | solution.py:433
  (6 other events, 17.2 us)
